TPU v7x, 32 devices: a whole 2x2x4 slice. The times are simulated.
32 devices in a mesh: expert: 4 (over x, core), shard: 8 (over z, y).
Axes of the slice: x: 2, y: 2, z: 4, core: 2. Of those that a mesh axis runs over, the one named last changes fastest.
Arguments:
- tokens: bfloat16 [65536, 512], P(('expert', 'shard')), may hold values from -6 to 6
- ln1_gain: float32 [512], P(('expert', 'shard')), may hold values from 0.5 to 1.5
- ln2_gain: float32 [512], P(('expert', 'shard')), may hold values from 0.5 to 1.5
- w_query: float32 [512, 512], P(('expert', 'shard')), may hold values from -0.25 to 0.25
- w_key: float32 [512, 512], P(('expert', 'shard')), may hold values from -0.25 to 0.25
- w_value: float32 [512, 512], P(('expert', 'shard')), may hold values from -0.25 to 0.25
- w_attn_out: float32 [512, 512], P(('expert', 'shard')), may hold values from -4 to 4
- w_ctrl: float32 [512, 32], P(('expert', 'shard')), may hold values from -0.1875 to 0.1875
- w_in: float32 [32, 512, 2048], P('expert', None, 'shard'), may hold values from -1 to 1
- b_in: float32 [32, 2048], P('expert', 'shard'), may hold values from -2 to 2
- w_exp_out: float32 [32, 2048, 512], P('expert', 'shard'), may hold values from -1.5 to 1.5
- routes: int32 [2048, 8], P(('expert', 'shard')), may hold values from 0 to 31, all different within a row; in each aligned block of 64 rows (0 to 63, 64 to 127, ...) at most 24 rows name the same one
- grad_out: bfloat16 [65536, 512], P(('expert', 'shard')), may hold values from -6 to 6
Outputs:
- output: bfloat16 [65536, 512], P(('expert', 'shard'))
- grad_tokens: bfloat16 [65536, 512], P(('expert', 'shard'))
- grad_ln1_gain: float32 [512], P(('expert', 'shard'))
- grad_ln2_gain: float32 [512], P(('expert', 'shard'))
- grad_w_query: float32 [512, 512], P(('expert', 'shard'))
- grad_w_key: float32 [512, 512], P(('expert', 'shard'))
- grad_w_value: float32 [512, 512], P(('expert', 'shard'))
- grad_w_attn_out: float32 [512, 512], P(('expert', 'shard'))
- grad_w_ctrl: float32 [512, 32], P(('expert', 'shard'))
- grad_w_in: float32 [32, 512, 2048], P('expert', None, 'shard')
- grad_b_in: float32 [32, 2048], P('expert', 'shard')
- grad_w_exp_out: float32 [32, 2048, 512], P('expert', 'shard')
Inputs may be any that keep to these rules, and one draw needn't show every extreme that they name: `routes`: each row names 8 different experts. Among the rows of one device (aligned blocks of 64 groups) no expert is named more than 24 times, a bound that some block reaches.
All inputs are finite; a program needn't handle non-finite values.
Results may differ from a plain program's by a relative error of at most 0.02.
Values may be sent and summed in bfloat16 or wider, within the bound.
No kernel may reach another device: no remote copies, remote signals or barrier semaphores. Data moves between devices by JAX's collectives and lax.ppermute only.
A program may use at most 256 MiB of HBM per device.

v0:
```python
import jax
import jax.numpy as jnp
from jax import lax
from jax.experimental import pallas as pl
from jax.experimental.pallas import tpu as pltpu
from jax.sharding import PartitionSpec as P

D = 512
HEAD_DIM = 64
GROUP = 32
ROUTES = 8
BLOCK = 256
CAP = 24
EPSILON = 1e-05
SCALE = 0.125 * 1.4426950408889634
BOTH = ("expert", "shard")

bf16 = jnp.bfloat16
f32 = jnp.float32
VMEM = pltpu.CompilerParams(vmem_limit_bytes=56 * 2**20)


def product(left_op, right_op):
    return jnp.dot(left_op, right_op, preferred_element_type=f32)


def transposed_product(left_op, right_op):
    return lax.dot_general(left_op, right_op, (((0,), (0,)), ((), ())), preferred_element_type=f32)


def against_rows(left_op, right_op):
    return lax.dot_general(left_op, right_op, (((1,), (1,)), ((), ())), preferred_element_type=f32)


def attention_forward_kernel(q_ref, k_ref, v_ref, o_ref, lse_ref):
    length = q_ref.shape[0]
    q_t = q_ref[...].T
    v_t = v_ref[...].T
    zero = jnp.zeros((HEAD_DIM, length), bf16)
    ones = jnp.ones((16, length), bf16)
    halves_q = [q_t[:HEAD_DIM], q_t[HEAD_DIM:]]
    sides = [
        jnp.concatenate([halves_q[0], zero], 0),
        jnp.concatenate([zero, halves_q[1]], 0),
    ]
    values = [
        jnp.concatenate([v_t[:HEAD_DIM], ones], 0),
        jnp.concatenate([v_t[HEAD_DIM:], ones], 0),
    ]

    def scores_of(b, h):
        n = (b + 1) * BLOCK
        return product(k_ref[:n, :], sides[h][:, b * BLOCK : n])

    items = [(b, h) for b in range(length // BLOCK) for h in range(2)]
    outs = []
    later = scores_of(*items[0])
    for i, (b, h) in enumerate(items):
        n = (b + 1) * BLOCK
        cols = slice(b * BLOCK, n)
        scores = later
        if i + 1 < len(items):
            later = scores_of(*items[i + 1])
        top = jnp.max(scores, axis=0, keepdims=True) * SCALE
        weights = jnp.exp2(scores * SCALE - top).astype(bf16)
        out = product(values[h][:, :n], weights)
        total = out[HEAD_DIM : HEAD_DIM + 1]
        outs.append(out[:HEAD_DIM] / total)
        lse_ref[0, h : h + 1, cols] = top + jnp.log2(total)
        if h == 1:
            o_ref[cols, :] = jnp.concatenate(outs, 0).T.astype(bf16)
            outs = []


def attention_backward_kernel(
    q_ref, k_ref, v_ref, g_ref, o_ref, lse_ref, dq_ref, dk_ref, dv_ref, dq_t
):
    length = q_ref.shape[0]
    q_t = q_ref[...].T
    g_t = g_ref[...].T
    k_t = k_ref[...].T
    both = (g_ref[...].astype(f32) * o_ref[...].astype(f32)).T
    zero = jnp.zeros((HEAD_DIM, length), bf16)
    heads = []
    for h in range(2):
        rows = slice(h * HEAD_DIM, (h + 1) * HEAD_DIM)
        heads.append(
            (
                rows,
                jnp.concatenate([q_t[rows], zero] if h == 0 else [zero, q_t[rows]], 0),
                jnp.concatenate([g_t[rows], zero] if h == 0 else [zero, g_t[rows]], 0),
                jnp.sum(both[rows], axis=0, keepdims=True),
                lse_ref[0, h : h + 1, :],
            )
        )

    def products_of(j, h):
        here = slice(j * BLOCK, (j + 1) * BLOCK)
        _, q_side, g_side, _, _ = heads[h]
        return (
            product(k_ref[here, :], q_side[:, j * BLOCK :]),
            product(v_ref[here, :], g_side[:, j * BLOCK :]),
        )

    items = [(j, h) for j in range(length // BLOCK) for h in range(2)]
    key_grads = []
    value_grads = []
    later = products_of(*items[0])
    for i, (j, h) in enumerate(items):
        lo = j * BLOCK
        here = slice(lo, lo + BLOCK)
        rows, _, _, delta, lse = heads[h]
        scores, share_grad = later
        if i + 1 < len(items):
            later = products_of(*items[i + 1])
        shares = jnp.exp2(scores * SCALE - lse[:, lo:])
        score_grad = (shares * (share_grad - delta[:, lo:])).astype(bf16)
        value_grads.append(against_rows(g_t[rows, lo:], shares.astype(bf16)))
        key_grads.append(against_rows(q_t[rows, lo:], score_grad))
        query_part = product(k_t[rows, here], score_grad)
        if j == 0:
            dq_t[rows, :] = query_part
        else:
            dq_t[rows, lo:] = dq_t[rows, lo:] + query_part
        if h == 1:
            dk_ref[here, :] = (jnp.concatenate(key_grads, 0) * 0.125).T.astype(bf16)
            dv_ref[here, :] = jnp.concatenate(value_grads, 0).T.astype(bf16)
            key_grads = []
            value_grads = []
    dq_ref[...] = (dq_t[...] * 0.125).T.astype(bf16)


def pair_columns(length, offset):
    return pl.BlockSpec((length, 2 * HEAD_DIM), lambda pair: (0, pair + offset))


def attention_forward(qkv):
    length = qkv.shape[0]
    pairs = D // (2 * HEAD_DIM)
    stats = pl.BlockSpec((1, 2, length), lambda pair: (pair, 0, 0))
    return pl.pallas_call(
        attention_forward_kernel,
        grid=(pairs,),
        in_specs=[pair_columns(length, i * pairs) for i in range(3)],
        out_specs=[pair_columns(length, 0), stats],
        out_shape=[
            jax.ShapeDtypeStruct((length, D), bf16),
            jax.ShapeDtypeStruct((pairs, 2, length), f32),
        ],
        compiler_params=VMEM,
        cost_estimate=pl.CostEstimate(
            flops=10_000_000_000, bytes_accessed=8 * 2**20, transcendentals=0
        ),
        name="attention_forward",
    )(qkv, qkv, qkv)


def attention_backward(qkv, grad, attended, lse):
    length = qkv.shape[0]
    pairs = D // (2 * HEAD_DIM)
    stats = pl.BlockSpec((1, 2, length), lambda pair: (pair, 0, 0))
    return pl.pallas_call(
        attention_backward_kernel,
        grid=(pairs,),
        in_specs=[pair_columns(length, i * pairs) for i in range(3)]
        + [pair_columns(length, 0), pair_columns(length, 0), stats],
        out_specs=[pair_columns(length, 0)] * 3,
        out_shape=[jax.ShapeDtypeStruct((length, D), bf16)] * 3,
        scratch_shapes=[pltpu.VMEM((2 * HEAD_DIM, length), f32)],
        compiler_params=VMEM,
        cost_estimate=pl.CostEstimate(
            flops=50_000_000_000, bytes_accessed=16 * 2**20, transcendentals=20_000_000
        ),
        name="attention_backward",
    )(qkv, qkv, qkv, grad, attended, lse)


CHUNK = 256
LANES = 128
BIAS_ROWS = 16
SHARDS_A_STEP = 2
GAIN_ONE = LANES - 2
GAIN_TWO = LANES - 1


def call(kernel, grid, in_specs, out_specs, out_shape, scratch, flops, moved, name):
    return pl.pallas_call(
        kernel,
        grid=(grid,),
        in_specs=in_specs,
        out_specs=out_specs,
        out_shape=out_shape,
        scratch_shapes=scratch,
        compiler_params=VMEM,
        cost_estimate=pl.CostEstimate(flops=flops, bytes_accessed=moved, transcendentals=0),
        name=name,
    )


def fixed(*shape):
    return pl.BlockSpec(shape, lambda i: (0,) * len(shape))


def small_columns(width, start):
    return pl.BlockSpec((D, width), lambda i: (0, start // width))


def leading(*shape):
    return pl.BlockSpec(shape, lambda i: (i,) + (0,) * (len(shape) - 1))


def normalise(matrix):
    average = jnp.mean(matrix, axis=1, keepdims=True)
    centered = matrix - average
    inverse = lax.rsqrt(jnp.mean(centered * centered, axis=1, keepdims=True) + EPSILON)
    return centered * inverse, inverse


def norm_input_grad(upstream, scaled, inverse, gain):
    adjusted = upstream * gain
    first_mean = jnp.mean(adjusted, axis=1, keepdims=True)
    second_mean = jnp.mean(adjusted * scaled, axis=1, keepdims=True)
    return inverse * (adjusted - first_mean - scaled * second_mean)


def small_kernel(q_ref, k_ref, v_ref, o_ref, ctrl_ref, one_ref, two_ref, out_ref):
    rows, experts = ctrl_ref.shape
    for i, ref in enumerate((q_ref, k_ref, v_ref, o_ref)):
        out_ref[:, i * D : (i + 1) * D] = ref[...].astype(bf16)
    square = (rows, rows)
    own = lax.broadcasted_iota(jnp.int32, square, 0) == lax.broadcasted_iota(jnp.int32, square, 1)
    one = jnp.sum(jnp.where(own, one_ref[...], 0.0), axis=1, keepdims=True)
    two = jnp.sum(jnp.where(own, two_ref[...], 0.0), axis=1, keepdims=True)
    lane = lax.broadcasted_iota(jnp.int32, (rows, LANES), 1)
    gains = jnp.where(lane == GAIN_ONE, one, jnp.where(lane == GAIN_TWO, two, 0.0))
    out_ref[:, 4 * D :] = gains.astype(bf16)
    out_ref[:, 4 * D : 4 * D + experts] = ctrl_ref[...].astype(bf16)


def pack_small(weights, ctrl, gain_one, gain_two):
    rows, experts = ctrl.shape
    width = 4 * D + LANES
    return call(
        small_kernel,
        1,
        [fixed(rows, D)] * 4 + [fixed(rows, experts), fixed(1, rows), fixed(1, rows)],
        fixed(rows, width),
        jax.ShapeDtypeStruct((rows, width), bf16),
        [],
        100_000,
        200_000,
        "pack_small",
    )(*weights, ctrl, gain_one.reshape(1, rows), gain_two.reshape(1, rows))


def gain_of(ctrl_block, lane):
    pick = (lax.broadcasted_iota(jnp.int32, (16, LANES), 1) == lane).astype(bf16)
    return against_rows(pick, ctrl_block)[:1]


def pack_kernel(first_ref, bias_ref, second_ref, out_ref):
    hidden = first_ref.shape[2]
    out_ref[0, :D, :] = first_ref[0].astype(bf16)
    out_ref[0, D : D + BIAS_ROWS, :] = jnp.broadcast_to(
        bias_ref[pl.ds(pl.program_id(0), 1), :], (BIAS_ROWS, hidden)
    ).astype(bf16)
    for c in range(D // hidden):
        start = D + BIAS_ROWS + c * hidden
        out_ref[0, start : start + hidden, :] = second_ref[
            0, :, c * hidden : (c + 1) * hidden
        ].astype(bf16)


def pack_weights(w_in, b_in, w_exp_out):
    local, _, hidden = w_in.shape
    total = 2 * D + BIAS_ROWS
    return call(
        pack_kernel,
        local,
        [leading(1, D, hidden), fixed(local, hidden), leading(1, hidden, D)],
        leading(1, total, hidden),
        jax.ShapeDtypeStruct((local, total, hidden), bf16),
        [],
        1_000_000,
        12 * 2**20,
        "pack_weights",
    )(w_in, b_in, w_exp_out)


def unpack_kernel(in_ref, first_ref, bias_ref, second_ref):
    hidden = first_ref.shape[2]
    first_ref[0] = in_ref[0, :D, :].astype(f32)
    bias_ref[pl.ds(pl.program_id(0), 1), :] = in_ref[0, D : D + BIAS_ROWS, :].astype(f32)[:1]
    for c in range(D // hidden):
        start = D + BIAS_ROWS + c * hidden
        second_ref[0, :, c * hidden : (c + 1) * hidden] = in_ref[
            0, start : start + hidden, :
        ].astype(f32)


def unpack_grads(packed):
    local, total, hidden = packed.shape
    return call(
        unpack_kernel,
        local,
        [leading(1, total, hidden)],
        [leading(1, D, hidden), fixed(local, hidden), leading(1, hidden, D)],
        [
            jax.ShapeDtypeStruct((local, D, hidden), f32),
            jax.ShapeDtypeStruct((local, hidden), f32),
            jax.ShapeDtypeStruct((local, hidden, D), f32),
        ],
        [],
        1_000_000,
        12 * 2**20,
        "unpack_grads",
    )(packed)


def expert_part(rows_ref, w_ref, i):
    hidden = w_ref.shape[2]
    first = w_ref[i, :D, :]
    bias = w_ref[i, D : D + BIAS_ROWS, :].astype(f32)[:1]
    pre_act = product(rows_ref[:, :D], first) + bias
    sigma = 0.5 + 0.5 * jnp.tanh(0.5 * pre_act)
    hidden_grad = jnp.zeros_like(pre_act)
    second = []
    for c in range(D // hidden):
        start = D + BIAS_ROWS + c * hidden
        second.append(w_ref[i, start : start + hidden, :])
        cols = slice(D + c * hidden, D + (c + 1) * hidden)
        hidden_grad = hidden_grad + against_rows(rows_ref[:, cols], second[-1])
    active = (pre_act * sigma).astype(bf16)
    pre_grad = (
        hidden_grad.astype(bf16).astype(f32) * (sigma * (1.0 + pre_act * (1.0 - sigma)))
    ).astype(bf16)
    return first, second, active, pre_grad


def expert_kernel(rows_ref, w_ref, out_ref, results, mixed_grad):
    step = pl.program_id(0)
    held, _, hidden = w_ref.shape
    chunks = D // hidden
    parts = [None] * (chunks + 1)
    for i in range(held):
        first, second, active, pre_grad = expert_part(rows_ref, w_ref, i)
        more = [product(active, block) for block in second] + [against_rows(pre_grad, first)]
        parts = more if i == 0 else [old + new for old, new in zip(parts, more)]

    @pl.when(step == 0)
    def _():
        for c in range(chunks):
            results[:, c * hidden : (c + 1) * hidden] = parts[c]
        mixed_grad[...] = parts[chunks]

    @pl.when(step > 0)
    def _():
        for c in range(chunks):
            cols = slice(c * hidden, (c + 1) * hidden)
            results[:, cols] = results[:, cols] + parts[c]
        mixed_grad[...] = mixed_grad[...] + parts[chunks]

    @pl.when(step == pl.num_programs(0) - 1)
    def _():
        out_ref[:, :D] = results[...].astype(bf16)
        out_ref[:, D:] = mixed_grad[...].astype(bf16)


def expert_rows(rows, weights):
    count = rows.shape[0]
    shards, total, hidden = weights.shape
    return call(
        expert_kernel,
        shards // SHARDS_A_STEP,
        [fixed(count, 2 * D), leading(SHARDS_A_STEP, total, hidden)],
        fixed(count, 2 * D),
        jax.ShapeDtypeStruct((count, 2 * D), bf16),
        [pltpu.VMEM((count, D), f32), pltpu.VMEM((count, D), f32)],
        8 * count * D * shards * hidden,
        8 * 2**20,
        "expert_rows",
    )(rows, weights)


def expert_grad_kernel(rows_ref, w_ref, out_ref, rows_t):
    hidden = out_ref.shape[2]

    @pl.when(pl.program_id(0) == 0)
    def _():
        rows_t[...] = rows_ref[:, :D].T

    _, _, active, pre_grad = expert_part(rows_ref, w_ref, 0)
    out_ref[0, :D, :] = product(rows_t[...], pre_grad).astype(bf16)
    out_ref[0, D : D + BIAS_ROWS, :] = jnp.broadcast_to(
        jnp.sum(pre_grad.astype(f32), axis=0, keepdims=True), (BIAS_ROWS, hidden)
    ).astype(bf16)
    active_t = active.T
    for c in range(D // hidden):
        start = D + BIAS_ROWS + c * hidden
        out_ref[0, start : start + hidden, :] = product(
            active_t, rows_ref[:, D + c * hidden : D + (c + 1) * hidden]
        ).astype(bf16)


def expert_grads(rows, weights):
    count = rows.shape[0]
    shards, total, hidden = weights.shape
    return call(
        expert_grad_kernel,
        shards,
        [fixed(count, 2 * D), leading(1, total, hidden)],
        leading(1, total, hidden),
        jax.ShapeDtypeStruct((shards, total, hidden), bf16),
        [pltpu.VMEM((D, count), bf16)],
        8 * count * D * shards * hidden,
        14 * 2**20,
        "expert_grads",
    )(rows, weights)


def project_kernel(tokens_ref, w_ref, ctrl_ref, qkv_ref, normed_ref):
    scaled, _ = normalise(tokens_ref[...].astype(f32))
    normed = (scaled * gain_of(ctrl_ref[...], GAIN_ONE)).astype(bf16)
    normed_ref[...] = normed
    qkv_ref[...] = product(normed, w_ref[...]).astype(bf16)


def project(tokens, small):
    length = tokens.shape[0]
    return call(
        project_kernel,
        length // CHUNK,
        [leading(CHUNK, D), small_columns(3 * D, 0), small_columns(LANES, 4 * D)],
        [leading(CHUNK, 3 * D), leading(CHUNK, D)],
        [jax.ShapeDtypeStruct((length, 3 * D), bf16), jax.ShapeDtypeStruct((length, D), bf16)],
        [],
        6 * length * D * D,
        12 * 2**20,
        "project",
    )(tokens, small, small)


def choose(probs, routes):
    columns = routes.shape[1]
    shape = (LANES, columns)
    onehot = (lax.broadcasted_iota(jnp.int32, shape, 0) == routes).astype(bf16)
    tokens = probs.shape[0]
    own = lax.broadcasted_iota(jnp.int32, (tokens, columns), 0) // GROUP == (
        lax.broadcasted_iota(jnp.int32, (tokens, columns), 1) // ROUTES
    )
    chosen = jnp.where(own, product(probs.astype(bf16), onehot), 0.0).astype(bf16)
    return chosen, onehot, own


def mix_kernel(
    attended_ref, tokens_ref, grad_ref, wo_ref, ctrl_ref, routes_ref, slots_ref,
    residual_ref, probs_ref, out_ref, rows,
):
    step = pl.program_id(0)
    residual = tokens_ref[...].astype(f32) + product(attended_ref[...], wo_ref[...])
    residual_ref[...] = residual
    scaled, _ = normalise(residual)
    normed = (scaled * gain_of(ctrl_ref[...], GAIN_TWO)).astype(bf16)
    logits = product(normed, ctrl_ref[...]).reshape(CHUNK // GROUP, GROUP, LANES)
    weights = jnp.exp(logits - jnp.max(logits, axis=1, keepdims=True))
    probs = (weights / jnp.sum(weights, axis=1, keepdims=True)).reshape(CHUNK, LANES)
    probs_ref[...] = probs
    chosen, _, _ = choose(probs, routes_ref[0])
    columns = chosen.shape[1]
    here = pl.ds(pl.multiple_of(step * columns, columns), columns)
    rows[here, :D] = transposed_product(chosen, normed).astype(bf16)
    rows[here, D:] = transposed_product(chosen, grad_ref[...]).astype(bf16)

    @pl.when(step == pl.num_programs(0) - 1)
    def _():
        shape = (out_ref.shape[0], rows.shape[0])
        dispatch = (lax.broadcasted_iota(jnp.int32, shape, 0) == slots_ref[...]).astype(bf16)
        out_ref[...] = product(dispatch, rows[...]).astype(bf16)


def mix(attended, tokens, grad_out, small, routes, slots, slot_count):
    length = tokens.shape[0]
    steps = length // CHUNK
    count = slots.shape[0]
    return call(
        mix_kernel,
        steps,
        [leading(CHUNK, D)] * 3
        + [small_columns(D, 3 * D), small_columns(LANES, 4 * D)]
        + [leading(1, 1, count // steps), fixed(1, count)],
        [leading(CHUNK, D), leading(CHUNK, LANES), fixed(slot_count, 2 * D)],
        [
            jax.ShapeDtypeStruct((length, D), f32),
            jax.ShapeDtypeStruct((length, LANES), f32),
            jax.ShapeDtypeStruct((slot_count, 2 * D), bf16),
        ],
        [pltpu.VMEM((count, 2 * D), bf16)],
        4 * length * D * D,
        14 * 2**20,
        "mix",
    )(
        attended, tokens, grad_out, small, small,
        routes.reshape(steps, 1, count // steps), slots.reshape(1, count),
    )


def combine_kernel(
    residual_ref, grad_ref, probs_ref, attended_ref, wo_ref, ctrl_ref, routes_ref,
    slots_ref, back_ref, output_ref, residual_grad_ref, attended_grad_ref, sums_ref, gain_sum,
):
    step = pl.program_id(0)
    gain = gain_of(ctrl_ref[...], GAIN_TWO)
    residual = residual_ref[...]
    scaled, inverse = normalise(residual)
    normed = (scaled * gain).astype(bf16)
    probs = probs_ref[...]
    grad = grad_ref[...]
    chosen, onehot, own = choose(probs, routes_ref[0])
    shape = (chosen.shape[1], back_ref.shape[0])
    collect = (lax.broadcasted_iota(jnp.int32, shape, 1) == slots_ref[...]).astype(bf16)
    rows = product(collect, back_ref[...]).astype(bf16)
    results = rows[:, :D]
    mixed_grad = rows[:, D:]
    output_ref[...] = (residual + product(chosen, results)).astype(bf16)
    chosen_grad = jnp.where(own, against_rows(grad, results) + against_rows(normed, mixed_grad), 0.0)
    high = chosen_grad.astype(bf16)
    low = (chosen_grad - high.astype(f32)).astype(bf16)
    prob_grad = against_rows(high, onehot) + against_rows(low, onehot)
    weighted = (probs * prob_grad).reshape(CHUNK // GROUP, GROUP, LANES)
    total = jnp.broadcast_to(jnp.sum(weighted, axis=1, keepdims=True), weighted.shape)
    logit_grad = (probs * (prob_grad - total.reshape(CHUNK, LANES))).astype(bf16)
    normed_grad = product(chosen, mixed_grad) + against_rows(logit_grad, ctrl_ref[...])
    gain_part = jnp.sum(normed_grad * scaled, axis=0, keepdims=True)
    residual_grad = grad.astype(f32) + norm_input_grad(normed_grad, scaled, inverse, gain)
    residual_grad_ref[...] = residual_grad
    branch = residual_grad.astype(bf16)
    attended_grad_ref[...] = against_rows(branch, wo_ref[...]).astype(bf16)
    wo_part = transposed_product(attended_ref[...], branch)
    ctrl_part = transposed_product(normed, logit_grad)

    @pl.when(step == 0)
    def _():
        sums_ref[:, :D] = wo_part
        sums_ref[:, D:] = ctrl_part
        gain_sum[...] = gain_part

    @pl.when(step > 0)
    def _():
        sums_ref[:, :D] = sums_ref[:, :D] + wo_part
        sums_ref[:, D:] = sums_ref[:, D:] + ctrl_part
        gain_sum[...] = gain_sum[...] + gain_part

    @pl.when(step == pl.num_programs(0) - 1)
    def _():
        column = jnp.broadcast_to(gain_sum[...], (LANES, D)).T
        lane = lax.broadcasted_iota(jnp.int32, (D, LANES), 1)
        sums_ref[:, D:] = jnp.where(lane == LANES - 1, column, sums_ref[:, D:])


def combine(residual, grad_out, probs, attended, small, routes, slots, back):
    length = residual.shape[0]
    steps = length // CHUNK
    count = slots.shape[0]
    return call(
        combine_kernel,
        steps,
        [leading(CHUNK, D), leading(CHUNK, D), leading(CHUNK, LANES), leading(CHUNK, D)]
        + [small_columns(D, 3 * D), small_columns(LANES, 4 * D), leading(1, 1, count // steps)]
        + [leading(count // steps, 1), fixed(*back.shape)],
        [leading(CHUNK, D)] * 3 + [fixed(D, D + LANES)],
        [
            jax.ShapeDtypeStruct((length, D), bf16),
            jax.ShapeDtypeStruct((length, D), f32),
            jax.ShapeDtypeStruct((length, D), bf16),
            jax.ShapeDtypeStruct((D, D + LANES), f32),
        ],
        [pltpu.VMEM((1, D), f32)],
        6 * length * D * D,
        24 * 2**20,
        "combine",
    )(
        residual, grad_out, probs, attended, small, small,
        routes.reshape(steps, 1, count // steps), slots.reshape(count, 1), back,
    )


def weight_grad_kernel(
    core_ref, normed_ref, q_ref, k_ref, v_ref, sums_ref, away_ref, kept_ref, total
):
    step = pl.program_id(0)
    normed_t = normed_ref[...].T

    for i, ref in enumerate((q_ref, k_ref, v_ref)):
        cols = slice(i * D, (i + 1) * D)
        part = product(normed_t, ref[...])

        @pl.when(step == 0)
        def _(cols=cols, part=part):
            total[:, cols] = part

        @pl.when(step > 0)
        def _(cols=cols, part=part):
            total[:, cols] = total[:, cols] + part

    @pl.when(step == pl.num_programs(0) - 1)
    def _():
        rows = kept_ref.shape[1]
        for x in range(kept_ref.shape[0]):
            mine = pl.ds(pl.multiple_of((2 * x + core_ref[0]) * rows, rows), rows)
            other = pl.ds(pl.multiple_of((2 * x + 1 - core_ref[0]) * rows, rows), rows)
            kept_ref[x, :, : 3 * D] = total[mine, :]
            kept_ref[x, :, 3 * D :] = sums_ref[mine, :]
            away_ref[x, :, : 3 * D] = total[other, :].astype(bf16)
            away_ref[x, :, 3 * D :] = sums_ref[other, :].astype(bf16)


def weight_grads(normed, query_grad, key_grad, value_grad, sums, core, n_expert):
    length = normed.shape[0]
    width = sums.shape[1]
    chunk = 512
    shape = (n_expert // 2, D // n_expert, 3 * D + width)
    return call(
        weight_grad_kernel,
        length // chunk,
        [pl.BlockSpec(memory_space=pltpu.SMEM)] + [leading(chunk, D)] * 4 + [fixed(D, width)],
        [fixed(*shape), fixed(*shape)],
        [jax.ShapeDtypeStruct(shape, bf16), jax.ShapeDtypeStruct(shape, f32)],
        [pltpu.VMEM((D, 3 * D), f32)],
        6 * length * D * D,
        12 * 2**20,
        "weight_grads",
    )(core, normed, query_grad, key_grad, value_grad, sums)


def input_grad_kernel(q_ref, k_ref, v_ref, w_ref, ctrl_ref, tokens_ref, residual_grad_ref, out_ref):
    upstream = against_rows(q_ref[...], w_ref[:, :D])
    upstream = upstream + against_rows(k_ref[...], w_ref[:, D : 2 * D])
    upstream = upstream + against_rows(v_ref[...], w_ref[:, 2 * D :])
    scaled, inverse = normalise(tokens_ref[...].astype(f32))
    gain = gain_of(ctrl_ref[...], GAIN_ONE)
    out_ref[...] = (
        residual_grad_ref[...] + norm_input_grad(upstream, scaled, inverse, gain)
    ).astype(bf16)


def input_grads(query_grad, key_grad, value_grad, small, tokens, residual_grad):
    length = tokens.shape[0]
    return call(
        input_grad_kernel,
        length // CHUNK,
        [leading(CHUNK, D)] * 3
        + [small_columns(3 * D, 0), small_columns(LANES, 4 * D)]
        + [leading(CHUNK, D), leading(CHUNK, D)],
        leading(CHUNK, D),
        jax.ShapeDtypeStruct((length, D), bf16),
        [],
        6 * length * D * D,
        18 * 2**20,
        "input_grads",
    )(query_grad, key_grad, value_grad, small, small, tokens, residual_grad)


def finish_kernel(pieces_ref, own_ref, q_ref, k_ref, v_ref, o_ref, ctrl_ref, one_ref, two_ref):
    rows, experts = ctrl_ref.shape
    total = jnp.sum(pieces_ref[...].astype(f32), axis=0)
    own = own_ref[...].astype(f32)
    for i, ref in enumerate((q_ref, k_ref, v_ref, o_ref)):
        ref[...] = total[:, i * D : (i + 1) * D]
    ctrl_ref[...] = total[:, 4 * D : 4 * D + experts]
    lane = lax.broadcasted_iota(jnp.int32, (rows, LANES), 1)

    def column(block, which):
        return jnp.sum(jnp.where(lane == which, block[:, 4 * D :], 0.0), axis=1, keepdims=True)

    one = jnp.sum(total[:, : 3 * D] * own[:, : 3 * D], axis=1, keepdims=True) / column(own, GAIN_ONE)
    square = (rows, rows)
    same = lax.broadcasted_iota(jnp.int32, square, 0) == lax.broadcasted_iota(jnp.int32, square, 1)
    one_ref[...] = jnp.sum(jnp.where(same, one, 0.0), axis=0, keepdims=True)
    two_ref[...] = jnp.sum(jnp.where(same, column(total, GAIN_TWO), 0.0), axis=0, keepdims=True)


def finish(pieces, own, experts):
    count, rows, width = pieces.shape
    outs = [(rows, D)] * 4 + [(rows, experts), (1, rows), (1, rows)]
    return call(
        finish_kernel,
        1,
        [fixed(count, rows, width), fixed(rows, width)],
        [fixed(*shape) for shape in outs],
        [jax.ShapeDtypeStruct(shape, f32) for shape in outs],
        [],
        1_000_000,
        1_000_000,
        "finish",
    )(pieces, own)


def swap(block, axis, bits):
    size = lax.axis_size(axis)
    return lax.ppermute(block, axis, [(i, i ^ bits) for i in range(size)])


def halves(size):
    inner = 1
    while inner * inner * 4 <= size:
        inner *= 2
    return size // inner, inner


def spread(block, size, stride, place):
    held = jnp.zeros((size,) + block.shape, block.dtype)
    held = lax.dynamic_update_slice(held, block[None], (place, 0, 0))
    for k in range(1, size):
        got = swap(block, "shard", k * stride)
        held = lax.dynamic_update_slice(held, got[None], (place ^ k, 0, 0))
    return held.reshape(-1, block.shape[1])


def gather_expert(held):
    n_expert = lax.axis_size("expert")
    mine = lax.axis_index("expert")
    rows, width = held.shape
    bit = n_expert // 2
    steps = 0
    while bit:
        got = swap(held, "expert", bit)
        low = (mine & bit) == 0
        held = jnp.stack([jnp.where(low, held, got), jnp.where(low, got, held)])
        bit //= 2
        steps += 1
    order = tuple(range(steps - 1, -1, -1)) + (steps, steps + 1)
    return held.transpose(order).reshape(n_expert * rows, width)


def sum_expert(away, kept):
    n_expert = lax.axis_size("expert")
    mine = lax.axis_index("expert")
    width = kept.shape[-1]
    steps = n_expert.bit_length() - 1
    held = kept + swap(away, "expert", 1).astype(f32)
    held = held.reshape((2,) * (steps - 1) + (-1, width))
    for step in range(1, steps):
        bit = 1 << step
        axis = steps - 1 - step
        high = (mine & bit) >> step
        away = lax.dynamic_index_in_dim(held, high ^ 1, axis, keepdims=False).astype(bf16)
        kept = lax.dynamic_index_in_dim(held, high, axis, keepdims=False)
        held = kept + swap(away, "expert", bit).astype(f32)
    return held


def along_shard(blocks):
    return lax.all_to_all(blocks, "shard", split_axis=0, concat_axis=0, tiled=True)


def to_experts(array, copies):
    if copies > 1:
        array = jnp.repeat(array, copies, axis=0)
    return along_shard(array)


def from_experts(array, copies):
    back = along_shard(array)
    if copies > 1:
        back = back.astype(f32).reshape((-1, copies) + back.shape[1:]).sum(axis=1)
    return back


def exchange(rows, copies):
    n_expert = lax.axis_size("expert")
    n_shard = lax.axis_size("shard")
    groups = None
    if copies > 1:
        groups = [
            [e * n_shard + s for e in range(n_expert) for s in range(p, n_shard, copies)]
            for p in range(copies)
        ]
    return lax.all_to_all(
        rows, BOTH, split_axis=0, concat_axis=0, tiled=True, axis_index_groups=groups
    )


def slots_of(routes, experts):
    groups = routes.shape[0]
    named = (routes[:, :, None] == jnp.arange(experts, dtype=jnp.int32)[None, None, :]).astype(f32)
    earlier = jnp.tril(jnp.ones((groups, groups), f32), -1).astype(bf16)
    before = product(earlier, jnp.sum(named, axis=1).astype(bf16))
    rank = jnp.sum(named * before[:, None, :], axis=2).astype(jnp.int32)
    return (routes * CAP + rank).reshape(-1)


def body(
    tokens,
    ln1_gain,
    ln2_gain,
    w_query,
    w_key,
    w_value,
    w_attn_out,
    w_ctrl,
    w_in,
    b_in,
    w_exp_out,
    routes,
    grad_out,
):
    experts = w_ctrl.shape[1]
    n_shard = lax.axis_size("shard")
    copies = n_shard * lax.axis_size("expert") // experts
    slots = slots_of(routes, experts)

    own = pack_small(
        (w_query, w_key, w_value, w_attn_out), w_ctrl, ln1_gain, ln2_gain
    )
    outer, inner = halves(n_shard)
    here = lax.axis_index("shard")
    held = spread(own, inner, 1, here & (inner - 1))
    held, w_in, w_exp_out = lax.optimization_barrier((held, w_in, w_exp_out))
    expert_w = to_experts(pack_weights(w_in, b_in, w_exp_out), copies)
    held = spread(held, outer, inner, here >> (inner.bit_length() - 1))
    small = gather_expert(held)

    qkv, normed_one = project(tokens, small)
    attended, lse = attention_forward(qkv)
    residual, probs, outgoing = mix(
        attended, tokens, grad_out, small, routes, slots, experts * CAP
    )
    outgoing, expert_w = lax.optimization_barrier((outgoing, expert_w))
    arrived = exchange(outgoing, copies)
    results = expert_rows(arrived, expert_w)
    returned = exchange(results, copies)
    expert_sums = expert_grads(arrived, expert_w)
    returned, expert_sums = lax.optimization_barrier((returned, expert_sums))
    expert_sums = from_experts(expert_sums, copies)
    output, residual_grad, attended_grad, sums = combine(
        residual, grad_out, probs, attended, small, routes, slots, returned
    )
    query_grad, key_grad, value_grad = attention_backward(qkv, attended_grad, attended, lse)
    core = (lax.axis_index("expert") & 1).reshape(1)
    away, kept = weight_grads(
        normed_one, query_grad, key_grad, value_grad, sums, core, lax.axis_size("expert")
    )
    late = sum_expert(away, kept)
    input_grad = input_grads(query_grad, key_grad, value_grad, small, tokens, residual_grad)
    late, input_grad, expert_sums = lax.optimization_barrier((late, input_grad, expert_sums))
    pieces = along_shard(late.astype(bf16).reshape((n_shard,) + own.shape))
    w_in_grad, b_in_grad, w_exp_out_grad = unpack_grads(expert_sums)
    wq_grad, wk_grad, wv_grad, wo_grad, wc_grad, ln1_grad, ln2_grad = finish(pieces, own, experts)
    return (
        output,
        input_grad,
        ln1_grad.reshape(-1),
        ln2_grad.reshape(-1),
        wq_grad,
        wk_grad,
        wv_grad,
        wo_grad,
        wc_grad,
        w_in_grad,
        b_in_grad,
        w_exp_out_grad,
    )


def solution(mesh):
    rows = P(BOTH, None)
    vector = P(BOTH)
    experts = (P("expert", None, "shard"), P("expert", "shard"), P("expert", "shard", None))
    in_specs = (rows, vector, vector) + (rows,) * 5 + experts + (rows, rows)
    out_specs = (rows, rows, vector, vector) + (rows,) * 5 + experts
    return jax.shard_map(body, mesh=mesh, in_specs=in_specs, out_specs=out_specs, check_vma=False)
```

profile of v0, /device:TPU:0, one launch (start us, length us, event | category | flops | bytes accessed | tf_op | source)
XLA Modules:
  0.0 344.5 jit_solution(8316458869425623991)
XLA Ops:
  0.6 1.5 pack_small.1.own_ref
  2.2 3.0 collective-permute-start
  5.2 0.9 bitcast_dynamic-update-slice_fusion.5
  6.1 1.6 collective-permute-done
  7.7 2.1 collective-permute-start.1
  9.8 2.6 collective-permute-start.2
  12.4 0.0 collective-permute-start.3
  12.4 7.7 %pack_weights.1 = bf16[8,1040,256]{2,1,0:T(8,128)(2,1)} custom-call(f32[8,512,256]{2,1,0:T(8,128)} %first_ref, f32[8,256]{1,0:T(8,128)} %bias_ref.1, f32[8,256,512]{2,1,0:T(8,128)} %second_ref), custom_call_target="tpu_custom_call" | custom-call | flops 1000000 | bytes 12582912 | tf_op jit(solution)/shard_map/pack_weights/pallas_call | solution.py:277
  20.1 6.1 %all-to-all-start = ((bf16[8,1040,256]{2,1,0:T(8,128)(2,1)}), bf16[8,1040,256]{2,1,0:T(8,128)(2,1)}, u32[]{:S(2)}, u32[]{:S(2)}) async-start(bf16[8,1040,256]{2,1,0:T(8,128)(2,1)} %pack_weights.1), calls=%async_computation | async-start | bytes 8519680 | tf_op jit(solution)/shard_map/all_to_all | solution.py:753
  26.3 0.0 collective-permute-done.1
  26.3 0.0 collective-permute-done.2
  26.3 0.0 collective-permute-done.3
  26.4 1.6 collective-permute-start.4
  27.9 0.0 copy-start.2
  27.9 10.6 %collective-permute-done.4 = bf16[128,2176]{1,0:T(8,128)(2,1)S(1)} collective-permute-done((bf16[128,2176]{1,0:T(8,128)(2,1)S(1)}, bf16[128,2176]{1,0:T(8,128)(2,1)S(1)}, u32[]{:S(2)}, u32[]{:S(2)}) %collective-permute-start.4) | collective-permute-done | bytes 557088 | tf_op jit(solution)/shard_map/ppermute | solution.py:700
  38.5 0.1 select_bitcast_fusion.3
  38.7 0.1 pad_maximum_fusion.1
  38.8 0.1 collective-permute-start.5
  38.9 0.0 copy-done.2
  38.9 0.1 copy.41
  39.0 0.2 fusion.1
  39.3 0.1 copy.42
  39.4 0.7 reshape_reshape.6.slots_ref
  40.0 0.7 reshape.67
  40.7 0.9 collective-permute-done.5
  41.6 0.2 select_bitcast_fusion.1
  41.9 1.6 pad_maximum_fusion
  43.4 9.9 %project.1 = (bf16[2048,1536]{1,0:T(8,128)(2,1)}, bf16[2048,512]{1,0:T(8,128)(2,1)}) custom-call(bf16[2048,512]{1,0:T(8,128)(2,1)} %tokens_ref.5, bf16[512,2176]{1,0:T(8,128)(2,1)} %bitcast.46, bf16[512,2176]{1,0:T(8,128)(2,1)} %bitcast.47), custom_call_target="tpu_custom_call" | custom-call | flops 3221225472 | bytes 12582912 | tf_op jit(solution)/shard_map/project/pallas_call | solution.py:430
  53.3 31.5 %attention_forward.1 = (bf16[2048,512]{1,0:T(8,128)(2,1)}, f32[4,2,2048]{2,1,0:T(2,128)}) custom-call(bf16[2048,1536]{1,0:T(8,128)(2,1)} %get-tuple-element.49.q_ref.k_ref.v_ref, bf16[2048,1536]{1,0:T(8,128)(2,1)} %get-tuple-element.49.q_ref.k_ref.v_ref, bf16[2048,1536]{1,0:T(8,128)(2,1)} %get-tuple-element.49.q_ref.k_ref.v_ref), custom_call_target="tpu_custom_call" | custom-call | flops 10000000000 | bytes 8388608 | tf_op jit(solution)/shard_map/attention_forward/pallas_call | solution.py:141
  84.8 13.4 %mix.1 = (f32[2048,512]{1,0:T(8,128)}, f32[2048,128]{1,0:T(8,128)}, bf16[768,1024]{1,0:T(8,128)(2,1)}) custom-call(bf16[2048,512]{1,0:T(8,128)(2,1)} %get-tuple-element.50.attended_ref.o_ref, bf16[2048,512]{1,0:T(8,128)(2,1)} %tokens_ref.5, bf16[2048,512]{1,0:T(8,128)(2,1)} %grad_ref.3, bf16[512,2176]{1,0:T(8,128)(2,1)} %bitcast.48, ...), custom_call_target="tpu_custom_call" | custom-call | flops 2147483648 | bytes 14680064 | tf_op jit(solution)/shard_map/mix/pallas_call | solution.py:485
  98.2 20.7 %all-to-all-done.w_ref = bf16[8,1040,256]{2,1,0:T(8,128)(2,1)} async-done(((bf16[8,1040,256]{2,1,0:T(8,128)(2,1)}), bf16[8,1040,256]{2,1,0:T(8,128)(2,1)}, u32[]{:S(2)}, u32[]{:S(2)}) %all-to-all-start) | async-done | bytes 4259872 | tf_op jit(solution)/shard_map/all_to_all | solution.py:753
  118.9 42.6 %all_to_all.38 = bf16[32,24,1024]{2,1,0:T(8,128)(2,1)} all-to-all(bf16[32,24,1024]{2,1,0:T(8,128)(2,1)} %bitcast.58), channel_id=1, replica_groups=mesh['expert'=4,'shard'=8] {'expert','shard'}, dimensions={0} | all-to-all | bytes 3145728 | tf_op jit(solution)/shard_map/all_to_all | solution.py:778
  161.5 11.9 %expert_rows.1 = bf16[768,1024]{1,0:T(8,128)(2,1)} custom-call(bf16[768,1024]{1,0:T(8,128)(2,1)} %bitcast.56, bf16[8,1040,256]{2,1,0:T(8,128)(2,1)} %all-to-all-done.w_ref), custom_call_target="tpu_custom_call" | custom-call | flops 6442450944 | bytes 8388608 | tf_op jit(solution)/shard_map/expert_rows/pallas_call | solution.py:372
  173.4 2.7 all-to-all-start.2
  176.1 0.8 reshape_reshape.8.slots_ref
  176.9 12.4 %expert_grads.1 = bf16[8,1040,256]{2,1,0:T(8,128)(2,1)} custom-call(bf16[768,1024]{1,0:T(8,128)(2,1)} %bitcast.57, bf16[8,1040,256]{2,1,0:T(8,128)(2,1)} %all-to-all-done.w_ref), custom_call_target="tpu_custom_call" | custom-call | flops 6442450944 | bytes 14680064 | tf_op jit(solution)/shard_map/expert_grads/pallas_call | solution.py:408
  189.3 25.6 %all-to-all-done.2 = bf16[32,24,1024]{2,1,0:T(8,128)(2,1)S(1)} async-done(((bf16[32,24,1024]{2,1,0:T(8,128)(2,1)}), bf16[32,24,1024]{2,1,0:T(8,128)(2,1)S(1)}, u32[]{:S(2)}, u32[]{:S(2)}) %all-to-all-start.2) | async-done | bytes 1572896 | tf_op jit(solution)/shard_map/all_to_all | solution.py:778
  215.0 0.0 copy-start
  215.0 1.2 copy-done
  216.1 4.6 %all-to-all-start.3 = ((bf16[8,1040,256]{2,1,0:T(8,128)(2,1)}), bf16[8,1040,256]{2,1,0:T(8,128)(2,1)}, u32[]{:S(2)}, u32[]{:S(2)}) async-start(bf16[8,1040,256]{2,1,0:T(8,128)(2,1)} %expert_grads.1), calls=%async_computation.3 | async-start | bytes 8519680 | tf_op jit(solution)/shard_map/all_to_all | solution.py:753
  220.7 20.6 %combine.1 = (bf16[2048,512]{1,0:T(8,128)(2,1)}, f32[2048,512]{1,0:T(8,128)}, bf16[2048,512]{1,0:T(8,128)(2,1)}, f32[512,640]{1,0:T(8,128)}) custom-call(f32[2048,512]{1,0:T(8,128)} %get-tuple-element.51.residual_ref, bf16[2048,512]{1,0:T(8,128)(2,1)} %grad_ref.3, f32[2048,128]{1,0:T(8,128)} %get-tuple-element.52.probs_ref, ...), custom_call_target="tpu_custom_call" | custom-call | flops 3221225472 | bytes 25165824 | tf_op jit(solution)/shard_map/combine/pallas_call | solution.py:564
  241.3 48.7 %attention_backward.1 = (bf16[2048,512]{1,0:T(8,128)(2,1)}, bf16[2048,512]{1,0:T(8,128)(2,1)}, bf16[2048,512]{1,0:T(8,128)(2,1)}) custom-call(bf16[2048,1536]{1,0:T(8,128)(2,1)} %get-tuple-element.49.q_ref.k_ref.v_ref, bf16[2048,1536]{1,0:T(8,128)(2,1)} %get-tuple-element.49.q_ref.k_ref.v_ref, bf16[2048,1536]{1,0:T(8,128)(2,1)} %get-tuple-element.49.q_ref.k_ref.v_ref, ...), custom_call_target="tpu_custom_call" | custom-call | flops 49999998976 | bytes 16777216 | tf_op jit(solution)/shard_map/attention_backward/pallas_call | solution.py:162
  290.0 10.8 %weight_grads.1 = (bf16[2,128,2176]{2,1,0:T(8,128)(2,1)}, f32[2,128,2176]{2,1,0:T(8,128)}) custom-call(s32[1]{0:T(128)} %bitcast.23.core_ref, bf16[2048,512]{1,0:T(8,128)(2,1)} %get-tuple-element.60.normed_ref, bf16[2048,512]{1,0:T(8,128)(2,1)} %get-tuple-element.63.q_ref, bf16[2048,512]{1,0:T(8,128)(2,1)} %get-tuple-element.64.k_ref, ...), custom_call_target="tpu_custom_call" | custom-call | flops 3221225472 | bytes 12582912 | tf_op jit(solution)/shard_map/weight_grads/pallas_call | solution.py:622
  300.8 0.0 collective-permute-start.6
  300.8 3.0 collective-permute-done.6
  303.8 1.8 convert_add_fusion
  305.6 0.1 fusion
  305.7 0.6 collective-permute-start.7
  306.3 11.8 %input_grads.1 = bf16[2048,512]{1,0:T(8,128)(2,1)} custom-call(bf16[2048,512]{1,0:T(8,128)(2,1)} %get-tuple-element.63.q_ref, bf16[2048,512]{1,0:T(8,128)(2,1)} %get-tuple-element.64.k_ref, bf16[2048,512]{1,0:T(8,128)(2,1)} %get-tuple-element.65.v_ref, bf16[512,2176]{1,0:T(8,128)(2,1)} %bitcast.52, bf16[512,2176]{1,0:T(8,128)(2,1)} %bitcast.53, ...), custom_call_target="tpu_custom_call" | custom-call | flops 3221225472 | bytes 18874368 | tf_op jit(solution)/shard_map/input_grads/pallas_call | solution.py:648
  318.1 2.3 collective-permute-done.7
  320.4 0.9 bitcast_add_fusion
  321.3 0.0 all-to-all-done.3.in_ref
  321.3 5.9 %all-to-all-start.4 = ((bf16[8,16,2176]{2,1,0:T(8,128)(2,1)}), bf16[8,16,2176]{2,1,0:T(8,128)(2,1)S(1)}, u32[]{:S(2)}, u32[]{:S(2)}) async-start(bf16[8,16,2176]{2,1,0:T(8,128)(2,1)} %bitcast.27), calls=%async_computation.4 | async-start | bytes 1114112 | tf_op jit(solution)/shard_map/all_to_all | solution.py:753
  327.2 7.2 %unpack_grads.1 = (f32[8,512,256]{2,1,0:T(8,128)}, f32[8,256]{1,0:T(8,128)}, f32[8,256,512]{2,1,0:T(8,128)}) custom-call(bf16[8,1040,256]{2,1,0:T(8,128)(2,1)} %all-to-all-done.3.in_ref), custom_call_target="tpu_custom_call" | custom-call | flops 1000000 | bytes 12582912 | tf_op jit(solution)/shard_map/unpack_grads/pallas_call | solution.py:303
  334.4 7.5 %all-to-all-done.4.pieces_ref = bf16[8,16,2176]{2,1,0:T(8,128)(2,1)S(1)} async-done(((bf16[8,16,2176]{2,1,0:T(8,128)(2,1)}), bf16[8,16,2176]{2,1,0:T(8,128)(2,1)S(1)}, u32[]{:S(2)}, u32[]{:S(2)}) %all-to-all-start.4) | async-done | bytes 557088 | tf_op jit(solution)/shard_map/all_to_all | solution.py:753
  341.9 0.0 copy-start.1
  341.9 0.8 copy-done.1
  342.7 1.8 finish.1
  (11 shorter events, 0.2 us)
Async XLA Ops:
  2.2 5.5 %collective-permute-start = (bf16[16,2176]{1,0:T(8,128)(2,1)}, bf16[16,2176]{1,0:T(8,128)(2,1)S(1)}, u32[]{:S(2)}, u32[]{:S(2)}) collective-permute-start(bf16[16,2176]{1,0:T(8,128)(2,1)} %pack_small.1.own_ref), channel_id=1, source_target_pairs={{0,1},{1,0},{2,3},{3,2},{4,5},{5,4},{6,7},{7,6},{8,9},{9,8},{10,11... | collective-permute-start | bytes 208904 | tf_op jit(solution)/shard_map/ppermute | solution.py:700
  7.7 18.6 %collective-permute-start.1 = (bf16[32,2176]{1,0:T(8,128)(2,1)S(1)}, bf16[32,2176]{1,0:T(8,128)(2,1)S(1)}, u32[]{:S(2)}, u32[]{:S(2)}) collective-permute-start(bf16[32,2176]{1,0:T(8,128)(2,1)S(1)} %bitcast.60), channel_id=1, source_target_pairs={{0,2},{1,3},{2,0},{3,1},{4,6},{5,7},{6,4},{7,5},{8,10},{9,11},{10,... | collective-permute-start | bytes 417800 | tf_op jit(solution)/shard_map/ppermute | solution.py:700
  9.8 16.5 %collective-permute-start.2 = (bf16[32,2176]{1,0:T(8,128)(2,1)S(1)}, bf16[32,2176]{1,0:T(8,128)(2,1)S(1)}, u32[]{:S(2)}, u32[]{:S(2)}) collective-permute-start(bf16[32,2176]{1,0:T(8,128)(2,1)S(1)} %bitcast.61), channel_id=1, source_target_pairs={{0,4},{1,5},{2,6},{3,7},{4,0},{5,1},{6,2},{7,3},{8,12},{9,13},{10,... | collective-permute-start | bytes 417800 | tf_op jit(solution)/shard_map/ppermute | solution.py:700
  12.4 13.9 %collective-permute-start.3 = (bf16[32,2176]{1,0:T(8,128)(2,1)S(1)}, bf16[32,2176]{1,0:T(8,128)(2,1)S(1)}, u32[]{:S(2)}, u32[]{:S(2)}) collective-permute-start(bf16[32,2176]{1,0:T(8,128)(2,1)S(1)} %bitcast.62), channel_id=1, source_target_pairs={{0,6},{1,7},{2,4},{3,5},{4,2},{5,3},{6,0},{7,1},{8,14},{9,15},{10,... | collective-permute-start | bytes 417800 | tf_op jit(solution)/shard_map/ppermute | solution.py:700
  20.1 98.8 %all-to-all-start = ((bf16[8,1040,256]{2,1,0:T(8,128)(2,1)}), bf16[8,1040,256]{2,1,0:T(8,128)(2,1)}, u32[]{:S(2)}, u32[]{:S(2)}) async-start(bf16[8,1040,256]{2,1,0:T(8,128)(2,1)} %pack_weights.1), calls=%async_computation | async-start | bytes 8519680 | tf_op jit(solution)/shard_map/all_to_all | solution.py:753
  26.4 12.2 %collective-permute-start.4 = (bf16[128,2176]{1,0:T(8,128)(2,1)S(1)}, bf16[128,2176]{1,0:T(8,128)(2,1)S(1)}, u32[]{:S(2)}, u32[]{:S(2)}) collective-permute-start(bf16[128,2176]{1,0:T(8,128)(2,1)S(1)} %bitcast.55), channel_id=1, source_target_pairs={{0,16},{8,24},{16,0},{24,8},{1,17},{9,25},{17,1},{25,9},{2,18},{10... | collective-permute-start | bytes 1671176 | tf_op jit(solution)/shard_map/ppermute | solution.py:700
  27.9 11.0 %copy-start.2 = (s32[64,8]{0,1:T(8,128)S(1)}, s32[64,8]{0,1:T(8,128)}, u32[]{:S(2)}) copy-start(s32[64,8]{0,1:T(8,128)} %param.24) | copy-start | bytes 6148
  38.8 2.8 collective-permute-start.5
  173.4 41.5 %all-to-all-start.2 = ((bf16[32,24,1024]{2,1,0:T(8,128)(2,1)}), bf16[32,24,1024]{2,1,0:T(8,128)(2,1)S(1)}, u32[]{:S(2)}, u32[]{:S(2)}) async-start(bf16[32,24,1024]{2,1,0:T(8,128)(2,1)} %bitcast.59), calls=%async_computation.2 | async-start | bytes 3145728 | tf_op jit(solution)/shard_map/all_to_all | solution.py:778
  215.0 1.2 copy-start
  216.1 105.2 %all-to-all-start.3 = ((bf16[8,1040,256]{2,1,0:T(8,128)(2,1)}), bf16[8,1040,256]{2,1,0:T(8,128)(2,1)}, u32[]{:S(2)}, u32[]{:S(2)}) async-start(bf16[8,1040,256]{2,1,0:T(8,128)(2,1)} %expert_grads.1), calls=%async_computation.3 | async-start | bytes 8519680 | tf_op jit(solution)/shard_map/all_to_all | solution.py:753
  300.8 3.0 collective-permute-start.6
  305.7 14.7 %collective-permute-start.7 = (bf16[128,2176]{1,0:T(8,128)(2,1)S(1)}, bf16[128,2176]{1,0:T(8,128)(2,1)S(1)}, u32[]{:S(2)}, u32[]{:S(2)}) collective-permute-start(bf16[128,2176]{1,0:T(8,128)(2,1)S(1)} %fusion), channel_id=1, source_target_pairs={{0,16},{8,24},{16,0},{24,8},{1,17},{9,25},{17,1},{25,9},{2,18},{10... | collective-permute-start | bytes 1671176 | tf_op jit(solution)/shard_map/ppermute | solution.py:700
  321.3 20.6 %all-to-all-start.4 = ((bf16[8,16,2176]{2,1,0:T(8,128)(2,1)}), bf16[8,16,2176]{2,1,0:T(8,128)(2,1)S(1)}, u32[]{:S(2)}, u32[]{:S(2)}) async-start(bf16[8,16,2176]{2,1,0:T(8,128)(2,1)} %bitcast.27), calls=%async_computation.4 | async-start | bytes 1114112 | tf_op jit(solution)/shard_map/all_to_all | solution.py:753
  341.9 0.8 copy-start.1
where the time goes:
time: 346 us; the launch traced here: 345 us
  Pallas kernels  189 us (55%)
  waiting for transfers between devices  72.2 us (21%)
  blocking collectives  42.6 us (12%)
  starting transfers between devices  29.1 us (8%)
  local copies, waits for them, and re-layouts  5.46 us (2%)
  other arithmetic  4.84 us (1%)
    pallas_call x1, Pallas kernels, attention_backward(): pl.pallas_call(attention_backward_kernel, grid=(pairs,), in_specs=[pair_c...  48.7 us
    all_to_all x1, blocking collectives, exchange(): lax.all_to_all(rows, BOTH, split_axis=0, concat_axis=0, tiled=True, axis_...  42.6 us
    pallas_call x1, Pallas kernels, attention_forward(): pl.pallas_call(attention_forward_kernel, grid=(pairs,), in_specs=[pair_co...  31.5 us
    all_to_all x3, waiting for transfers between devices, along_shard(): lax.all_to_all(blocks, 'shard', split_axis=0, concat_axis=0, tiled=True)  28.2 us
    all_to_all x1, waiting for transfers between devices, exchange(): lax.all_to_all(rows, BOTH, split_axis=0, concat_axis=0, tiled=True, axis_...  25.6 us
    pallas_call x1, Pallas kernels, combine(): call(combine_kernel, steps, [leading(CHUNK, D), leading(CHUNK, D), leadin...  20.6 us
    ppermute x8, waiting for transfers between devices, swap(): return lax.ppermute(block, axis, [(i, i ^ bits) for i in range(size)])  18.4 us
    all_to_all x3, starting transfers between devices, along_shard(): lax.all_to_all(blocks, 'shard', split_axis=0, concat_axis=0, tiled=True)  16.5 us
  transfers between devices with their start and end apart: 12, of which 8 were waited for; matrix products, arithmetic and copies ran while one was open for 2% of the time, Pallas kernels for 51%

commit v1 on v0

--- a/solution.py
+++ b/solution.py
@@ -17,7 +17,10 @@
 
 bf16 = jnp.bfloat16
 f32 = jnp.float32
-VMEM = pltpu.CompilerParams(vmem_limit_bytes=56 * 2**20)
+
+
+def vmem(mebibytes):
+    return pltpu.CompilerParams(vmem_limit_bytes=mebibytes * 2**20)
 
 
 def product(left_op, right_op):
@@ -32,9 +35,11 @@
     return lax.dot_general(left_op, right_op, (((1,), (1,)), ((), ())), preferred_element_type=f32)
 
 
-def attention_forward_kernel(q_ref, k_ref, v_ref, o_ref, lse_ref):
+def attention_forward_kernel(q_ref, k_ref, v_ref, o_ref, lse_ref, qt_ref, kt_ref, ot_ref):
     length = q_ref.shape[0]
     q_t = q_ref[...].T
+    qt_ref[...] = q_t
+    kt_ref[...] = k_ref[...].T
     v_t = v_ref[...].T
     zero = jnp.zeros((HEAD_DIM, length), bf16)
     ones = jnp.ones((16, length), bf16)
@@ -68,18 +73,20 @@
         outs.append(out[:HEAD_DIM] / total)
         lse_ref[0, h : h + 1, cols] = top + jnp.log2(total)
         if h == 1:
-            o_ref[cols, :] = jnp.concatenate(outs, 0).T.astype(bf16)
+            both = jnp.concatenate(outs, 0).astype(bf16)
+            ot_ref[:, cols] = both
+            o_ref[cols, :] = both.T
             outs = []
 
 
 def attention_backward_kernel(
-    q_ref, k_ref, v_ref, g_ref, o_ref, lse_ref, dq_ref, dk_ref, dv_ref, dq_t
+    qt_ref, kt_ref, k_ref, v_ref, gt_ref, ot_ref, lse_ref, out_ref, dq_t
 ):
-    length = q_ref.shape[0]
-    q_t = q_ref[...].T
-    g_t = g_ref[...].T
-    k_t = k_ref[...].T
-    both = (g_ref[...].astype(f32) * o_ref[...].astype(f32)).T
+    length = k_ref.shape[0]
+    q_t = qt_ref[...]
+    g_t = gt_ref[...]
+    k_t = kt_ref[...]
+    both = g_t.astype(f32) * ot_ref[...].astype(f32)
     zero = jnp.zeros((HEAD_DIM, length), bf16)
     heads = []
     for h in range(2):
@@ -123,15 +130,19 @@
         else:
             dq_t[rows, lo:] = dq_t[rows, lo:] + query_part
         if h == 1:
-            dk_ref[here, :] = (jnp.concatenate(key_grads, 0) * 0.125).T.astype(bf16)
-            dv_ref[here, :] = jnp.concatenate(value_grads, 0).T.astype(bf16)
+            out_ref[1, here, :] = (jnp.concatenate(key_grads, 0) * 0.125).astype(bf16).T
+            out_ref[2, here, :] = jnp.concatenate(value_grads, 0).astype(bf16).T
             key_grads = []
             value_grads = []
-    dq_ref[...] = (dq_t[...] * 0.125).T.astype(bf16)
+    out_ref[0] = (dq_t[...] * 0.125).astype(bf16).T
 
 
 def pair_columns(length, offset):
     return pl.BlockSpec((length, 2 * HEAD_DIM), lambda pair: (0, pair + offset))
+
+
+def pair_rows(length):
+    return pl.BlockSpec((2 * HEAD_DIM, length), lambda pair: (pair, 0))
 
 
 def attention_forward(qkv):
@@ -142,12 +153,13 @@
         attention_forward_kernel,
         grid=(pairs,),
         in_specs=[pair_columns(length, i * pairs) for i in range(3)],
-        out_specs=[pair_columns(length, 0), stats],
+        out_specs=[pair_columns(length, 0), stats] + [pair_rows(length)] * 3,
         out_shape=[
             jax.ShapeDtypeStruct((length, D), bf16),
             jax.ShapeDtypeStruct((pairs, 2, length), f32),
-        ],
-        compiler_params=VMEM,
+        ]
+        + [jax.ShapeDtypeStruct((D, length), bf16)] * 3,
+        compiler_params=vmem(56),
         cost_estimate=pl.CostEstimate(
             flops=10_000_000_000, bytes_accessed=8 * 2**20, transcendentals=0
         ),
@@ -155,35 +167,38 @@
     )(qkv, qkv, qkv)
 
 
-def attention_backward(qkv, grad, attended, lse):
+def attention_backward(qkv, query_t, key_t, grad_t, attended_t, lse):
     length = qkv.shape[0]
     pairs = D // (2 * HEAD_DIM)
     stats = pl.BlockSpec((1, 2, length), lambda pair: (pair, 0, 0))
     return pl.pallas_call(
         attention_backward_kernel,
         grid=(pairs,),
-        in_specs=[pair_columns(length, i * pairs) for i in range(3)]
-        + [pair_columns(length, 0), pair_columns(length, 0), stats],
-        out_specs=[pair_columns(length, 0)] * 3,
-        out_shape=[jax.ShapeDtypeStruct((length, D), bf16)] * 3,
+        in_specs=[pair_rows(length)] * 2
+        + [pair_columns(length, pairs), pair_columns(length, 2 * pairs)]
+        + [pair_rows(length)] * 2
+        + [stats],
+        out_specs=pl.BlockSpec((3, length, 2 * HEAD_DIM), lambda pair: (0, 0, pair)),
+        out_shape=jax.ShapeDtypeStruct((3, length, D), bf16),
         scratch_shapes=[pltpu.VMEM((2 * HEAD_DIM, length), f32)],
-        compiler_params=VMEM,
+        compiler_params=vmem(56),
         cost_estimate=pl.CostEstimate(
             flops=50_000_000_000, bytes_accessed=16 * 2**20, transcendentals=20_000_000
         ),
         name="attention_backward",
-    )(qkv, qkv, qkv, grad, attended, lse)
+    )(query_t, key_t, qkv, qkv, grad_t, attended_t, lse)
 
 
 CHUNK = 256
+COMBINE = 512
 LANES = 128
 BIAS_ROWS = 16
-SHARDS_A_STEP = 2
+SHARDS_A_STEP = 4
 GAIN_ONE = LANES - 2
 GAIN_TWO = LANES - 1
 
 
-def call(kernel, grid, in_specs, out_specs, out_shape, scratch, flops, moved, name):
+def call(kernel, grid, in_specs, out_specs, out_shape, scratch, flops, moved, name, limit=56):
     return pl.pallas_call(
         kernel,
         grid=(grid,),
@@ -191,7 +206,7 @@
         out_specs=out_specs,
         out_shape=out_shape,
         scratch_shapes=scratch,
-        compiler_params=VMEM,
+        compiler_params=vmem(limit),
         cost_estimate=pl.CostEstimate(flops=flops, bytes_accessed=moved, transcendentals=0),
         name=name,
     )
@@ -259,16 +274,17 @@
 
 
 def pack_kernel(first_ref, bias_ref, second_ref, out_ref):
-    hidden = first_ref.shape[2]
-    out_ref[0, :D, :] = first_ref[0].astype(bf16)
-    out_ref[0, D : D + BIAS_ROWS, :] = jnp.broadcast_to(
-        bias_ref[pl.ds(pl.program_id(0), 1), :], (BIAS_ROWS, hidden)
-    ).astype(bf16)
-    for c in range(D // hidden):
-        start = D + BIAS_ROWS + c * hidden
-        out_ref[0, start : start + hidden, :] = second_ref[
-            0, :, c * hidden : (c + 1) * hidden
-        ].astype(bf16)
+    held, _, hidden = first_ref.shape
+    for i in range(held):
+        out_ref[i, :D, :] = first_ref[i].astype(bf16)
+        out_ref[i, D : D + BIAS_ROWS, :] = jnp.broadcast_to(
+            bias_ref[pl.ds(pl.program_id(0) * held + i, 1), :], (BIAS_ROWS, hidden)
+        ).astype(bf16)
+        for c in range(D // hidden):
+            start = D + BIAS_ROWS + c * hidden
+            out_ref[i, start : start + hidden, :] = second_ref[
+                i, :, c * hidden : (c + 1) * hidden
+            ].astype(bf16)
 
 
 def pack_weights(w_in, b_in, w_exp_out):
@@ -276,9 +292,9 @@
     total = 2 * D + BIAS_ROWS
     return call(
         pack_kernel,
-        local,
-        [leading(1, D, hidden), fixed(local, hidden), leading(1, hidden, D)],
-        leading(1, total, hidden),
+        local // 2,
+        [leading(2, D, hidden), fixed(local, hidden), leading(2, hidden, D)],
+        leading(2, total, hidden),
         jax.ShapeDtypeStruct((local, total, hidden), bf16),
         [],
         1_000_000,
@@ -317,24 +333,25 @@
     )(packed)
 
 
-def expert_part(rows_ref, w_ref, i):
+def expert_products(rows_ref, w_ref, i):
     hidden = w_ref.shape[2]
-    first = w_ref[i, :D, :]
     bias = w_ref[i, D : D + BIAS_ROWS, :].astype(f32)[:1]
-    pre_act = product(rows_ref[:, :D], first) + bias
-    sigma = 0.5 + 0.5 * jnp.tanh(0.5 * pre_act)
+    pre_act = product(rows_ref[:, :D], w_ref[i, :D, :]) + bias
     hidden_grad = jnp.zeros_like(pre_act)
-    second = []
     for c in range(D // hidden):
         start = D + BIAS_ROWS + c * hidden
-        second.append(w_ref[i, start : start + hidden, :])
         cols = slice(D + c * hidden, D + (c + 1) * hidden)
-        hidden_grad = hidden_grad + against_rows(rows_ref[:, cols], second[-1])
-    active = (pre_act * sigma).astype(bf16)
-    pre_grad = (
-        hidden_grad.astype(bf16).astype(f32) * (sigma * (1.0 + pre_act * (1.0 - sigma)))
-    ).astype(bf16)
-    return first, second, active, pre_grad
+        hidden_grad = hidden_grad + against_rows(
+            rows_ref[:, cols], w_ref[i, start : start + hidden, :]
+        )
+    return pre_act, hidden_grad
+
+
+def activate(pre_act, hidden_grad):
+    sigma = 0.5 + 0.5 * jnp.tanh(0.5 * pre_act)
+    slope = sigma * (1.0 + pre_act * (1.0 - sigma))
+    pre_grad = (hidden_grad.astype(bf16).astype(f32) * slope).astype(bf16)
+    return (pre_act * sigma).astype(bf16), pre_grad
 
 
 def expert_kernel(rows_ref, w_ref, out_ref, results, mixed_grad):
@@ -342,9 +359,17 @@
     held, _, hidden = w_ref.shape
     chunks = D // hidden
     parts = [None] * (chunks + 1)
+    later = expert_products(rows_ref, w_ref, 0)
     for i in range(held):
-        first, second, active, pre_grad = expert_part(rows_ref, w_ref, i)
-        more = [product(active, block) for block in second] + [against_rows(pre_grad, first)]
+        now = later
+        if i + 1 < held:
+            later = expert_products(rows_ref, w_ref, i + 1)
+        active, pre_grad = activate(*now)
+        more = []
+        for c in range(chunks):
+            start = D + BIAS_ROWS + c * hidden
+            more.append(product(active, w_ref[i, start : start + hidden, :]))
+        more.append(against_rows(pre_grad, w_ref[i, :D, :]))
         parts = more if i == 0 else [old + new for old, new in zip(parts, more)]
 
     @pl.when(step == 0)
@@ -389,7 +414,7 @@
     def _():
         rows_t[...] = rows_ref[:, :D].T
 
-    _, _, active, pre_grad = expert_part(rows_ref, w_ref, 0)
+    active, pre_grad = activate(*expert_products(rows_ref, w_ref, 0))
     out_ref[0, :D, :] = product(rows_t[...], pre_grad).astype(bf16)
     out_ref[0, D : D + BIAS_ROWS, :] = jnp.broadcast_to(
         jnp.sum(pre_grad.astype(f32), axis=0, keepdims=True), (BIAS_ROWS, hidden)
@@ -415,13 +440,14 @@
         8 * count * D * shards * hidden,
         14 * 2**20,
         "expert_grads",
+        63,
     )(rows, weights)
 
 
-def project_kernel(tokens_ref, w_ref, ctrl_ref, qkv_ref, normed_ref):
+def project_kernel(tokens_ref, w_ref, ctrl_ref, qkv_ref, normed_t_ref):
     scaled, _ = normalise(tokens_ref[...].astype(f32))
     normed = (scaled * gain_of(ctrl_ref[...], GAIN_ONE)).astype(bf16)
-    normed_ref[...] = normed
+    normed_t_ref[...] = normed.T
     qkv_ref[...] = product(normed, w_ref[...]).astype(bf16)
 
 
@@ -431,8 +457,8 @@
         project_kernel,
         length // CHUNK,
         [leading(CHUNK, D), small_columns(3 * D, 0), small_columns(LANES, 4 * D)],
-        [leading(CHUNK, 3 * D), leading(CHUNK, D)],
-        [jax.ShapeDtypeStruct((length, 3 * D), bf16), jax.ShapeDtypeStruct((length, D), bf16)],
+        [leading(CHUNK, 3 * D), pl.BlockSpec((D, CHUNK), lambda i: (0, i))],
+        [jax.ShapeDtypeStruct((length, 3 * D), bf16), jax.ShapeDtypeStruct((D, length), bf16)],
         [],
         6 * length * D * D,
         12 * 2**20,
@@ -526,15 +552,15 @@
     high = chosen_grad.astype(bf16)
     low = (chosen_grad - high.astype(f32)).astype(bf16)
     prob_grad = against_rows(high, onehot) + against_rows(low, onehot)
-    weighted = (probs * prob_grad).reshape(CHUNK // GROUP, GROUP, LANES)
+    weighted = (probs * prob_grad).reshape(COMBINE // GROUP, GROUP, LANES)
     total = jnp.broadcast_to(jnp.sum(weighted, axis=1, keepdims=True), weighted.shape)
-    logit_grad = (probs * (prob_grad - total.reshape(CHUNK, LANES))).astype(bf16)
+    logit_grad = (probs * (prob_grad - total.reshape(COMBINE, LANES))).astype(bf16)
     normed_grad = product(chosen, mixed_grad) + against_rows(logit_grad, ctrl_ref[...])
     gain_part = jnp.sum(normed_grad * scaled, axis=0, keepdims=True)
     residual_grad = grad.astype(f32) + norm_input_grad(normed_grad, scaled, inverse, gain)
     residual_grad_ref[...] = residual_grad
     branch = residual_grad.astype(bf16)
-    attended_grad_ref[...] = against_rows(branch, wo_ref[...]).astype(bf16)
+    attended_grad_ref[...] = against_rows(wo_ref[...], branch).astype(bf16)
     wo_part = transposed_product(attended_ref[...], branch)
     ctrl_part = transposed_product(normed, logit_grad)
 
@@ -559,83 +585,76 @@
 
 def combine(residual, grad_out, probs, attended, small, routes, slots, back):
     length = residual.shape[0]
-    steps = length // CHUNK
+    steps = length // COMBINE
     count = slots.shape[0]
     return call(
         combine_kernel,
         steps,
-        [leading(CHUNK, D), leading(CHUNK, D), leading(CHUNK, LANES), leading(CHUNK, D)]
+        [leading(COMBINE, D), leading(COMBINE, D), leading(COMBINE, LANES), leading(COMBINE, D)]
         + [small_columns(D, 3 * D), small_columns(LANES, 4 * D), leading(1, 1, count // steps)]
         + [leading(count // steps, 1), fixed(*back.shape)],
-        [leading(CHUNK, D)] * 3 + [fixed(D, D + LANES)],
+        [leading(COMBINE, D)] * 2
+        + [pl.BlockSpec((D, COMBINE), lambda i: (0, i)), fixed(D, D + LANES)],
         [
             jax.ShapeDtypeStruct((length, D), bf16),
             jax.ShapeDtypeStruct((length, D), f32),
-            jax.ShapeDtypeStruct((length, D), bf16),
+            jax.ShapeDtypeStruct((D, length), bf16),
             jax.ShapeDtypeStruct((D, D + LANES), f32),
         ],
         [pltpu.VMEM((1, D), f32)],
         6 * length * D * D,
         24 * 2**20,
         "combine",
+        63,
     )(
         residual, grad_out, probs, attended, small, small,
         routes.reshape(steps, 1, count // steps), slots.reshape(count, 1), back,
     )
 
 
-def weight_grad_kernel(
-    core_ref, normed_ref, q_ref, k_ref, v_ref, sums_ref, away_ref, kept_ref, total
-):
+def weight_grad_kernel(core_ref, normed_t_ref, grad_ref, sums_ref, away_ref, kept_ref):
     step = pl.program_id(0)
-    normed_t = normed_ref[...].T
-
-    for i, ref in enumerate((q_ref, k_ref, v_ref)):
-        cols = slice(i * D, (i + 1) * D)
-        part = product(normed_t, ref[...])
+    count, rows, _ = kept_ref.shape
+    for x in range(count):
+        mine = pl.ds(pl.multiple_of((2 * x + core_ref[0]) * rows, rows), rows)
+        other = pl.ds(pl.multiple_of((2 * x + 1 - core_ref[0]) * rows, rows), rows)
+        kept = product(normed_t_ref[mine, :], grad_ref[0])
+        away = product(normed_t_ref[other, :], grad_ref[0]).astype(bf16)
+        for i in range(3):
+
+            @pl.when(step == i)
+            def _(x=x, i=i, kept=kept, away=away):
+                kept_ref[x, :, i * D : (i + 1) * D] = kept
+                away_ref[x, :, i * D : (i + 1) * D] = away
 
         @pl.when(step == 0)
-        def _(cols=cols, part=part):
-            total[:, cols] = part
-
-        @pl.when(step > 0)
-        def _(cols=cols, part=part):
-            total[:, cols] = total[:, cols] + part
-
-    @pl.when(step == pl.num_programs(0) - 1)
-    def _():
-        rows = kept_ref.shape[1]
-        for x in range(kept_ref.shape[0]):
-            mine = pl.ds(pl.multiple_of((2 * x + core_ref[0]) * rows, rows), rows)
-            other = pl.ds(pl.multiple_of((2 * x + 1 - core_ref[0]) * rows, rows), rows)
-            kept_ref[x, :, : 3 * D] = total[mine, :]
+        def _(x=x, mine=mine, other=other):
             kept_ref[x, :, 3 * D :] = sums_ref[mine, :]
-            away_ref[x, :, : 3 * D] = total[other, :].astype(bf16)
             away_ref[x, :, 3 * D :] = sums_ref[other, :].astype(bf16)
 
 
-def weight_grads(normed, query_grad, key_grad, value_grad, sums, core, n_expert):
-    length = normed.shape[0]
+def weight_grads(normed_t, grads, sums, core, n_expert):
+    length = normed_t.shape[1]
     width = sums.shape[1]
-    chunk = 512
     shape = (n_expert // 2, D // n_expert, 3 * D + width)
     return call(
         weight_grad_kernel,
-        length // chunk,
-        [pl.BlockSpec(memory_space=pltpu.SMEM)] + [leading(chunk, D)] * 4 + [fixed(D, width)],
+        3,
+        [pl.BlockSpec(memory_space=pltpu.SMEM), fixed(D, length), leading(1, length, D)]
+        + [fixed(D, width)],
         [fixed(*shape), fixed(*shape)],
         [jax.ShapeDtypeStruct(shape, bf16), jax.ShapeDtypeStruct(shape, f32)],
-        [pltpu.VMEM((D, 3 * D), f32)],
+        [],
         6 * length * D * D,
         12 * 2**20,
         "weight_grads",
-    )(core, normed, query_grad, key_grad, value_grad, sums)
-
-
-def input_grad_kernel(q_ref, k_ref, v_ref, w_ref, ctrl_ref, tokens_ref, residual_grad_ref, out_ref):
-    upstream = against_rows(q_ref[...], w_ref[:, :D])
-    upstream = upstream + against_rows(k_ref[...], w_ref[:, D : 2 * D])
-    upstream = upstream + against_rows(v_ref[...], w_ref[:, 2 * D :])
+    )(core, normed_t, grads, sums)
+
+
+def input_grad_kernel(grads_ref, w_ref, ctrl_ref, tokens_ref, residual_grad_ref, out_ref):
+    upstream = against_rows(grads_ref[0], w_ref[:, :D])
+    upstream = upstream + against_rows(grads_ref[1], w_ref[:, D : 2 * D])
+    upstream = upstream + against_rows(grads_ref[2], w_ref[:, 2 * D :])
     scaled, inverse = normalise(tokens_ref[...].astype(f32))
     gain = gain_of(ctrl_ref[...], GAIN_ONE)
     out_ref[...] = (
@@ -643,12 +662,12 @@
     ).astype(bf16)
 
 
-def input_grads(query_grad, key_grad, value_grad, small, tokens, residual_grad):
+def input_grads(grads, small, tokens, residual_grad):
     length = tokens.shape[0]
     return call(
         input_grad_kernel,
         length // CHUNK,
-        [leading(CHUNK, D)] * 3
+        [pl.BlockSpec((3, CHUNK, D), lambda i: (0, i, 0))]
         + [small_columns(3 * D, 0), small_columns(LANES, 4 * D)]
         + [leading(CHUNK, D), leading(CHUNK, D)],
         leading(CHUNK, D),
@@ -657,7 +676,7 @@
         6 * length * D * D,
         18 * 2**20,
         "input_grads",
-    )(query_grad, key_grad, value_grad, small, small, tokens, residual_grad)
+    )(grads, small, small, tokens, residual_grad)
 
 
 def finish_kernel(pieces_ref, own_ref, q_ref, k_ref, v_ref, o_ref, ctrl_ref, one_ref, two_ref):
@@ -692,6 +711,7 @@
         1_000_000,
         1_000_000,
         "finish",
+        8,
     )(pieces, own)
 
 
@@ -820,8 +840,8 @@
     held = spread(held, outer, inner, here >> (inner.bit_length() - 1))
     small = gather_expert(held)
 
-    qkv, normed_one = project(tokens, small)
-    attended, lse = attention_forward(qkv)
+    qkv, normed_t = project(tokens, small)
+    attended, lse, query_t, key_t, attended_t = attention_forward(qkv)
     residual, probs, outgoing = mix(
         attended, tokens, grad_out, small, routes, slots, experts * CAP
     )
@@ -832,16 +852,14 @@
     expert_sums = expert_grads(arrived, expert_w)
     returned, expert_sums = lax.optimization_barrier((returned, expert_sums))
     expert_sums = from_experts(expert_sums, copies)
-    output, residual_grad, attended_grad, sums = combine(
+    output, residual_grad, grad_t, sums = combine(
         residual, grad_out, probs, attended, small, routes, slots, returned
     )
-    query_grad, key_grad, value_grad = attention_backward(qkv, attended_grad, attended, lse)
+    grads = attention_backward(qkv, query_t, key_t, grad_t, attended_t, lse)
     core = (lax.axis_index("expert") & 1).reshape(1)
-    away, kept = weight_grads(
-        normed_one, query_grad, key_grad, value_grad, sums, core, lax.axis_size("expert")
-    )
+    away, kept = weight_grads(normed_t, grads, sums, core, lax.axis_size("expert"))
     late = sum_expert(away, kept)
-    input_grad = input_grads(query_grad, key_grad, value_grad, small, tokens, residual_grad)
+    input_grad = input_grads(grads, small, tokens, residual_grad)
     late, input_grad, expert_sums = lax.optimization_barrier((late, input_grad, expert_sums))
     pieces = along_shard(late.astype(bf16).reshape((n_shard,) + own.shape))
     w_in_grad, b_in_grad, w_exp_out_grad = unpack_grads(expert_sums)

time: 346 us -> 337 us (0.974)
  Pallas kernels: 189 us -> 182 us
    pallas_call x5, Pallas kernels: 99.7 us -> 93.9 us  [the longest x1 50 us: attention_backward(): pl.pallas_call(attention_backward_kernel, grid=(pairs,), in_specs=[pair_r...]
  transfers between devices with their start and end apart: 12 -> 12, of which waited for: 8 -> 8; matrix products, arithmetic and copies ran while one was open for 2% -> 3% of each run, Pallas kernels for 51% -> 50%
where the time goes in v1:
time: 337 us; the launch traced here: 336 us
  Pallas kernels  182 us (54%)
  waiting for transfers between devices  70.9 us (21%)
  blocking collectives  42.6 us (13%)
  starting transfers between devices  29.9 us (9%)
  other arithmetic  4.89 us (1%)
  local copies, waits for them, and re-layouts  4.18 us (1%)
    pallas_call x1, Pallas kernels, attention_backward(): pl.pallas_call(attention_backward_kernel, grid=(pairs,), in_specs=[pair_r...  50 us
    all_to_all x1, blocking collectives, exchange(): lax.all_to_all(rows, BOTH, split_axis=0, concat_axis=0, tiled=True, axis_...  42.6 us
    pallas_call x1, Pallas kernels, attention_forward(): pl.pallas_call(attention_forward_kernel, grid=(pairs,), in_specs=[pair_co...  31.9 us
    all_to_all x3, waiting for transfers between devices, along_shard(): lax.all_to_all(blocks, 'shard', split_axis=0, concat_axis=0, tiled=True)  27.5 us
    all_to_all x1, waiting for transfers between devices, exchange(): lax.all_to_all(rows, BOTH, split_axis=0, concat_axis=0, tiled=True, axis_...  24.9 us
    ppermute x8, waiting for transfers between devices, swap(): return lax.ppermute(block, axis, [(i, i ^ bits) for i in range(size)])  18.5 us
    pallas_call x1, Pallas kernels, combine(): call(combine_kernel, steps, [leading(COMBINE, D), leading(COMBINE, D), le...  17.4 us
    all_to_all x3, starting transfers between devices, along_shard(): lax.all_to_all(blocks, 'shard', split_axis=0, concat_axis=0, tiled=True)  16.5 us
  transfers between devices with their start and end apart: 12, of which 8 were waited for; matrix products, arithmetic and copies ran while one was open for 3% of the time, Pallas kernels for 50%

profile of v1, /device:TPU:0, one launch (start us, length us, event | category | flops | bytes accessed | tf_op | source)
XLA Modules:
  0.0 335.7 jit_solution(214550223698105899)
XLA Ops:
  0.6 1.5 pack_small.1.own_ref
  2.2 3.0 collective-permute-start
  5.2 0.9 bitcast_dynamic-update-slice_fusion.5
  6.1 1.6 collective-permute-done
  7.7 2.1 collective-permute-start.1
  9.8 2.6 collective-permute-start.2
  12.4 0.0 collective-permute-start.3
  12.4 5.8 %pack_weights.1 = bf16[8,1040,256]{2,1,0:T(8,128)(2,1)} custom-call(f32[8,512,256]{2,1,0:T(8,128)} %first_ref, f32[8,256]{1,0:T(8,128)} %bias_ref.1, f32[8,256,512]{2,1,0:T(8,128)} %second_ref), custom_call_target="tpu_custom_call" | custom-call | flops 1000000 | bytes 12582912 | tf_op jit(solution)/shard_map/pack_weights/pallas_call | solution.py:293
  18.2 6.1 %all-to-all-start = ((bf16[8,1040,256]{2,1,0:T(8,128)(2,1)}), bf16[8,1040,256]{2,1,0:T(8,128)(2,1)}, u32[]{:S(2)}, u32[]{:S(2)}) async-start(bf16[8,1040,256]{2,1,0:T(8,128)(2,1)} %pack_weights.1), calls=%async_computation | async-start | bytes 8519680 | tf_op jit(solution)/shard_map/all_to_all | solution.py:773
  24.3 0.0 collective-permute-done.1
  24.4 0.0 collective-permute-done.2
  24.4 0.0 collective-permute-done.3
  24.4 1.6 collective-permute-start.4
  26.0 0.0 copy-start.1
  26.0 10.6 %collective-permute-done.4 = bf16[128,2176]{1,0:T(8,128)(2,1)S(1)} collective-permute-done((bf16[128,2176]{1,0:T(8,128)(2,1)S(1)}, bf16[128,2176]{1,0:T(8,128)(2,1)S(1)}, u32[]{:S(2)}, u32[]{:S(2)}) %collective-permute-start.4) | collective-permute-done | bytes 557088 | tf_op jit(solution)/shard_map/ppermute | solution.py:720
  36.6 0.1 select_bitcast_fusion.3
  36.7 0.1 pad_maximum_fusion.1
  36.9 0.1 collective-permute-start.5
  36.9 0.0 copy-done.1
  37.0 0.1 copy.43
  37.1 0.2 fusion.1
  37.3 0.1 copy.44
  37.4 0.7 reshape_reshape.6.slots_ref
  38.1 0.7 reshape.69
  38.8 0.9 collective-permute-done.5
  39.7 0.2 select_bitcast_fusion.1
  39.9 1.6 pad_maximum_fusion
  41.5 10.0 %project.1 = (bf16[2048,1536]{1,0:T(8,128)(2,1)}, bf16[512,2048]{1,0:T(8,128)(2,1)}) custom-call(bf16[2048,512]{1,0:T(8,128)(2,1)} %tokens_ref.5, bf16[512,2176]{1,0:T(8,128)(2,1)} %bitcast.46, bf16[512,2176]{1,0:T(8,128)(2,1)} %bitcast.47), custom_call_target="tpu_custom_call" | custom-call | flops 3221225472 | bytes 12582912 | tf_op jit(solution)/shard_map/project/pallas_call | solution.py:456
  51.5 31.9 %attention_forward.1 = (bf16[2048,512]{1,0:T(8,128)(2,1)}, f32[4,2,2048]{2,1,0:T(2,128)}, bf16[512,2048]{1,0:T(8,128)(2,1)}, bf16[512,2048]{1,0:T(8,128)(2,1)}, bf16[512,2048]{1,0:T(8,128)(2,1)}) custom-call(bf16[2048,1536]{1,0:T(8,128)(2,1)} %get-tuple-element.49.q_ref.k_ref.v_ref, bf16[2048,1536]{1,0:T(8,128)(2,1)} %get-tuple-element.49.q_ref.k_ref.v_ref, ...), custom_call_target="tpu_custom_call" | custom-call | flops 10000000000 | bytes 8388608 | tf_op jit(solution)/shard_map/attention_forward/pallas_call | solution.py:152
  83.5 13.5 %mix.1 = (f32[2048,512]{1,0:T(8,128)}, f32[2048,128]{1,0:T(8,128)}, bf16[768,1024]{1,0:T(8,128)(2,1)}) custom-call(bf16[2048,512]{1,0:T(8,128)(2,1)} %get-tuple-element.50.attended_ref, bf16[2048,512]{1,0:T(8,128)(2,1)} %tokens_ref.5, bf16[2048,512]{1,0:T(8,128)(2,1)} %grad_ref.3, bf16[512,2176]{1,0:T(8,128)(2,1)} %bitcast.48, bf16[512,2176]{1,0:T(8,128)(2,1)} %bitcast.49, ...), custom_call_target="tpu_custom_call" | custom-call | flops 2147483648 | bytes 14680064 | tf_op jit(solution)/shard_map/mix/pallas_call | solution.py:511
  97.0 20.0 %all-to-all-done.w_ref = bf16[8,1040,256]{2,1,0:T(8,128)(2,1)} async-done(((bf16[8,1040,256]{2,1,0:T(8,128)(2,1)}), bf16[8,1040,256]{2,1,0:T(8,128)(2,1)}, u32[]{:S(2)}, u32[]{:S(2)}) %all-to-all-start) | async-done | bytes 4259872 | tf_op jit(solution)/shard_map/all_to_all | solution.py:773
  116.9 42.6 %all_to_all.38 = bf16[32,24,1024]{2,1,0:T(8,128)(2,1)} all-to-all(bf16[32,24,1024]{2,1,0:T(8,128)(2,1)} %bitcast.58), channel_id=1, replica_groups=mesh['expert'=4,'shard'=8] {'expert','shard'}, dimensions={0} | all-to-all | bytes 3145728 | tf_op jit(solution)/shard_map/all_to_all | solution.py:798
  159.5 11.1 %expert_rows.1 = bf16[768,1024]{1,0:T(8,128)(2,1)} custom-call(bf16[768,1024]{1,0:T(8,128)(2,1)} %bitcast.55, bf16[8,1040,256]{2,1,0:T(8,128)(2,1)} %all-to-all-done.w_ref), custom_call_target="tpu_custom_call" | custom-call | flops 6442450944 | bytes 8388608 | tf_op jit(solution)/shard_map/expert_rows/pallas_call | solution.py:397
  170.6 3.4 %all-to-all-start.2 = ((bf16[32,24,1024]{2,1,0:T(8,128)(2,1)}), bf16[32,24,1024]{2,1,0:T(8,128)(2,1)}, u32[]{:S(2)}, u32[]{:S(2)}) async-start(bf16[32,24,1024]{2,1,0:T(8,128)(2,1)} %bitcast.57), calls=%async_computation.2 | async-start | bytes 3145728 | tf_op jit(solution)/shard_map/all_to_all | solution.py:798
  174.0 0.8 reshape_reshape.8.slots_ref
  174.9 0.7 reshape.70
  175.6 12.4 %expert_grads.1 = bf16[8,1040,256]{2,1,0:T(8,128)(2,1)} custom-call(bf16[768,1024]{1,0:T(8,128)(2,1)} %bitcast.56, bf16[8,1040,256]{2,1,0:T(8,128)(2,1)} %all-to-all-done.w_ref), custom_call_target="tpu_custom_call" | custom-call | flops 6442450944 | bytes 14680064 | tf_op jit(solution)/shard_map/expert_grads/pallas_call | solution.py:433
  188.0 24.9 %all-to-all-done.2 = bf16[32,24,1024]{2,1,0:T(8,128)(2,1)} async-done(((bf16[32,24,1024]{2,1,0:T(8,128)(2,1)}), bf16[32,24,1024]{2,1,0:T(8,128)(2,1)}, u32[]{:S(2)}, u32[]{:S(2)}) %all-to-all-start.2) | async-done | bytes 1572896 | tf_op jit(solution)/shard_map/all_to_all | solution.py:798
  212.9 4.6 %all-to-all-start.3 = ((bf16[8,1040,256]{2,1,0:T(8,128)(2,1)}), bf16[8,1040,256]{2,1,0:T(8,128)(2,1)}, u32[]{:S(2)}, u32[]{:S(2)}) async-start(bf16[8,1040,256]{2,1,0:T(8,128)(2,1)} %expert_grads.1), calls=%async_computation.3 | async-start | bytes 8519680 | tf_op jit(solution)/shard_map/all_to_all | solution.py:773
  217.5 17.4 %combine.1 = (bf16[2048,512]{1,0:T(8,128)(2,1)}, f32[2048,512]{1,0:T(8,128)}, bf16[512,2048]{1,0:T(8,128)(2,1)}, f32[512,640]{1,0:T(8,128)}) custom-call(f32[2048,512]{1,0:T(8,128)} %get-tuple-element.51.residual_ref, bf16[2048,512]{1,0:T(8,128)(2,1)} %grad_ref.3, f32[2048,128]{1,0:T(8,128)} %get-tuple-element.52.probs_ref, ...), custom_call_target="tpu_custom_call" | custom-call | flops 3221225472 | bytes 25165824 | tf_op jit(solution)/shard_map/combine/pallas_call | solution.py:590
  234.9 50.0 %attention_backward.1.grad_ref.grads_ref = bf16[3,2048,512]{2,1,0:T(8,128)(2,1)} custom-call(bf16[512,2048]{1,0:T(8,128)(2,1)} %get-tuple-element.61.qt_ref, bf16[512,2048]{1,0:T(8,128)(2,1)} %get-tuple-element.62.kt_ref, bf16[2048,1536]{1,0:T(8,128)(2,1)} %get-tuple-element.49.q_ref.k_ref.v_ref, bf16[2048,1536]{1,0:T(8,128)(2,1)} %get-tuple-element.49.q_ref.k_ref.v_ref, ...), custom_call_target="tpu_custom_call" | custom-call | flops 49999998976 | bytes 16777216 | tf_op jit(solution)/shard_map/attention_backward/pallas_call | solution.py:174
  284.9 9.0 %weight_grads.1 = (bf16[2,128,2176]{2,1,0:T(8,128)(2,1)}, f32[2,128,2176]{2,1,0:T(8,128)}) custom-call(s32[1]{0:T(128)} %bitcast.23.core_ref, bf16[512,2048]{1,0:T(8,128)(2,1)} %get-tuple-element.60.normed_t_ref, bf16[3,2048,512]{2,1,0:T(8,128)(2,1)} %attention_backward.1.grad_ref.grads_ref, f32[512,640]{1,0:T(8,128)} %get-tuple-element.66.sums_ref), custom_call_target="tpu_custom_call" | custom-call | flops 3221225472 | bytes 12582912 | tf_op jit(solution)/shard_map/weight_grads/pallas_call | solution.py:640
  293.9 0.0 collective-permute-start.6
  293.9 3.0 collective-permute-done.6
  296.8 1.8 convert_add_fusion
  298.6 0.1 fusion
  298.7 0.6 collective-permute-start.7
  299.3 11.7 %input_grads.1 = bf16[2048,512]{1,0:T(8,128)(2,1)} custom-call(bf16[3,2048,512]{2,1,0:T(8,128)(2,1)} %attention_backward.1.grad_ref.grads_ref, bf16[512,2176]{1,0:T(8,128)(2,1)} %bitcast.52, bf16[512,2176]{1,0:T(8,128)(2,1)} %bitcast.53, bf16[2048,512]{1,0:T(8,128)(2,1)} %tokens_ref.5, f32[2048,512]{1,0:T(8,128)} %get-tuple-element.69.residual_grad_ref), custom_call_target="tpu_custom_call" | custom-call | flops 3221225472 | bytes 18874368 | tf_op jit(solution)/shard_map/input_grads/pallas_call | solution.py:667
  311.0 2.5 collective-permute-done.7
  313.5 0.9 bitcast_add_fusion
  314.4 0.0 all-to-all-done.3.in_ref
  314.4 5.9 %all-to-all-start.4 = ((bf16[8,16,2176]{2,1,0:T(8,128)(2,1)}), bf16[8,16,2176]{2,1,0:T(8,128)(2,1)S(1)}, u32[]{:S(2)}, u32[]{:S(2)}) async-start(bf16[8,16,2176]{2,1,0:T(8,128)(2,1)} %bitcast.27), calls=%async_computation.4 | async-start | bytes 1114112 | tf_op jit(solution)/shard_map/all_to_all | solution.py:773
  320.3 0.0 copy-start
  320.3 7.2 %unpack_grads.1 = (f32[8,512,256]{2,1,0:T(8,128)}, f32[8,256]{1,0:T(8,128)}, f32[8,256,512]{2,1,0:T(8,128)}) custom-call(bf16[8,1040,256]{2,1,0:T(8,128)(2,1)} %all-to-all-done.3.in_ref), custom_call_target="tpu_custom_call" | custom-call | flops 1000000 | bytes 12582912 | tf_op jit(solution)/shard_map/unpack_grads/pallas_call | solution.py:319
  327.5 7.5 %all-to-all-done.4.pieces_ref = bf16[8,16,2176]{2,1,0:T(8,128)(2,1)S(1)} async-done(((bf16[8,16,2176]{2,1,0:T(8,128)(2,1)}), bf16[8,16,2176]{2,1,0:T(8,128)(2,1)S(1)}, u32[]{:S(2)}, u32[]{:S(2)}) %all-to-all-start.4) | async-done | bytes 557088 | tf_op jit(solution)/shard_map/all_to_all | solution.py:773
  335.0 0.0 copy-done
  335.0 0.7 finish.1
  (11 shorter events, 0.2 us)
Async XLA Ops:
  2.2 5.5 %collective-permute-start = (bf16[16,2176]{1,0:T(8,128)(2,1)}, bf16[16,2176]{1,0:T(8,128)(2,1)S(1)}, u32[]{:S(2)}, u32[]{:S(2)}) collective-permute-start(bf16[16,2176]{1,0:T(8,128)(2,1)} %pack_small.1.own_ref), channel_id=1, source_target_pairs={{0,1},{1,0},{2,3},{3,2},{4,5},{5,4},{6,7},{7,6},{8,9},{9,8},{10,11... | collective-permute-start | bytes 208904 | tf_op jit(solution)/shard_map/ppermute | solution.py:720
  7.7 16.7 %collective-permute-start.1 = (bf16[32,2176]{1,0:T(8,128)(2,1)S(1)}, bf16[32,2176]{1,0:T(8,128)(2,1)S(1)}, u32[]{:S(2)}, u32[]{:S(2)}) collective-permute-start(bf16[32,2176]{1,0:T(8,128)(2,1)S(1)} %bitcast.59), channel_id=1, source_target_pairs={{0,2},{1,3},{2,0},{3,1},{4,6},{5,7},{6,4},{7,5},{8,10},{9,11},{10,... | collective-permute-start | bytes 417800 | tf_op jit(solution)/shard_map/ppermute | solution.py:720
  9.8 14.6 %collective-permute-start.2 = (bf16[32,2176]{1,0:T(8,128)(2,1)S(1)}, bf16[32,2176]{1,0:T(8,128)(2,1)S(1)}, u32[]{:S(2)}, u32[]{:S(2)}) collective-permute-start(bf16[32,2176]{1,0:T(8,128)(2,1)S(1)} %bitcast.60), channel_id=1, source_target_pairs={{0,4},{1,5},{2,6},{3,7},{4,0},{5,1},{6,2},{7,3},{8,12},{9,13},{10,... | collective-permute-start | bytes 417800 | tf_op jit(solution)/shard_map/ppermute | solution.py:720
  12.4 12.0 %collective-permute-start.3 = (bf16[32,2176]{1,0:T(8,128)(2,1)S(1)}, bf16[32,2176]{1,0:T(8,128)(2,1)S(1)}, u32[]{:S(2)}, u32[]{:S(2)}) collective-permute-start(bf16[32,2176]{1,0:T(8,128)(2,1)S(1)} %bitcast.61), channel_id=1, source_target_pairs={{0,6},{1,7},{2,4},{3,5},{4,2},{5,3},{6,0},{7,1},{8,14},{9,15},{10,... | collective-permute-start | bytes 417800 | tf_op jit(solution)/shard_map/ppermute | solution.py:720
  18.2 98.8 %all-to-all-start = ((bf16[8,1040,256]{2,1,0:T(8,128)(2,1)}), bf16[8,1040,256]{2,1,0:T(8,128)(2,1)}, u32[]{:S(2)}, u32[]{:S(2)}) async-start(bf16[8,1040,256]{2,1,0:T(8,128)(2,1)} %pack_weights.1), calls=%async_computation | async-start | bytes 8519680 | tf_op jit(solution)/shard_map/all_to_all | solution.py:773
  24.4 12.2 %collective-permute-start.4 = (bf16[128,2176]{1,0:T(8,128)(2,1)S(1)}, bf16[128,2176]{1,0:T(8,128)(2,1)S(1)}, u32[]{:S(2)}, u32[]{:S(2)}) collective-permute-start(bf16[128,2176]{1,0:T(8,128)(2,1)S(1)} %bitcast.54), channel_id=1, source_target_pairs={{0,16},{8,24},{16,0},{24,8},{1,17},{9,25},{17,1},{25,9},{2,18},{10... | collective-permute-start | bytes 1671176 | tf_op jit(solution)/shard_map/ppermute | solution.py:720
  26.0 11.0 %copy-start.1 = (s32[64,8]{0,1:T(8,128)S(1)}, s32[64,8]{0,1:T(8,128)}, u32[]{:S(2)}) copy-start(s32[64,8]{0,1:T(8,128)} %param.24) | copy-start | bytes 6148
  36.9 2.8 collective-permute-start.5
  170.6 42.3 %all-to-all-start.2 = ((bf16[32,24,1024]{2,1,0:T(8,128)(2,1)}), bf16[32,24,1024]{2,1,0:T(8,128)(2,1)}, u32[]{:S(2)}, u32[]{:S(2)}) async-start(bf16[32,24,1024]{2,1,0:T(8,128)(2,1)} %bitcast.57), calls=%async_computation.2 | async-start | bytes 3145728 | tf_op jit(solution)/shard_map/all_to_all | solution.py:798
  212.9 101.5 %all-to-all-start.3 = ((bf16[8,1040,256]{2,1,0:T(8,128)(2,1)}), bf16[8,1040,256]{2,1,0:T(8,128)(2,1)}, u32[]{:S(2)}, u32[]{:S(2)}) async-start(bf16[8,1040,256]{2,1,0:T(8,128)(2,1)} %expert_grads.1), calls=%async_computation.3 | async-start | bytes 8519680 | tf_op jit(solution)/shard_map/all_to_all | solution.py:773
  293.9 3.0 collective-permute-start.6
  298.7 14.7 %collective-permute-start.7 = (bf16[128,2176]{1,0:T(8,128)(2,1)S(1)}, bf16[128,2176]{1,0:T(8,128)(2,1)S(1)}, u32[]{:S(2)}, u32[]{:S(2)}) collective-permute-start(bf16[128,2176]{1,0:T(8,128)(2,1)S(1)} %fusion), channel_id=1, source_target_pairs={{0,16},{8,24},{16,0},{24,8},{1,17},{9,25},{17,1},{25,9},{2,18},{10... | collective-permute-start | bytes 1671176 | tf_op jit(solution)/shard_map/ppermute | solution.py:720
  314.4 20.6 %all-to-all-start.4 = ((bf16[8,16,2176]{2,1,0:T(8,128)(2,1)}), bf16[8,16,2176]{2,1,0:T(8,128)(2,1)S(1)}, u32[]{:S(2)}, u32[]{:S(2)}) async-start(bf16[8,16,2176]{2,1,0:T(8,128)(2,1)} %bitcast.27), calls=%async_computation.4 | async-start | bytes 1114112 | tf_op jit(solution)/shard_map/all_to_all | solution.py:773
  320.3 14.7 %copy-start = (bf16[16,2176]{1,0:T(8,128)(2,1)S(1)}, bf16[16,2176]{1,0:T(8,128)(2,1)}, u32[]{:S(2)}) copy-start(bf16[16,2176]{1,0:T(8,128)(2,1)} %pack_small.1.own_ref) | copy-start | bytes 208900

commit v2 on v1

--- a/solution.py
+++ b/solution.py
@@ -80,33 +80,40 @@
 
 
 def attention_backward_kernel(
-    qt_ref, kt_ref, k_ref, v_ref, gt_ref, ot_ref, lse_ref, out_ref, dq_t
+    q_ref, v_ref, qt_ref, kt_ref, gt_ref, ot_ref, lse_ref, out_ref, dq_t, stats
 ):
-    length = k_ref.shape[0]
+    length = q_ref.shape[0]
     q_t = qt_ref[...]
+    k_t = kt_ref[...]
     g_t = gt_ref[...]
-    k_t = kt_ref[...]
+    q = q_ref[...]
+    g = g_t.T
+    v_t = v_ref[...].T
     both = g_t.astype(f32) * ot_ref[...].astype(f32)
+    rows_of = [slice(0, HEAD_DIM), slice(HEAD_DIM, 2 * HEAD_DIM)]
+    lines = [lse_ref[0]] + [jnp.sum(both[rows], axis=0, keepdims=True) for rows in rows_of]
+    columns = jnp.concatenate(lines + [jnp.zeros((4, length), f32)], 0).T
+    for i in range(4):
+        stats[i] = jnp.broadcast_to(columns[:, i : i + 1], (length, 2 * HEAD_DIM))
     zero = jnp.zeros((HEAD_DIM, length), bf16)
-    heads = []
-    for h in range(2):
-        rows = slice(h * HEAD_DIM, (h + 1) * HEAD_DIM)
-        heads.append(
-            (
-                rows,
-                jnp.concatenate([q_t[rows], zero] if h == 0 else [zero, q_t[rows]], 0),
-                jnp.concatenate([g_t[rows], zero] if h == 0 else [zero, g_t[rows]], 0),
-                jnp.sum(both[rows], axis=0, keepdims=True),
-                lse_ref[0, h : h + 1, :],
-            )
-        )
+    k_sides = [
+        jnp.concatenate([k_t[:HEAD_DIM], zero], 0),
+        jnp.concatenate([zero, k_t[HEAD_DIM:]], 0),
+    ]
+    v_sides = [
+        jnp.concatenate([v_t[:HEAD_DIM], zero], 0),
+        jnp.concatenate([zero, v_t[HEAD_DIM:]], 0),
+    ]
+
+    def stat(i, lo):
+        half = stats[i, lo:, :]
+        return jnp.concatenate([half, half], 1)
 
     def products_of(j, h):
         here = slice(j * BLOCK, (j + 1) * BLOCK)
-        _, q_side, g_side, _, _ = heads[h]
         return (
-            product(k_ref[here, :], q_side[:, j * BLOCK :]),
-            product(v_ref[here, :], g_side[:, j * BLOCK :]),
+            product(q[j * BLOCK :], k_sides[h][:, here]),
+            product(g[j * BLOCK :], v_sides[h][:, here]),
         )
 
     items = [(j, h) for j in range(length // BLOCK) for h in range(2)]
@@ -116,15 +123,15 @@
     for i, (j, h) in enumerate(items):
         lo = j * BLOCK
         here = slice(lo, lo + BLOCK)
-        rows, _, _, delta, lse = heads[h]
+        rows = rows_of[h]
         scores, share_grad = later
         if i + 1 < len(items):
             later = products_of(*items[i + 1])
-        shares = jnp.exp2(scores * SCALE - lse[:, lo:])
-        score_grad = (shares * (share_grad - delta[:, lo:])).astype(bf16)
-        value_grads.append(against_rows(g_t[rows, lo:], shares.astype(bf16)))
-        key_grads.append(against_rows(q_t[rows, lo:], score_grad))
-        query_part = product(k_t[rows, here], score_grad)
+        shares = jnp.exp2(scores * SCALE - stat(h, lo))
+        score_grad = (shares * (share_grad - stat(2 + h, lo))).astype(bf16)
+        value_grads.append(product(g_t[rows, lo:], shares.astype(bf16)))
+        key_grads.append(product(q_t[rows, lo:], score_grad))
+        query_part = against_rows(k_t[rows, here], score_grad)
         if j == 0:
             dq_t[rows, :] = query_part
         else:
@@ -174,19 +181,21 @@
     return pl.pallas_call(
         attention_backward_kernel,
         grid=(pairs,),
-        in_specs=[pair_rows(length)] * 2
-        + [pair_columns(length, pairs), pair_columns(length, 2 * pairs)]
-        + [pair_rows(length)] * 2
+        in_specs=[pair_columns(length, 0), pair_columns(length, 2 * pairs)]
+        + [pair_rows(length)] * 4
         + [stats],
         out_specs=pl.BlockSpec((3, length, 2 * HEAD_DIM), lambda pair: (0, 0, pair)),
         out_shape=jax.ShapeDtypeStruct((3, length, D), bf16),
-        scratch_shapes=[pltpu.VMEM((2 * HEAD_DIM, length), f32)],
+        scratch_shapes=[
+            pltpu.VMEM((2 * HEAD_DIM, length), f32),
+            pltpu.VMEM((4, length, 2 * HEAD_DIM), f32),
+        ],
         compiler_params=vmem(56),
         cost_estimate=pl.CostEstimate(
             flops=50_000_000_000, bytes_accessed=16 * 2**20, transcendentals=20_000_000
         ),
         name="attention_backward",
-    )(query_t, key_t, qkv, qkv, grad_t, attended_t, lse)
+    )(qkv, qkv, query_t, key_t, grad_t, attended_t, lse)
 
 
 CHUNK = 256

time: 337 us -> 335 us (level)
  transfers between devices with their start and end apart: 12 -> 12, of which waited for: 8 -> 9; matrix products, arithmetic and copies ran while one was open for 3% -> 3% of each run, Pallas kernels for 50% -> 50%
where the time goes in v2:
time: 335 us; the launch traced here: 333 us
  Pallas kernels  180 us (54%)
  waiting for transfers between devices  71.3 us (21%)
  blocking collectives  42.6 us (13%)
  starting transfers between devices  29.5 us (9%)
  other arithmetic  4.89 us (1%)
  local copies, waits for them, and re-layouts  4.18 us (1%)
    pallas_call x1, Pallas kernels, attention_backward(): pl.pallas_call(attention_backward_kernel, grid=(pairs,), in_specs=[pair_c...  47.4 us
    all_to_all x1, blocking collectives, exchange(): lax.all_to_all(rows, BOTH, split_axis=0, concat_axis=0, tiled=True, axis_...  42.6 us
    pallas_call x1, Pallas kernels, attention_forward(): pl.pallas_call(attention_forward_kernel, grid=(pairs,), in_specs=[pair_co...  31.9 us
    all_to_all x3, waiting for transfers between devices, along_shard(): lax.all_to_all(blocks, 'shard', split_axis=0, concat_axis=0, tiled=True)  27.9 us
    all_to_all x1, waiting for transfers between devices, exchange(): lax.all_to_all(rows, BOTH, split_axis=0, concat_axis=0, tiled=True, axis_...  24.9 us
    ppermute x8, waiting for transfers between devices, swap(): return lax.ppermute(block, axis, [(i, i ^ bits) for i in range(size)])  18.5 us
    pallas_call x1, Pallas kernels, combine(): call(combine_kernel, steps, [leading(COMBINE, D), leading(COMBINE, D), le...  17.4 us
    all_to_all x3, starting transfers between devices, along_shard(): lax.all_to_all(blocks, 'shard', split_axis=0, concat_axis=0, tiled=True)  16.1 us
  transfers between devices with their start and end apart: 12, of which 9 were waited for; matrix products, arithmetic and copies ran while one was open for 3% of the time, Pallas kernels for 50%

profile of v2, /device:TPU:0, one launch (start us, length us, event | category | flops | bytes accessed | tf_op | source)
XLA Modules:
  0.0 333.1 jit_solution(5465660806552903992)
XLA Ops:
  0.6 1.5 pack_small.1.own_ref
  2.2 3.0 collective-permute-start
  5.2 0.9 bitcast_dynamic-update-slice_fusion.5
  6.1 1.6 collective-permute-done
  7.7 2.1 collective-permute-start.1
  9.8 2.6 collective-permute-start.2
  12.4 0.0 collective-permute-start.3
  12.4 5.8 %pack_weights.1 = bf16[8,1040,256]{2,1,0:T(8,128)(2,1)} custom-call(f32[8,512,256]{2,1,0:T(8,128)} %first_ref, f32[8,256]{1,0:T(8,128)} %bias_ref.1, f32[8,256,512]{2,1,0:T(8,128)} %second_ref), custom_call_target="tpu_custom_call" | custom-call | flops 1000000 | bytes 12582912 | tf_op jit(solution)/shard_map/pack_weights/pallas_call | solution.py:302
  18.2 6.1 %all-to-all-start = ((bf16[8,1040,256]{2,1,0:T(8,128)(2,1)}), bf16[8,1040,256]{2,1,0:T(8,128)(2,1)}, u32[]{:S(2)}, u32[]{:S(2)}) async-start(bf16[8,1040,256]{2,1,0:T(8,128)(2,1)} %pack_weights.1), calls=%async_computation | async-start | bytes 8519680 | tf_op jit(solution)/shard_map/all_to_all | solution.py:782
  24.3 0.0 collective-permute-done.1
  24.4 0.0 collective-permute-done.2
  24.4 0.0 collective-permute-done.3
  24.4 1.6 collective-permute-start.4
  26.0 0.0 copy-start.1
  26.0 10.6 %collective-permute-done.4 = bf16[128,2176]{1,0:T(8,128)(2,1)S(1)} collective-permute-done((bf16[128,2176]{1,0:T(8,128)(2,1)S(1)}, bf16[128,2176]{1,0:T(8,128)(2,1)S(1)}, u32[]{:S(2)}, u32[]{:S(2)}) %collective-permute-start.4) | collective-permute-done | bytes 557088 | tf_op jit(solution)/shard_map/ppermute | solution.py:729
  36.6 0.1 select_bitcast_fusion.3
  36.7 0.1 pad_maximum_fusion.1
  36.9 0.1 collective-permute-start.5
  36.9 0.0 copy-done.1
  37.0 0.1 copy.43
  37.1 0.2 fusion.1
  37.3 0.1 copy.44
  37.4 0.7 reshape_reshape.6.slots_ref
  38.1 0.7 reshape.69
  38.8 0.9 collective-permute-done.5
  39.7 0.2 select_bitcast_fusion.1
  39.9 1.6 pad_maximum_fusion
  41.5 10.0 %project.1 = (bf16[2048,1536]{1,0:T(8,128)(2,1)}, bf16[512,2048]{1,0:T(8,128)(2,1)}) custom-call(bf16[2048,512]{1,0:T(8,128)(2,1)} %tokens_ref.5, bf16[512,2176]{1,0:T(8,128)(2,1)} %bitcast.46, bf16[512,2176]{1,0:T(8,128)(2,1)} %bitcast.47), custom_call_target="tpu_custom_call" | custom-call | flops 3221225472 | bytes 12582912 | tf_op jit(solution)/shard_map/project/pallas_call | solution.py:465
  51.5 31.9 %attention_forward.1 = (bf16[2048,512]{1,0:T(8,128)(2,1)}, f32[4,2,2048]{2,1,0:T(2,128)}, bf16[512,2048]{1,0:T(8,128)(2,1)}, bf16[512,2048]{1,0:T(8,128)(2,1)}, bf16[512,2048]{1,0:T(8,128)(2,1)}) custom-call(bf16[2048,1536]{1,0:T(8,128)(2,1)} %get-tuple-element.49.q_ref.k_ref.v_ref, bf16[2048,1536]{1,0:T(8,128)(2,1)} %get-tuple-element.49.q_ref.k_ref.v_ref, ...), custom_call_target="tpu_custom_call" | custom-call | flops 10000000000 | bytes 8388608 | tf_op jit(solution)/shard_map/attention_forward/pallas_call | solution.py:159
  83.5 13.5 %mix.1 = (f32[2048,512]{1,0:T(8,128)}, f32[2048,128]{1,0:T(8,128)}, bf16[768,1024]{1,0:T(8,128)(2,1)}) custom-call(bf16[2048,512]{1,0:T(8,128)(2,1)} %get-tuple-element.50.attended_ref, bf16[2048,512]{1,0:T(8,128)(2,1)} %tokens_ref.5, bf16[2048,512]{1,0:T(8,128)(2,1)} %grad_ref.3, bf16[512,2176]{1,0:T(8,128)(2,1)} %bitcast.48, bf16[512,2176]{1,0:T(8,128)(2,1)} %bitcast.49, ...), custom_call_target="tpu_custom_call" | custom-call | flops 2147483648 | bytes 14680064 | tf_op jit(solution)/shard_map/mix/pallas_call | solution.py:520
  97.0 20.0 %all-to-all-done.w_ref = bf16[8,1040,256]{2,1,0:T(8,128)(2,1)} async-done(((bf16[8,1040,256]{2,1,0:T(8,128)(2,1)}), bf16[8,1040,256]{2,1,0:T(8,128)(2,1)}, u32[]{:S(2)}, u32[]{:S(2)}) %all-to-all-start) | async-done | bytes 4259872 | tf_op jit(solution)/shard_map/all_to_all | solution.py:782
  116.9 42.6 %all_to_all.38 = bf16[32,24,1024]{2,1,0:T(8,128)(2,1)} all-to-all(bf16[32,24,1024]{2,1,0:T(8,128)(2,1)} %bitcast.58), channel_id=1, replica_groups=mesh['expert'=4,'shard'=8] {'expert','shard'}, dimensions={0} | all-to-all | bytes 3145728 | tf_op jit(solution)/shard_map/all_to_all | solution.py:807
  159.5 11.1 %expert_rows.1 = bf16[768,1024]{1,0:T(8,128)(2,1)} custom-call(bf16[768,1024]{1,0:T(8,128)(2,1)} %bitcast.55, bf16[8,1040,256]{2,1,0:T(8,128)(2,1)} %all-to-all-done.w_ref), custom_call_target="tpu_custom_call" | custom-call | flops 6442450944 | bytes 8388608 | tf_op jit(solution)/shard_map/expert_rows/pallas_call | solution.py:406
  170.6 3.4 %all-to-all-start.2 = ((bf16[32,24,1024]{2,1,0:T(8,128)(2,1)}), bf16[32,24,1024]{2,1,0:T(8,128)(2,1)}, u32[]{:S(2)}, u32[]{:S(2)}) async-start(bf16[32,24,1024]{2,1,0:T(8,128)(2,1)} %bitcast.57), calls=%async_computation.2 | async-start | bytes 3145728 | tf_op jit(solution)/shard_map/all_to_all | solution.py:807
  174.0 0.8 reshape_reshape.8.slots_ref
  174.9 0.7 reshape.70
  175.6 12.4 %expert_grads.1 = bf16[8,1040,256]{2,1,0:T(8,128)(2,1)} custom-call(bf16[768,1024]{1,0:T(8,128)(2,1)} %bitcast.56, bf16[8,1040,256]{2,1,0:T(8,128)(2,1)} %all-to-all-done.w_ref), custom_call_target="tpu_custom_call" | custom-call | flops 6442450944 | bytes 14680064 | tf_op jit(solution)/shard_map/expert_grads/pallas_call | solution.py:442
  188.0 24.9 %all-to-all-done.2 = bf16[32,24,1024]{2,1,0:T(8,128)(2,1)} async-done(((bf16[32,24,1024]{2,1,0:T(8,128)(2,1)}), bf16[32,24,1024]{2,1,0:T(8,128)(2,1)}, u32[]{:S(2)}, u32[]{:S(2)}) %all-to-all-start.2) | async-done | bytes 1572896 | tf_op jit(solution)/shard_map/all_to_all | solution.py:807
  212.9 4.6 %all-to-all-start.3 = ((bf16[8,1040,256]{2,1,0:T(8,128)(2,1)}), bf16[8,1040,256]{2,1,0:T(8,128)(2,1)}, u32[]{:S(2)}, u32[]{:S(2)}) async-start(bf16[8,1040,256]{2,1,0:T(8,128)(2,1)} %expert_grads.1), calls=%async_computation.3 | async-start | bytes 8519680 | tf_op jit(solution)/shard_map/all_to_all | solution.py:782
  217.5 17.4 %combine.1 = (bf16[2048,512]{1,0:T(8,128)(2,1)}, f32[2048,512]{1,0:T(8,128)}, bf16[512,2048]{1,0:T(8,128)(2,1)}, f32[512,640]{1,0:T(8,128)}) custom-call(f32[2048,512]{1,0:T(8,128)} %get-tuple-element.51.residual_ref, bf16[2048,512]{1,0:T(8,128)(2,1)} %grad_ref.3, f32[2048,128]{1,0:T(8,128)} %get-tuple-element.52.probs_ref, ...), custom_call_target="tpu_custom_call" | custom-call | flops 3221225472 | bytes 25165824 | tf_op jit(solution)/shard_map/combine/pallas_call | solution.py:599
  234.9 47.4 %attention_backward.1.grad_ref.grads_ref = bf16[3,2048,512]{2,1,0:T(8,128)(2,1)} custom-call(bf16[2048,1536]{1,0:T(8,128)(2,1)} %get-tuple-element.49.q_ref.k_ref.v_ref, bf16[2048,1536]{1,0:T(8,128)(2,1)} %get-tuple-element.49.q_ref.k_ref.v_ref, bf16[512,2048]{1,0:T(8,128)(2,1)} %get-tuple-element.61.qt_ref, bf16[512,2048]{1,0:T(8,128)(2,1)} %get-tuple-element.62.kt_ref, ...), custom_call_target="tpu_custom_call" | custom-call | flops 49999998976 | bytes 16777216 | tf_op jit(solution)/shard_map/attention_backward/pallas_call | solution.py:181
  282.3 9.0 %weight_grads.1 = (bf16[2,128,2176]{2,1,0:T(8,128)(2,1)}, f32[2,128,2176]{2,1,0:T(8,128)}) custom-call(s32[1]{0:T(128)} %bitcast.23.core_ref, bf16[512,2048]{1,0:T(8,128)(2,1)} %get-tuple-element.60.normed_t_ref, bf16[3,2048,512]{2,1,0:T(8,128)(2,1)} %attention_backward.1.grad_ref.grads_ref, f32[512,640]{1,0:T(8,128)} %get-tuple-element.66.sums_ref), custom_call_target="tpu_custom_call" | custom-call | flops 3221225472 | bytes 12582912 | tf_op jit(solution)/shard_map/weight_grads/pallas_call | solution.py:649
  291.2 0.0 collective-permute-start.6
  291.2 3.0 collective-permute-done.6
  294.2 1.8 convert_add_fusion
  296.0 0.1 fusion
  296.1 0.6 collective-permute-start.7
  296.7 11.7 %input_grads.1 = bf16[2048,512]{1,0:T(8,128)(2,1)} custom-call(bf16[3,2048,512]{2,1,0:T(8,128)(2,1)} %attention_backward.1.grad_ref.grads_ref, bf16[512,2176]{1,0:T(8,128)(2,1)} %bitcast.52, bf16[512,2176]{1,0:T(8,128)(2,1)} %bitcast.53, bf16[2048,512]{1,0:T(8,128)(2,1)} %tokens_ref.5, f32[2048,512]{1,0:T(8,128)} %get-tuple-element.69.residual_grad_ref), custom_call_target="tpu_custom_call" | custom-call | flops 3221225472 | bytes 18874368 | tf_op jit(solution)/shard_map/input_grads/pallas_call | solution.py:676
  308.4 2.5 collective-permute-done.7
  310.8 0.9 bitcast_add_fusion
  311.8 0.4 all-to-all-done.3.in_ref
  312.2 5.5 %all-to-all-start.4 = ((bf16[8,16,2176]{2,1,0:T(8,128)(2,1)}), bf16[8,16,2176]{2,1,0:T(8,128)(2,1)S(1)}, u32[]{:S(2)}, u32[]{:S(2)}) async-start(bf16[8,16,2176]{2,1,0:T(8,128)(2,1)} %bitcast.27), calls=%async_computation.4 | async-start | bytes 1114112 | tf_op jit(solution)/shard_map/all_to_all | solution.py:782
  317.6 0.0 copy-start
  317.6 7.2 %unpack_grads.1 = (f32[8,512,256]{2,1,0:T(8,128)}, f32[8,256]{1,0:T(8,128)}, f32[8,256,512]{2,1,0:T(8,128)}) custom-call(bf16[8,1040,256]{2,1,0:T(8,128)(2,1)} %all-to-all-done.3.in_ref), custom_call_target="tpu_custom_call" | custom-call | flops 1000000 | bytes 12582912 | tf_op jit(solution)/shard_map/unpack_grads/pallas_call | solution.py:328
  324.9 7.5 %all-to-all-done.4.pieces_ref = bf16[8,16,2176]{2,1,0:T(8,128)(2,1)S(1)} async-done(((bf16[8,16,2176]{2,1,0:T(8,128)(2,1)}), bf16[8,16,2176]{2,1,0:T(8,128)(2,1)S(1)}, u32[]{:S(2)}, u32[]{:S(2)}) %all-to-all-start.4) | async-done | bytes 557088 | tf_op jit(solution)/shard_map/all_to_all | solution.py:782
  332.4 0.0 copy-done
  332.4 0.7 finish.1
  (11 shorter events, 0.2 us)
Async XLA Ops:
  2.2 5.5 %collective-permute-start = (bf16[16,2176]{1,0:T(8,128)(2,1)}, bf16[16,2176]{1,0:T(8,128)(2,1)S(1)}, u32[]{:S(2)}, u32[]{:S(2)}) collective-permute-start(bf16[16,2176]{1,0:T(8,128)(2,1)} %pack_small.1.own_ref), channel_id=1, source_target_pairs={{0,1},{1,0},{2,3},{3,2},{4,5},{5,4},{6,7},{7,6},{8,9},{9,8},{10,11... | collective-permute-start | bytes 208904 | tf_op jit(solution)/shard_map/ppermute | solution.py:729
  7.7 16.7 %collective-permute-start.1 = (bf16[32,2176]{1,0:T(8,128)(2,1)S(1)}, bf16[32,2176]{1,0:T(8,128)(2,1)S(1)}, u32[]{:S(2)}, u32[]{:S(2)}) collective-permute-start(bf16[32,2176]{1,0:T(8,128)(2,1)S(1)} %bitcast.59), channel_id=1, source_target_pairs={{0,2},{1,3},{2,0},{3,1},{4,6},{5,7},{6,4},{7,5},{8,10},{9,11},{10,... | collective-permute-start | bytes 417800 | tf_op jit(solution)/shard_map/ppermute | solution.py:729
  9.8 14.6 %collective-permute-start.2 = (bf16[32,2176]{1,0:T(8,128)(2,1)S(1)}, bf16[32,2176]{1,0:T(8,128)(2,1)S(1)}, u32[]{:S(2)}, u32[]{:S(2)}) collective-permute-start(bf16[32,2176]{1,0:T(8,128)(2,1)S(1)} %bitcast.60), channel_id=1, source_target_pairs={{0,4},{1,5},{2,6},{3,7},{4,0},{5,1},{6,2},{7,3},{8,12},{9,13},{10,... | collective-permute-start | bytes 417800 | tf_op jit(solution)/shard_map/ppermute | solution.py:729
  12.4 12.0 %collective-permute-start.3 = (bf16[32,2176]{1,0:T(8,128)(2,1)S(1)}, bf16[32,2176]{1,0:T(8,128)(2,1)S(1)}, u32[]{:S(2)}, u32[]{:S(2)}) collective-permute-start(bf16[32,2176]{1,0:T(8,128)(2,1)S(1)} %bitcast.61), channel_id=1, source_target_pairs={{0,6},{1,7},{2,4},{3,5},{4,2},{5,3},{6,0},{7,1},{8,14},{9,15},{10,... | collective-permute-start | bytes 417800 | tf_op jit(solution)/shard_map/ppermute | solution.py:729
  18.2 98.8 %all-to-all-start = ((bf16[8,1040,256]{2,1,0:T(8,128)(2,1)}), bf16[8,1040,256]{2,1,0:T(8,128)(2,1)}, u32[]{:S(2)}, u32[]{:S(2)}) async-start(bf16[8,1040,256]{2,1,0:T(8,128)(2,1)} %pack_weights.1), calls=%async_computation | async-start | bytes 8519680 | tf_op jit(solution)/shard_map/all_to_all | solution.py:782
  24.4 12.2 %collective-permute-start.4 = (bf16[128,2176]{1,0:T(8,128)(2,1)S(1)}, bf16[128,2176]{1,0:T(8,128)(2,1)S(1)}, u32[]{:S(2)}, u32[]{:S(2)}) collective-permute-start(bf16[128,2176]{1,0:T(8,128)(2,1)S(1)} %bitcast.54), channel_id=1, source_target_pairs={{0,16},{8,24},{16,0},{24,8},{1,17},{9,25},{17,1},{25,9},{2,18},{10... | collective-permute-start | bytes 1671176 | tf_op jit(solution)/shard_map/ppermute | solution.py:729
  26.0 11.0 %copy-start.1 = (s32[64,8]{0,1:T(8,128)S(1)}, s32[64,8]{0,1:T(8,128)}, u32[]{:S(2)}) copy-start(s32[64,8]{0,1:T(8,128)} %param.24) | copy-start | bytes 6148
  36.9 2.8 collective-permute-start.5
  170.6 42.3 %all-to-all-start.2 = ((bf16[32,24,1024]{2,1,0:T(8,128)(2,1)}), bf16[32,24,1024]{2,1,0:T(8,128)(2,1)}, u32[]{:S(2)}, u32[]{:S(2)}) async-start(bf16[32,24,1024]{2,1,0:T(8,128)(2,1)} %bitcast.57), calls=%async_computation.2 | async-start | bytes 3145728 | tf_op jit(solution)/shard_map/all_to_all | solution.py:807
  212.9 99.3 %all-to-all-start.3 = ((bf16[8,1040,256]{2,1,0:T(8,128)(2,1)}), bf16[8,1040,256]{2,1,0:T(8,128)(2,1)}, u32[]{:S(2)}, u32[]{:S(2)}) async-start(bf16[8,1040,256]{2,1,0:T(8,128)(2,1)} %expert_grads.1), calls=%async_computation.3 | async-start | bytes 8519680 | tf_op jit(solution)/shard_map/all_to_all | solution.py:782
  291.2 3.0 collective-permute-start.6
  296.1 14.7 %collective-permute-start.7 = (bf16[128,2176]{1,0:T(8,128)(2,1)S(1)}, bf16[128,2176]{1,0:T(8,128)(2,1)S(1)}, u32[]{:S(2)}, u32[]{:S(2)}) collective-permute-start(bf16[128,2176]{1,0:T(8,128)(2,1)S(1)} %fusion), channel_id=1, source_target_pairs={{0,16},{8,24},{16,0},{24,8},{1,17},{9,25},{17,1},{25,9},{2,18},{10... | collective-permute-start | bytes 1671176 | tf_op jit(solution)/shard_map/ppermute | solution.py:729
  312.2 20.2 %all-to-all-start.4 = ((bf16[8,16,2176]{2,1,0:T(8,128)(2,1)}), bf16[8,16,2176]{2,1,0:T(8,128)(2,1)S(1)}, u32[]{:S(2)}, u32[]{:S(2)}) async-start(bf16[8,16,2176]{2,1,0:T(8,128)(2,1)} %bitcast.27), calls=%async_computation.4 | async-start | bytes 1114112 | tf_op jit(solution)/shard_map/all_to_all | solution.py:782
  317.6 14.7 %copy-start = (bf16[16,2176]{1,0:T(8,128)(2,1)S(1)}, bf16[16,2176]{1,0:T(8,128)(2,1)}, u32[]{:S(2)}) copy-start(bf16[16,2176]{1,0:T(8,128)(2,1)} %pack_small.1.own_ref) | copy-start | bytes 208900

commit v3 on v2

--- a/solution.py
+++ b/solution.py
@@ -201,7 +201,7 @@
 CHUNK = 256
 COMBINE = 512
 LANES = 128
-BIAS_ROWS = 16
+BIAS_LANE = 64
 SHARDS_A_STEP = 4
 GAIN_ONE = LANES - 2
 GAIN_TWO = LANES - 1
@@ -247,7 +247,7 @@
     return inverse * (adjusted - first_mean - scaled * second_mean)
 
 
-def small_kernel(q_ref, k_ref, v_ref, o_ref, ctrl_ref, one_ref, two_ref, out_ref):
+def small_kernel(q_ref, k_ref, v_ref, o_ref, ctrl_ref, one_ref, two_ref, bias_ref, out_ref):
     rows, experts = ctrl_ref.shape
     for i, ref in enumerate((q_ref, k_ref, v_ref, o_ref)):
         out_ref[:, i * D : (i + 1) * D] = ref[...].astype(bf16)
@@ -257,24 +257,27 @@
     two = jnp.sum(jnp.where(own, two_ref[...], 0.0), axis=1, keepdims=True)
     lane = lax.broadcasted_iota(jnp.int32, (rows, LANES), 1)
     gains = jnp.where(lane == GAIN_ONE, one, jnp.where(lane == GAIN_TWO, two, 0.0))
-    out_ref[:, 4 * D :] = gains.astype(bf16)
+    out_ref[:, 4 * D : 4 * D + LANES] = gains.astype(bf16)
     out_ref[:, 4 * D : 4 * D + experts] = ctrl_ref[...].astype(bf16)
-
-
-def pack_small(weights, ctrl, gain_one, gain_two):
+    parts = [bias_ref[:, c : c + LANES] for c in range(0, bias_ref.shape[1], LANES)]
+    out_ref[:, 4 * D + LANES :] = jnp.concatenate(parts, 0).astype(bf16)
+
+
+def pack_small(weights, ctrl, gain_one, gain_two, bias):
     rows, experts = ctrl.shape
-    width = 4 * D + LANES
+    width = 4 * D + 2 * LANES
     return call(
         small_kernel,
         1,
-        [fixed(rows, D)] * 4 + [fixed(rows, experts), fixed(1, rows), fixed(1, rows)],
+        [fixed(rows, D)] * 4
+        + [fixed(rows, experts), fixed(1, rows), fixed(1, rows), fixed(*bias.shape)],
         fixed(rows, width),
         jax.ShapeDtypeStruct((rows, width), bf16),
         [],
         100_000,
         200_000,
         "pack_small",
-    )(*weights, ctrl, gain_one.reshape(1, rows), gain_two.reshape(1, rows))
+    )(*weights, ctrl, gain_one.reshape(1, rows), gain_two.reshape(1, rows), bias)
 
 
 def gain_of(ctrl_block, lane):
@@ -282,42 +285,37 @@
     return against_rows(pick, ctrl_block)[:1]
 
 
-def pack_kernel(first_ref, bias_ref, second_ref, out_ref):
+def pack_kernel(first_ref, second_ref, out_ref):
     held, _, hidden = first_ref.shape
     for i in range(held):
         out_ref[i, :D, :] = first_ref[i].astype(bf16)
-        out_ref[i, D : D + BIAS_ROWS, :] = jnp.broadcast_to(
-            bias_ref[pl.ds(pl.program_id(0) * held + i, 1), :], (BIAS_ROWS, hidden)
-        ).astype(bf16)
         for c in range(D // hidden):
-            start = D + BIAS_ROWS + c * hidden
+            start = D + c * hidden
             out_ref[i, start : start + hidden, :] = second_ref[
                 i, :, c * hidden : (c + 1) * hidden
             ].astype(bf16)
 
 
-def pack_weights(w_in, b_in, w_exp_out):
+def pack_weights(w_in, w_exp_out):
     local, _, hidden = w_in.shape
-    total = 2 * D + BIAS_ROWS
     return call(
         pack_kernel,
         local // 2,
-        [leading(2, D, hidden), fixed(local, hidden), leading(2, hidden, D)],
-        leading(2, total, hidden),
-        jax.ShapeDtypeStruct((local, total, hidden), bf16),
+        [leading(2, D, hidden), leading(2, hidden, D)],
+        leading(2, 2 * D, hidden),
+        jax.ShapeDtypeStruct((local, 2 * D, hidden), bf16),
         [],
         1_000_000,
         12 * 2**20,
         "pack_weights",
-    )(w_in, b_in, w_exp_out)
-
-
-def unpack_kernel(in_ref, first_ref, bias_ref, second_ref):
+    )(w_in, w_exp_out)
+
+
+def unpack_kernel(in_ref, first_ref, second_ref):
     hidden = first_ref.shape[2]
     first_ref[0] = in_ref[0, :D, :].astype(f32)
-    bias_ref[pl.ds(pl.program_id(0), 1), :] = in_ref[0, D : D + BIAS_ROWS, :].astype(f32)[:1]
     for c in range(D // hidden):
-        start = D + BIAS_ROWS + c * hidden
+        start = D + c * hidden
         second_ref[0, :, c * hidden : (c + 1) * hidden] = in_ref[
             0, start : start + hidden, :
         ].astype(f32)
@@ -329,10 +327,9 @@
         unpack_kernel,
         local,
         [leading(1, total, hidden)],
-        [leading(1, D, hidden), fixed(local, hidden), leading(1, hidden, D)],
+        [leading(1, D, hidden), leading(1, hidden, D)],
         [
             jax.ShapeDtypeStruct((local, D, hidden), f32),
-            jax.ShapeDtypeStruct((local, hidden), f32),
             jax.ShapeDtypeStruct((local, hidden, D), f32),
         ],
         [],
@@ -342,13 +339,12 @@
     )(packed)
 
 
-def expert_products(rows_ref, w_ref, i):
+def expert_products(rows_ref, w_ref, bias_ref, i, shard):
     hidden = w_ref.shape[2]
-    bias = w_ref[i, D : D + BIAS_ROWS, :].astype(f32)[:1]
-    pre_act = product(rows_ref[:, :D], w_ref[i, :D, :]) + bias
+    pre_act = product(rows_ref[:, :D], w_ref[i, :D, :]) + bias_ref[pl.ds(shard, 1), :]
     hidden_grad = jnp.zeros_like(pre_act)
     for c in range(D // hidden):
-        start = D + BIAS_ROWS + c * hidden
+        start = D + c * hidden
         cols = slice(D + c * hidden, D + (c + 1) * hidden)
         hidden_grad = hidden_grad + against_rows(
             rows_ref[:, cols], w_ref[i, start : start + hidden, :]
@@ -363,20 +359,20 @@
     return (pre_act * sigma).astype(bf16), pre_grad
 
 
-def expert_kernel(rows_ref, w_ref, out_ref, results, mixed_grad):
+def expert_kernel(rows_ref, w_ref, bias_ref, out_ref, results, mixed_grad):
     step = pl.program_id(0)
     held, _, hidden = w_ref.shape
     chunks = D // hidden
     parts = [None] * (chunks + 1)
-    later = expert_products(rows_ref, w_ref, 0)
+    later = expert_products(rows_ref, w_ref, bias_ref, 0, step * held)
     for i in range(held):
         now = later
         if i + 1 < held:
-            later = expert_products(rows_ref, w_ref, i + 1)
+            later = expert_products(rows_ref, w_ref, bias_ref, i + 1, step * held + i + 1)
         active, pre_grad = activate(*now)
         more = []
         for c in range(chunks):
-            start = D + BIAS_ROWS + c * hidden
+            start = D + c * hidden
             more.append(product(active, w_ref[i, start : start + hidden, :]))
         more.append(against_rows(pre_grad, w_ref[i, :D, :]))
         parts = more if i == 0 else [old + new for old, new in zip(parts, more)]
@@ -400,57 +396,75 @@
         out_ref[:, D:] = mixed_grad[...].astype(bf16)
 
 
-def expert_rows(rows, weights):
+def expert_rows(rows, weights, bias):
     count = rows.shape[0]
     shards, total, hidden = weights.shape
     return call(
         expert_kernel,
         shards // SHARDS_A_STEP,
-        [fixed(count, 2 * D), leading(SHARDS_A_STEP, total, hidden)],
+        [fixed(count, 2 * D), leading(SHARDS_A_STEP, total, hidden), fixed(shards, hidden)],
         fixed(count, 2 * D),
         jax.ShapeDtypeStruct((count, 2 * D), bf16),
         [pltpu.VMEM((count, D), f32), pltpu.VMEM((count, D), f32)],
         8 * count * D * shards * hidden,
         8 * 2**20,
         "expert_rows",
-    )(rows, weights)
-
-
-def expert_grad_kernel(rows_ref, w_ref, out_ref, rows_t):
+        40,
+    )(rows, weights, bias)
+
+
+def bias_places(rows, hidden):
+    each = hidden // rows
+    shape = (rows, hidden)
+    owner = lax.broadcasted_iota(jnp.int32, shape, 1) // each == lax.broadcasted_iota(
+        jnp.int32, shape, 0
+    )
+    shape = (LANES, hidden)
+    lane = lax.broadcasted_iota(jnp.int32, shape, 1) % each + BIAS_LANE
+    return owner, (lane == lax.broadcasted_iota(jnp.int32, shape, 0)).astype(bf16)
+
+
+def expert_grad_kernel(rows_ref, w_ref, bias_ref, out_ref, sums_ref, rows_t):
     hidden = out_ref.shape[2]
 
     @pl.when(pl.program_id(0) == 0)
     def _():
         rows_t[...] = rows_ref[:, :D].T
 
-    active, pre_grad = activate(*expert_products(rows_ref, w_ref, 0))
+    shard = pl.program_id(0)
+    active, pre_grad = activate(*expert_products(rows_ref, w_ref, bias_ref, 0, shard))
     out_ref[0, :D, :] = product(rows_t[...], pre_grad).astype(bf16)
-    out_ref[0, D : D + BIAS_ROWS, :] = jnp.broadcast_to(
-        jnp.sum(pre_grad.astype(f32), axis=0, keepdims=True), (BIAS_ROWS, hidden)
-    ).astype(bf16)
+    bias_grad = jnp.sum(pre_grad.astype(f32), axis=0, keepdims=True)
+    rows = sums_ref.shape[1]
+    owner, lanes = bias_places(rows, hidden)
+    parts = jnp.where(owner, bias_grad, 0.0).astype(bf16)
+    sums_ref[0] = against_rows(parts, lanes).astype(bf16)
     active_t = active.T
     for c in range(D // hidden):
-        start = D + BIAS_ROWS + c * hidden
+        start = D + c * hidden
         out_ref[0, start : start + hidden, :] = product(
             active_t, rows_ref[:, D + c * hidden : D + (c + 1) * hidden]
         ).astype(bf16)
 
 
-def expert_grads(rows, weights):
+def expert_grads(rows, weights, bias, block):
     count = rows.shape[0]
     shards, total, hidden = weights.shape
     return call(
         expert_grad_kernel,
         shards,
-        [fixed(count, 2 * D), leading(1, total, hidden)],
-        leading(1, total, hidden),
-        jax.ShapeDtypeStruct((shards, total, hidden), bf16),
+        [fixed(count, 2 * D), leading(1, total, hidden), fixed(shards, hidden)],
+        [leading(1, total, hidden), leading(1, block, LANES)],
+        [
+            jax.ShapeDtypeStruct((shards, total, hidden), bf16),
+            jax.ShapeDtypeStruct((shards, block, LANES), bf16),
+        ],
         [pltpu.VMEM((D, count), bf16)],
         8 * count * D * shards * hidden,
         14 * 2**20,
         "expert_grads",
         63,
-    )(rows, weights)
+    )(rows, weights, bias)
 
 
 def project_kernel(tokens_ref, w_ref, ctrl_ref, qkv_ref, normed_t_ref):
@@ -657,6 +671,7 @@
         6 * length * D * D,
         12 * 2**20,
         "weight_grads",
+        24,
     )(core, normed_t, grads, sums)
 
 
@@ -688,7 +703,9 @@
     )(grads, small, small, tokens, residual_grad)
 
 
-def finish_kernel(pieces_ref, own_ref, q_ref, k_ref, v_ref, o_ref, ctrl_ref, one_ref, two_ref):
+def finish_kernel(
+    pieces_ref, own_ref, q_ref, k_ref, v_ref, o_ref, ctrl_ref, one_ref, two_ref, bias_ref
+):
     rows, experts = ctrl_ref.shape
     total = jnp.sum(pieces_ref[...].astype(f32), axis=0)
     own = own_ref[...].astype(f32)
@@ -698,22 +715,30 @@
     lane = lax.broadcasted_iota(jnp.int32, (rows, LANES), 1)
 
     def column(block, which):
-        return jnp.sum(jnp.where(lane == which, block[:, 4 * D :], 0.0), axis=1, keepdims=True)
+        return jnp.sum(jnp.where(lane == which, block[:, 4 * D : 4 * D + LANES], 0.0), axis=1, keepdims=True)
 
     one = jnp.sum(total[:, : 3 * D] * own[:, : 3 * D], axis=1, keepdims=True) / column(own, GAIN_ONE)
     square = (rows, rows)
     same = lax.broadcasted_iota(jnp.int32, square, 0) == lax.broadcasted_iota(jnp.int32, square, 1)
     one_ref[...] = jnp.sum(jnp.where(same, one, 0.0), axis=0, keepdims=True)
     two_ref[...] = jnp.sum(jnp.where(same, column(total, GAIN_TWO), 0.0), axis=0, keepdims=True)
-
-
-def finish(pieces, own, experts):
+    local, hidden = bias_ref.shape
+    owner, lanes = bias_places(rows, hidden)
+    copies = pieces_ref.shape[0] // local
+    for e in range(local):
+        for i in range(copies):
+            part = product(pieces_ref[e * copies + i, :, 4 * D :], lanes)
+            line = jnp.sum(jnp.where(owner, part, 0.0), axis=0, keepdims=True)
+            bias_ref[e : e + 1, :] = line if i == 0 else bias_ref[e : e + 1, :] + line
+
+
+def finish(pieces, own, experts, bias_shape):
     count, rows, width = pieces.shape
-    outs = [(rows, D)] * 4 + [(rows, experts), (1, rows), (1, rows)]
+    outs = [(rows, D)] * 4 + [(rows, experts), (1, rows), (1, rows), bias_shape]
     return call(
         finish_kernel,
         1,
-        [fixed(count, rows, width), fixed(rows, width)],
+        [fixed(count, rows, width), fixed(*own.shape)],
         [fixed(*shape) for shape in outs],
         [jax.ShapeDtypeStruct(shape, f32) for shape in outs],
         [],
@@ -839,15 +864,24 @@
     slots = slots_of(routes, experts)
 
     own = pack_small(
-        (w_query, w_key, w_value, w_attn_out), w_ctrl, ln1_gain, ln2_gain
+        (w_query, w_key, w_value, w_attn_out), w_ctrl, ln1_gain, ln2_gain, b_in
     )
     outer, inner = halves(n_shard)
     here = lax.axis_index("shard")
     held = spread(own, inner, 1, here & (inner - 1))
     held, w_in, w_exp_out = lax.optimization_barrier((held, w_in, w_exp_out))
-    expert_w = to_experts(pack_weights(w_in, b_in, w_exp_out), copies)
+    expert_w = to_experts(pack_weights(w_in, w_exp_out), copies)
     held = spread(held, outer, inner, here >> (inner.bit_length() - 1))
     small = gather_expert(held)
+    local, hidden = b_in.shape
+    biases = held.reshape(n_shard, -1, held.shape[1])[:, :, 4 * D + LANES :]
+    bias = jnp.concatenate(
+        [
+            lax.dynamic_index_in_dim(biases, c * local + here // copies, 1, keepdims=False)
+            for c in range(hidden // LANES)
+        ],
+        axis=1,
+    ).astype(f32)
 
     qkv, normed_t = project(tokens, small)
     attended, lse, query_t, key_t, attended_t = attention_forward(qkv)
@@ -856,9 +890,9 @@
     )
     outgoing, expert_w = lax.optimization_barrier((outgoing, expert_w))
     arrived = exchange(outgoing, copies)
-    results = expert_rows(arrived, expert_w)
+    results = expert_rows(arrived, expert_w, bias)
     returned = exchange(results, copies)
-    expert_sums = expert_grads(arrived, expert_w)
+    expert_sums, bias_sums = expert_grads(arrived, expert_w, bias, own.shape[0])
     returned, expert_sums = lax.optimization_barrier((returned, expert_sums))
     expert_sums = from_experts(expert_sums, copies)
     output, residual_grad, grad_t, sums = combine(
@@ -870,9 +904,13 @@
     late = sum_expert(away, kept)
     input_grad = input_grads(grads, small, tokens, residual_grad)
     late, input_grad, expert_sums = lax.optimization_barrier((late, input_grad, expert_sums))
-    pieces = along_shard(late.astype(bf16).reshape((n_shard,) + own.shape))
-    w_in_grad, b_in_grad, w_exp_out_grad = unpack_grads(expert_sums)
-    wq_grad, wk_grad, wv_grad, wo_grad, wc_grad, ln1_grad, ln2_grad = finish(pieces, own, experts)
+    late = late.reshape(n_shard, own.shape[0], -1)
+    late = late + jnp.pad(bias_sums.astype(f32), ((0, 0), (0, 0), (4 * D, 0)))
+    pieces = along_shard(late.astype(bf16))
+    w_in_grad, w_exp_out_grad = unpack_grads(expert_sums)
+    wq_grad, wk_grad, wv_grad, wo_grad, wc_grad, ln1_grad, ln2_grad, b_in_grad = finish(
+        pieces, own, experts, b_in.shape
+    )
     return (
         output,
         input_grad,

time: 335 us -> 333 us (level)
  blocking collectives: 42.6 us -> 0 us
  waiting for transfers between devices: 71.3 us -> 106 us
  local copies, waits for them, and re-layouts: 4.18 us -> 8.32 us
  starting transfers between devices: 29.5 us -> 33.4 us
    all_to_all x1 -> x0, blocking collectives: 42.6 us -> none  [exchange(): lax.all_to_all(rows, BOTH, split_axis=0, concat_axis=0, tiled=True, axis_...]
    all_to_all x1 -> x2, waiting for transfers between devices: 24.9 us -> 62 us  [exchange(): lax.all_to_all(rows, BOTH, split_axis=0, concat_axis=0, tiled=True, axis_...]
    pallas_call x1, Pallas kernels: 8.97 us -> 4.58 us  [weight_grads(): call(weight_grad_kernel, 3, [pl.BlockSpec(memory_space=pltpu.SMEM), fixed...]
    unnamed x5 -> x22, local copies, waits for them, and re-layouts: 0.09 us -> 4.26 us
    all_to_all x1 -> x2, starting transfers between devices: 3.43 us -> 7.25 us  [exchange(): lax.all_to_all(rows, BOTH, split_axis=0, concat_axis=0, tiled=True, axis_...]
  transfers between devices with their start and end apart: 12 -> 13, of which waited for: 9 -> 10; matrix products, arithmetic and copies ran while one was open for 3% -> 3% of each run, Pallas kernels for 50% -> 49%
where the time goes in v3:
time: 333 us; the launch traced here: 331 us
  Pallas kernels  177 us (53%)
  waiting for transfers between devices  106 us (32%)
  starting transfers between devices  33.4 us (10%)
  local copies, waits for them, and re-layouts  8.32 us (2%)
  other arithmetic  5.49 us (2%)
    all_to_all x2, waiting for transfers between devices, exchange(): lax.all_to_all(rows, BOTH, split_axis=0, concat_axis=0, tiled=True, axis_...  62 us
    pallas_call x1, Pallas kernels, attention_backward(): pl.pallas_call(attention_backward_kernel, grid=(pairs,), in_specs=[pair_c...  47.5 us
    pallas_call x1, Pallas kernels, attention_forward(): pl.pallas_call(attention_forward_kernel, grid=(pairs,), in_specs=[pair_co...  31.9 us
    all_to_all x3, waiting for transfers between devices, along_shard(): lax.all_to_all(blocks, 'shard', split_axis=0, concat_axis=0, tiled=True)  24.5 us
    ppermute x8, waiting for transfers between devices, swap(): return lax.ppermute(block, axis, [(i, i ^ bits) for i in range(size)])  19.4 us
    pallas_call x1, Pallas kernels, combine(): call(combine_kernel, steps, [leading(COMBINE, D), leading(COMBINE, D), le...  17.4 us
    all_to_all x3, starting transfers between devices, along_shard(): lax.all_to_all(blocks, 'shard', split_axis=0, concat_axis=0, tiled=True)  16.2 us
    pallas_call x1, Pallas kernels, expert_grads(): call(expert_grad_kernel, shards, [fixed(count, 2 * D), leading(1, total,...  13.9 us
  transfers between devices with their start and end apart: 13, of which 10 were waited for; matrix products, arithmetic and copies ran while one was open for 3% of the time, Pallas kernels for 49%

profile of v3, /device:TPU:0, one launch (start us, length us, event | category | flops | bytes accessed | tf_op | source)
XLA Modules:
  0.0 331.3 jit_solution(1739987418884819240)
XLA Ops:
  0.6 1.5 pack_small.1.own_ref
  2.2 3.0 collective-permute-start
  5.2 0.9 bitcast_dynamic-update-slice_fusion.5
  6.1 1.6 collective-permute-done
  7.7 2.1 collective-permute-start.1
  9.9 2.6 collective-permute-start.2
  12.4 0.0 collective-permute-start.3
  12.4 5.7 %pack_weights.1 = bf16[8,1024,256]{2,1,0:T(8,128)(2,1)} custom-call(f32[8,512,256]{2,1,0:T(8,128)} %first_ref, f32[8,256,512]{2,1,0:T(8,128)} %second_ref), custom_call_target="tpu_custom_call" | custom-call | flops 1000000 | bytes 12582912 | tf_op jit(solution)/shard_map/pack_weights/pallas_call | solution.py:301
  18.2 6.1 %all-to-all-start = ((bf16[8,1024,256]{2,1,0:T(8,128)(2,1)}), bf16[8,1024,256]{2,1,0:T(8,128)(2,1)}, u32[]{:S(2)}, u32[]{:S(2)}) async-start(bf16[8,1024,256]{2,1,0:T(8,128)(2,1)} %pack_weights.1), calls=%async_computation | async-start | bytes 8388608 | tf_op jit(solution)/shard_map/all_to_all | solution.py:807
  24.3 0.0 collective-permute-done.1
  24.3 0.0 collective-permute-done.2
  24.4 0.0 collective-permute-done.3
  24.4 1.6 collective-permute-start.4
  26.0 11.3 %collective-permute-done.4 = bf16[128,2304]{1,0:T(8,128)(2,1)S(1)} collective-permute-done((bf16[128,2304]{1,0:T(8,128)(2,1)S(1)}, bf16[128,2304]{1,0:T(8,128)(2,1)S(1)}, u32[]{:S(2)}, u32[]{:S(2)}) %collective-permute-start.4) | collective-permute-done | bytes 589856 | tf_op jit(solution)/shard_map/ppermute | solution.py:754
  37.3 0.1 select_bitcast_fusion.3
  37.4 1.1 pad_maximum_fusion.1
  38.5 0.0 collective-permute-start.5
  38.5 0.0 copy-done.8
  38.5 0.1 copy.53
  38.6 0.2 fusion.1
  38.9 0.1 copy.54
  39.0 0.7 reshape_reshape.9.slots_ref
  39.7 0.7 reshape.69
  40.3 1.3 collective-permute-done.5
  41.6 0.2 select_bitcast_fusion.1
  41.7 1.6 pad_maximum_fusion
  43.4 10.0 %project.1 = (bf16[2048,1536]{1,0:T(8,128)(2,1)}, bf16[512,2048]{1,0:T(8,128)(2,1)}) custom-call(bf16[2048,512]{1,0:T(8,128)(2,1)} %tokens_ref.5, bf16[512,2304]{1,0:T(8,128)(2,1)} %bitcast.53, bf16[512,2304]{1,0:T(8,128)(2,1)} %bitcast.54), custom_call_target="tpu_custom_call" | custom-call | flops 3221225472 | bytes 12582912 | tf_op jit(solution)/shard_map/project/pallas_call | solution.py:479
  53.4 31.9 %attention_forward.1 = (bf16[2048,512]{1,0:T(8,128)(2,1)}, f32[4,2,2048]{2,1,0:T(2,128)}, bf16[512,2048]{1,0:T(8,128)(2,1)}, bf16[512,2048]{1,0:T(8,128)(2,1)}, bf16[512,2048]{1,0:T(8,128)(2,1)}) custom-call(bf16[2048,1536]{1,0:T(8,128)(2,1)} %get-tuple-element.51.q_ref.k_ref.v_ref, bf16[2048,1536]{1,0:T(8,128)(2,1)} %get-tuple-element.51.q_ref.k_ref.v_ref, ...), custom_call_target="tpu_custom_call" | custom-call | flops 10000000000 | bytes 8388608 | tf_op jit(solution)/shard_map/attention_forward/pallas_call | solution.py:159
  85.3 13.5 %mix.1 = (f32[2048,512]{1,0:T(8,128)}, f32[2048,128]{1,0:T(8,128)}, bf16[768,1024]{1,0:T(8,128)(2,1)}) custom-call(bf16[2048,512]{1,0:T(8,128)(2,1)} %get-tuple-element.52.attended_ref, bf16[2048,512]{1,0:T(8,128)(2,1)} %tokens_ref.5, bf16[2048,512]{1,0:T(8,128)(2,1)} %grad_ref.3, bf16[512,2304]{1,0:T(8,128)(2,1)} %bitcast.55, bf16[512,2304]{1,0:T(8,128)(2,1)} %bitcast.56, ...), custom_call_target="tpu_custom_call" | custom-call | flops 2147483648 | bytes 14680064 | tf_op jit(solution)/shard_map/mix/pallas_call | solution.py:534
  98.8 16.8 %all-to-all-done.w_ref = bf16[8,1024,256]{2,1,0:T(8,128)(2,1)} async-done(((bf16[8,1024,256]{2,1,0:T(8,128)(2,1)}), bf16[8,1024,256]{2,1,0:T(8,128)(2,1)}, u32[]{:S(2)}, u32[]{:S(2)}) %all-to-all-start) | async-done | bytes 4194336 | tf_op jit(solution)/shard_map/all_to_all | solution.py:807
  115.5 3.8 %all-to-all-start.1 = ((bf16[32,24,1024]{2,1,0:T(8,128)(2,1)}), bf16[32,24,1024]{2,1,0:T(8,128)(2,1)S(1)}, u32[]{:S(2)}, u32[]{:S(2)}) async-start(bf16[32,24,1024]{2,1,0:T(8,128)(2,1)} %bitcast.64), calls=%async_computation.1 | async-start | bytes 3145728 | tf_op jit(solution)/shard_map/all_to_all | solution.py:832
  119.5 0.0 copy-start.3
  119.5 38.6 %all-to-all-done.1 = bf16[32,24,1024]{2,1,0:T(8,128)(2,1)S(1)} async-done(((bf16[32,24,1024]{2,1,0:T(8,128)(2,1)}), bf16[32,24,1024]{2,1,0:T(8,128)(2,1)S(1)}, u32[]{:S(2)}, u32[]{:S(2)}) %all-to-all-start.1) | async-done | bytes 1572896 | tf_op jit(solution)/shard_map/all_to_all | solution.py:832
  158.0 11.2 %expert_rows.1 = bf16[768,1024]{1,0:T(8,128)(2,1)} custom-call(bf16[768,1024]{1,0:T(8,128)(2,1)S(1)} %bitcast.51, bf16[8,1024,256]{2,1,0:T(8,128)(2,1)} %all-to-all-done.w_ref, f32[8,256]{1,0:T(8,128)S(1)} %maximum_convert_fusion.bias_ref), custom_call_target="tpu_custom_call" | custom-call | flops 6442450944 | bytes 8388608 | tf_op jit(solution)/shard_map/expert_rows/pallas_call | solution.py:402
  169.2 0.0 copy-done.3
  169.2 0.0 copy-done.1
  169.2 3.4 %all-to-all-start.2 = ((bf16[32,24,1024]{2,1,0:T(8,128)(2,1)}), bf16[32,24,1024]{2,1,0:T(8,128)(2,1)}, u32[]{:S(2)}, u32[]{:S(2)}) async-start(bf16[32,24,1024]{2,1,0:T(8,128)(2,1)} %bitcast.22), calls=%async_computation.2 | async-start | bytes 3145728 | tf_op jit(solution)/shard_map/all_to_all | solution.py:832
  172.7 0.8 reshape_reshape.12.slots_ref
  173.5 0.7 reshape.70
  174.2 13.9 %expert_grads.1 = (bf16[8,1024,256]{2,1,0:T(8,128)(2,1)}, bf16[8,16,128]{2,1,0:T(8,128)(2,1)}) custom-call(bf16[768,1024]{1,0:T(8,128)(2,1)} %bitcast.52, bf16[8,1024,256]{2,1,0:T(8,128)(2,1)} %all-to-all-done.w_ref, f32[8,256]{1,0:T(8,128)} %copy-done.3), custom_call_target="tpu_custom_call" | custom-call | flops 6442450944 | bytes 14680064 | tf_op jit(solution)/shard_map/expert_grads/pallas_call | solution.py:453
  188.1 23.4 %all-to-all-done.2 = bf16[32,24,1024]{2,1,0:T(8,128)(2,1)} async-done(((bf16[32,24,1024]{2,1,0:T(8,128)(2,1)}), bf16[32,24,1024]{2,1,0:T(8,128)(2,1)}, u32[]{:S(2)}, u32[]{:S(2)}) %all-to-all-start.2) | async-done | bytes 1572896 | tf_op jit(solution)/shard_map/all_to_all | solution.py:832
  211.5 4.5 %all-to-all-start.3 = ((bf16[8,1024,256]{2,1,0:T(8,128)(2,1)}), bf16[8,1024,256]{2,1,0:T(8,128)(2,1)}, u32[]{:S(2)}, u32[]{:S(2)}) async-start(bf16[8,1024,256]{2,1,0:T(8,128)(2,1)} %get-tuple-element.73), calls=%async_computation.3 | async-start | bytes 8388608 | tf_op jit(solution)/shard_map/all_to_all | solution.py:807
  216.1 17.4 %combine.1 = (bf16[2048,512]{1,0:T(8,128)(2,1)}, f32[2048,512]{1,0:T(8,128)}, bf16[512,2048]{1,0:T(8,128)(2,1)}, f32[512,640]{1,0:T(8,128)}) custom-call(f32[2048,512]{1,0:T(8,128)} %get-tuple-element.53.residual_ref, bf16[2048,512]{1,0:T(8,128)(2,1)} %grad_ref.3, f32[2048,128]{1,0:T(8,128)} %get-tuple-element.54.probs_ref, ...), custom_call_target="tpu_custom_call" | custom-call | flops 3221225472 | bytes 25165824 | tf_op jit(solution)/shard_map/combine/pallas_call | solution.py:613
  233.5 0.0 copy-start.5
  233.5 47.5 %attention_backward.1.grad_ref.grads_ref = bf16[3,2048,512]{2,1,0:T(8,128)(2,1)} custom-call(bf16[2048,1536]{1,0:T(8,128)(2,1)} %get-tuple-element.51.q_ref.k_ref.v_ref, bf16[2048,1536]{1,0:T(8,128)(2,1)} %get-tuple-element.51.q_ref.k_ref.v_ref, bf16[512,2048]{1,0:T(8,128)(2,1)} %get-tuple-element.64.qt_ref, bf16[512,2048]{1,0:T(8,128)(2,1)} %get-tuple-element.65.kt_ref, ...), custom_call_target="tpu_custom_call" | custom-call | flops 49999998976 | bytes 16777216 | tf_op jit(solution)/shard_map/attention_backward/pallas_call | solution.py:181
  281.0 0.0 copy-start
  281.0 2.8 copy-done
  283.8 4.6 %weight_grads.1 = (bf16[2,128,2176]{2,1,0:T(8,128)(2,1)S(1)}, f32[2,128,2176]{2,1,0:T(8,128)S(1)}) custom-call(s32[1]{0:T(128)} %bitcast.24.core_ref, bf16[512,2048]{1,0:T(8,128)(2,1)S(1)} %copy-done.5, bf16[3,2048,512]{2,1,0:T(8,128)(2,1)S(1)} %copy-done, f32[512,640]{1,0:T(8,128)S(1)} %copy-done.4), custom_call_target="tpu_custom_call" | custom-call | flops 3221225472 | bytes 12582912 | tf_op jit(solution)/shard_map/weight_grads/pallas_call | solution.py:663
  288.4 0.1 collective-permute-start.6
  288.5 2.9 collective-permute-done.6
  291.4 1.4 convert_add_fusion
  292.8 0.0 copy-start.6
  292.8 1.4 copy-done.6
  294.2 0.1 fusion
  294.2 0.6 collective-permute-start.7
  294.8 11.8 %input_grads.1 = bf16[2048,512]{1,0:T(8,128)(2,1)} custom-call(bf16[3,2048,512]{2,1,0:T(8,128)(2,1)} %attention_backward.1.grad_ref.grads_ref, bf16[512,2304]{1,0:T(8,128)(2,1)} %bitcast.59, bf16[512,2304]{1,0:T(8,128)(2,1)} %bitcast.60, bf16[2048,512]{1,0:T(8,128)(2,1)} %tokens_ref.5, f32[2048,512]{1,0:T(8,128)} %get-tuple-element.72.residual_grad_ref), custom_call_target="tpu_custom_call" | custom-call | flops 3221225472 | bytes 18874368 | tf_op jit(solution)/shard_map/input_grads/pallas_call | solution.py:691
  306.6 2.3 collective-permute-done.7
  309.0 0.1 bitcast_add_fusion
  309.1 0.3 all-to-all-done.3.in_ref
  309.3 0.9 add_convert_fusion
  310.2 5.6 %all-to-all-start.4 = ((bf16[8,16,2176]{2,1,0:T(8,128)(2,1)}), bf16[8,16,2176]{2,1,0:T(8,128)(2,1)S(1)}, u32[]{:S(2)}, u32[]{:S(2)}) async-start(bf16[8,16,2176]{2,1,0:T(8,128)(2,1)} %add_convert_fusion), calls=%async_computation.4 | async-start | bytes 1114112 | tf_op jit(solution)/shard_map/all_to_all | solution.py:807
  315.8 7.2 %unpack_grads.1 = (f32[8,512,256]{2,1,0:T(8,128)}, f32[8,256,512]{2,1,0:T(8,128)}) custom-call(bf16[8,1024,256]{2,1,0:T(8,128)(2,1)} %all-to-all-done.3.in_ref), custom_call_target="tpu_custom_call" | custom-call | flops 1000000 | bytes 12582912 | tf_op jit(solution)/shard_map/unpack_grads/pallas_call | solution.py:326
  323.0 7.5 %all-to-all-done.4.pieces_ref = bf16[8,16,2176]{2,1,0:T(8,128)(2,1)S(1)} async-done(((bf16[8,16,2176]{2,1,0:T(8,128)(2,1)}), bf16[8,16,2176]{2,1,0:T(8,128)(2,1)S(1)}, u32[]{:S(2)}, u32[]{:S(2)}) %all-to-all-start.4) | async-done | bytes 557088 | tf_op jit(solution)/shard_map/all_to_all | solution.py:807
  330.5 0.8 finish.1
  (26 shorter events, 0.3 us)
Async XLA Ops:
  2.2 5.5 %collective-permute-start = (bf16[16,2304]{1,0:T(8,128)(2,1)}, bf16[16,2304]{1,0:T(8,128)(2,1)S(1)}, u32[]{:S(2)}, u32[]{:S(2)}) collective-permute-start(bf16[16,2304]{1,0:T(8,128)(2,1)} %pack_small.1.own_ref), channel_id=1, source_target_pairs={{0,1},{1,0},{2,3},{3,2},{4,5},{5,4},{6,7},{7,6},{8,9},{9,8},{10,11... | collective-permute-start | bytes 221192 | tf_op jit(solution)/shard_map/ppermute | solution.py:754
  7.7 16.6 %collective-permute-start.1 = (bf16[32,2304]{1,0:T(8,128)(2,1)S(1)}, bf16[32,2304]{1,0:T(8,128)(2,1)S(1)}, u32[]{:S(2)}, u32[]{:S(2)}) collective-permute-start(bf16[32,2304]{1,0:T(8,128)(2,1)S(1)} %bitcast.65), channel_id=1, source_target_pairs={{0,2},{1,3},{2,0},{3,1},{4,6},{5,7},{6,4},{7,5},{8,10},{9,11},{10,... | collective-permute-start | bytes 442376 | tf_op jit(solution)/shard_map/ppermute | solution.py:754
  9.9 14.5 %collective-permute-start.2 = (bf16[32,2304]{1,0:T(8,128)(2,1)S(1)}, bf16[32,2304]{1,0:T(8,128)(2,1)S(1)}, u32[]{:S(2)}, u32[]{:S(2)}) collective-permute-start(bf16[32,2304]{1,0:T(8,128)(2,1)S(1)} %bitcast.66), channel_id=1, source_target_pairs={{0,4},{1,5},{2,6},{3,7},{4,0},{5,1},{6,2},{7,3},{8,12},{9,13},{10,... | collective-permute-start | bytes 442376 | tf_op jit(solution)/shard_map/ppermute | solution.py:754
  12.4 11.9 %collective-permute-start.3 = (bf16[32,2304]{1,0:T(8,128)(2,1)S(1)}, bf16[32,2304]{1,0:T(8,128)(2,1)S(1)}, u32[]{:S(2)}, u32[]{:S(2)}) collective-permute-start(bf16[32,2304]{1,0:T(8,128)(2,1)S(1)} %bitcast.67), channel_id=1, source_target_pairs={{0,6},{1,7},{2,4},{3,5},{4,2},{5,3},{6,0},{7,1},{8,14},{9,15},{10,... | collective-permute-start | bytes 442376 | tf_op jit(solution)/shard_map/ppermute | solution.py:754
  18.2 97.3 %all-to-all-start = ((bf16[8,1024,256]{2,1,0:T(8,128)(2,1)}), bf16[8,1024,256]{2,1,0:T(8,128)(2,1)}, u32[]{:S(2)}, u32[]{:S(2)}) async-start(bf16[8,1024,256]{2,1,0:T(8,128)(2,1)} %pack_weights.1), calls=%async_computation | async-start | bytes 8388608 | tf_op jit(solution)/shard_map/all_to_all | solution.py:807
  24.4 12.9 %collective-permute-start.4 = (bf16[128,2304]{1,0:T(8,128)(2,1)S(1)}, bf16[128,2304]{1,0:T(8,128)(2,1)S(1)}, u32[]{:S(2)}, u32[]{:S(2)}) collective-permute-start(bf16[128,2304]{1,0:T(8,128)(2,1)S(1)} %bitcast.62), channel_id=1, source_target_pairs={{0,16},{8,24},{16,0},{24,8},{1,17},{9,25},{17,1},{25,9},{2,18},{10... | collective-permute-start | bytes 1769480 | tf_op jit(solution)/shard_map/ppermute | solution.py:754
  26.0 12.5 %copy-start.8 = (s32[64,8]{0,1:T(8,128)S(1)}, s32[64,8]{0,1:T(8,128)}, u32[]{:S(2)}) copy-start(s32[64,8]{0,1:T(8,128)} %param.24) | copy-start | bytes 6148
  38.5 3.1 collective-permute-start.5
  115.5 42.5 %all-to-all-start.1 = ((bf16[32,24,1024]{2,1,0:T(8,128)(2,1)}), bf16[32,24,1024]{2,1,0:T(8,128)(2,1)S(1)}, u32[]{:S(2)}, u32[]{:S(2)}) async-start(bf16[32,24,1024]{2,1,0:T(8,128)(2,1)} %bitcast.64), calls=%async_computation.1 | async-start | bytes 3145728 | tf_op jit(solution)/shard_map/all_to_all | solution.py:832
  119.5 49.8 %copy-start.3 = (f32[8,256]{1,0:T(8,128)}, f32[8,256]{1,0:T(8,128)S(1)}, u32[]{:S(2)}) copy-start(f32[8,256]{1,0:T(8,128)S(1)} %maximum_convert_fusion.bias_ref) | copy-start | bytes 24580
  158.0 11.2 %copy-start.1 = (bf16[32,24,1024]{2,1,0:T(8,128)(2,1)}, bf16[32,24,1024]{2,1,0:T(8,128)(2,1)S(1)}, u32[]{:S(2)}) copy-start(bf16[32,24,1024]{2,1,0:T(8,128)(2,1)S(1)} %all-to-all-done.1) | copy-start | bytes 4718596
  169.2 42.3 %all-to-all-start.2 = ((bf16[32,24,1024]{2,1,0:T(8,128)(2,1)}), bf16[32,24,1024]{2,1,0:T(8,128)(2,1)}, u32[]{:S(2)}, u32[]{:S(2)}) async-start(bf16[32,24,1024]{2,1,0:T(8,128)(2,1)} %bitcast.22), calls=%async_computation.2 | async-start | bytes 3145728 | tf_op jit(solution)/shard_map/all_to_all | solution.py:832
  211.5 97.8 %all-to-all-start.3 = ((bf16[8,1024,256]{2,1,0:T(8,128)(2,1)}), bf16[8,1024,256]{2,1,0:T(8,128)(2,1)}, u32[]{:S(2)}, u32[]{:S(2)}) async-start(bf16[8,1024,256]{2,1,0:T(8,128)(2,1)} %get-tuple-element.73), calls=%async_computation.3 | async-start | bytes 8388608 | tf_op jit(solution)/shard_map/all_to_all | solution.py:807
  233.5 47.6 %copy-start.4 = (f32[512,640]{1,0:T(8,128)S(1)}, f32[512,640]{1,0:T(8,128)}, u32[]{:S(2)}) copy-start(f32[512,640]{1,0:T(8,128)} %get-tuple-element.69.sums_ref) | copy-start | bytes 3932164
  233.5 47.5 %copy-start.5 = (bf16[512,2048]{1,0:T(8,128)(2,1)S(1)}, bf16[512,2048]{1,0:T(8,128)(2,1)}, u32[]{:S(2)}) copy-start(bf16[512,2048]{1,0:T(8,128)(2,1)} %get-tuple-element.63.normed_t_ref) | copy-start | bytes 6291460
  281.0 2.8 copy-start
  288.4 3.0 collective-permute-start.6
  292.8 1.4 copy-start.6
  294.2 14.7 %collective-permute-start.7 = (bf16[128,2176]{1,0:T(8,128)(2,1)S(1)}, bf16[128,2176]{1,0:T(8,128)(2,1)S(1)}, u32[]{:S(2)}, u32[]{:S(2)}) collective-permute-start(bf16[128,2176]{1,0:T(8,128)(2,1)S(1)} %fusion), channel_id=1, source_target_pairs={{0,16},{8,24},{16,0},{24,8},{1,17},{9,25},{17,1},{25,9},{2,18},{10... | collective-permute-start | bytes 1671176 | tf_op jit(solution)/shard_map/ppermute | solution.py:754
  294.8 14.1 %copy-start.7 = (f32[2,128,2176]{2,1,0:T(8,128)S(1)}, f32[2,128,2176]{2,1,0:T(8,128)}, u32[]{:S(2)}) copy-start(f32[2,128,2176]{2,1,0:T(8,128)} %copy-done.6) | copy-start | bytes 6684676
  306.6 2.7 copy-start.9
  310.2 20.4 %all-to-all-start.4 = ((bf16[8,16,2176]{2,1,0:T(8,128)(2,1)}), bf16[8,16,2176]{2,1,0:T(8,128)(2,1)S(1)}, u32[]{:S(2)}, u32[]{:S(2)}) async-start(bf16[8,16,2176]{2,1,0:T(8,128)(2,1)} %add_convert_fusion), calls=%async_computation.4 | async-start | bytes 1114112 | tf_op jit(solution)/shard_map/all_to_all | solution.py:807
  315.8 14.7 %copy-start.2 = (bf16[16,2304]{1,0:T(8,128)(2,1)S(1)}, bf16[16,2304]{1,0:T(8,128)(2,1)}, u32[]{:S(2)}) copy-start(bf16[16,2304]{1,0:T(8,128)(2,1)} %pack_small.1.own_ref) | copy-start | bytes 221188

commit v4 on v3

--- a/solution.py
+++ b/solution.py
@@ -791,16 +791,19 @@
     mine = lax.axis_index("expert")
     width = kept.shape[-1]
     steps = n_expert.bit_length() - 1
-    held = kept + swap(away, "expert", 1).astype(f32)
-    held = held.reshape((2,) * (steps - 1) + (-1, width))
+    shape = (2,) * (steps - 1) + (-1, width)
+    terms = [kept.reshape(shape), swap(away, "expert", 1).reshape(shape)]
     for step in range(1, steps):
         bit = 1 << step
         axis = steps - 1 - step
         high = (mine & bit) >> step
-        away = lax.dynamic_index_in_dim(held, high ^ 1, axis, keepdims=False).astype(bf16)
-        kept = lax.dynamic_index_in_dim(held, high, axis, keepdims=False)
-        held = kept + swap(away, "expert", bit).astype(f32)
-    return held
+
+        def half(which, axis=axis):
+            return [lax.dynamic_index_in_dim(t, which, axis, keepdims=False) for t in terms]
+
+        away = sum(t.astype(f32) for t in half(high ^ 1)).astype(bf16)
+        terms = half(high) + [swap(away, "expert", bit)]
+    return sum(t.astype(f32) for t in terms)
 
 
 def along_shard(blocks):
@@ -901,12 +904,12 @@
     grads = attention_backward(qkv, query_t, key_t, grad_t, attended_t, lse)
     core = (lax.axis_index("expert") & 1).reshape(1)
     away, kept = weight_grads(normed_t, grads, sums, core, lax.axis_size("expert"))
-    late = sum_expert(away, kept)
+    late = sum_expert(away, kept).reshape(n_shard, own.shape[0], -1)
+    late = late + jnp.pad(bias_sums.astype(f32), ((0, 0), (0, 0), (4 * D, 0)))
+    late = late.astype(bf16)
     input_grad = input_grads(grads, small, tokens, residual_grad)
     late, input_grad, expert_sums = lax.optimization_barrier((late, input_grad, expert_sums))
-    late = late.reshape(n_shard, own.shape[0], -1)
-    late = late + jnp.pad(bias_sums.astype(f32), ((0, 0), (0, 0), (4 * D, 0)))
-    pieces = along_shard(late.astype(bf16))
+    pieces = along_shard(late)
     w_in_grad, w_exp_out_grad = unpack_grads(expert_sums)
     wq_grad, wk_grad, wv_grad, wo_grad, wc_grad, ln1_grad, ln2_grad, b_in_grad = finish(
         pieces, own, experts, b_in.shape

time: 333 us -> 332 us (level)
  transfers between devices with their start and end apart: 13 -> 13, of which waited for: 10 -> 9; matrix products, arithmetic and copies ran while one was open for 3% -> 3% of each run, Pallas kernels for 49% -> 49%
where the time goes in v4:
time: 332 us; the launch traced here: 331 us
  Pallas kernels  177 us (53%)
  waiting for transfers between devices  106 us (32%)
  starting transfers between devices  33.7 us (10%)
  local copies, waits for them, and re-layouts  6.9 us (2%)
  other arithmetic  6.3 us (2%)
    all_to_all x2, waiting for transfers between devices, exchange(): lax.all_to_all(rows, BOTH, split_axis=0, concat_axis=0, tiled=True, axis_...  62 us
    pallas_call x1, Pallas kernels, attention_backward(): pl.pallas_call(attention_backward_kernel, grid=(pairs,), in_specs=[pair_c...  47.5 us
    pallas_call x1, Pallas kernels, attention_forward(): pl.pallas_call(attention_forward_kernel, grid=(pairs,), in_specs=[pair_co...  31.9 us
    all_to_all x3, waiting for transfers between devices, along_shard(): lax.all_to_all(blocks, 'shard', split_axis=0, concat_axis=0, tiled=True)  24.3 us
    ppermute x8, waiting for transfers between devices, swap(): return lax.ppermute(block, axis, [(i, i ^ bits) for i in range(size)])  19.5 us
    pallas_call x1, Pallas kernels, combine(): call(combine_kernel, steps, [leading(COMBINE, D), leading(COMBINE, D), le...  17.4 us
    all_to_all x3, starting transfers between devices, along_shard(): lax.all_to_all(blocks, 'shard', split_axis=0, concat_axis=0, tiled=True)  16.5 us
    pallas_call x1, Pallas kernels, expert_grads(): call(expert_grad_kernel, shards, [fixed(count, 2 * D), leading(1, total,...  13.9 us
  transfers between devices with their start and end apart: 13, of which 9 were waited for; matrix products, arithmetic and copies ran while one was open for 3% of the time, Pallas kernels for 49%

profile of v4, /device:TPU:0, one launch (start us, length us, event | category | flops | bytes accessed | tf_op | source)
XLA Modules:
  0.0 330.8 jit_solution(1155341484711769141)
XLA Ops:
  0.6 1.6 pack_small.1.own_ref
  2.2 3.0 collective-permute-start
  5.2 0.9 bitcast_dynamic-update-slice_fusion.5
  6.1 1.6 collective-permute-done
  7.7 2.1 collective-permute-start.1
  9.9 2.6 collective-permute-start.2
  12.5 0.0 collective-permute-start.3
  12.5 5.7 %pack_weights.1 = bf16[8,1024,256]{2,1,0:T(8,128)(2,1)} custom-call(f32[8,512,256]{2,1,0:T(8,128)} %first_ref, f32[8,256,512]{2,1,0:T(8,128)} %second_ref), custom_call_target="tpu_custom_call" | custom-call | flops 1000000 | bytes 12582912 | tf_op jit(solution)/shard_map/pack_weights/pallas_call | solution.py:301
  18.2 6.1 %all-to-all-start = ((bf16[8,1024,256]{2,1,0:T(8,128)(2,1)}), bf16[8,1024,256]{2,1,0:T(8,128)(2,1)}, u32[]{:S(2)}, u32[]{:S(2)}) async-start(bf16[8,1024,256]{2,1,0:T(8,128)(2,1)} %pack_weights.1), calls=%async_computation | async-start | bytes 8388608 | tf_op jit(solution)/shard_map/all_to_all | solution.py:810
  24.3 0.0 collective-permute-done.1
  24.4 0.0 collective-permute-done.2
  24.4 0.0 collective-permute-done.3
  24.4 1.6 collective-permute-start.4
  26.0 11.3 %collective-permute-done.4 = bf16[128,2304]{1,0:T(8,128)(2,1)S(1)} collective-permute-done((bf16[128,2304]{1,0:T(8,128)(2,1)S(1)}, bf16[128,2304]{1,0:T(8,128)(2,1)S(1)}, u32[]{:S(2)}, u32[]{:S(2)}) %collective-permute-start.4) | collective-permute-done | bytes 589856 | tf_op jit(solution)/shard_map/ppermute | solution.py:754
  37.3 0.1 select_bitcast_fusion.3
  37.4 0.0 copy-start.6
  37.4 1.1 pad_maximum_fusion.1
  38.5 0.0 collective-permute-start.5
  38.6 0.0 copy-done.6
  38.6 0.1 copy.53
  38.7 0.2 fusion.1
  38.9 0.1 copy.54
  39.0 0.7 reshape_reshape.9.slots_ref
  39.7 0.7 reshape.73
  40.3 1.3 collective-permute-done.5
  41.6 0.2 select_bitcast_fusion.1
  41.8 1.6 pad_maximum_fusion
  43.4 10.0 %project.1 = (bf16[2048,1536]{1,0:T(8,128)(2,1)}, bf16[512,2048]{1,0:T(8,128)(2,1)}) custom-call(bf16[2048,512]{1,0:T(8,128)(2,1)} %tokens_ref.5, bf16[512,2304]{1,0:T(8,128)(2,1)} %bitcast.53, bf16[512,2304]{1,0:T(8,128)(2,1)} %bitcast.54), custom_call_target="tpu_custom_call" | custom-call | flops 3221225472 | bytes 12582912 | tf_op jit(solution)/shard_map/project/pallas_call | solution.py:479
  53.4 31.9 %attention_forward.1 = (bf16[2048,512]{1,0:T(8,128)(2,1)}, f32[4,2,2048]{2,1,0:T(2,128)}, bf16[512,2048]{1,0:T(8,128)(2,1)}, bf16[512,2048]{1,0:T(8,128)(2,1)}, bf16[512,2048]{1,0:T(8,128)(2,1)}) custom-call(bf16[2048,1536]{1,0:T(8,128)(2,1)} %get-tuple-element.51.q_ref.k_ref.v_ref, bf16[2048,1536]{1,0:T(8,128)(2,1)} %get-tuple-element.51.q_ref.k_ref.v_ref, ...), custom_call_target="tpu_custom_call" | custom-call | flops 10000000000 | bytes 8388608 | tf_op jit(solution)/shard_map/attention_forward/pallas_call | solution.py:159
  85.3 13.5 %mix.1 = (f32[2048,512]{1,0:T(8,128)}, f32[2048,128]{1,0:T(8,128)}, bf16[768,1024]{1,0:T(8,128)(2,1)}) custom-call(bf16[2048,512]{1,0:T(8,128)(2,1)} %get-tuple-element.52.attended_ref, bf16[2048,512]{1,0:T(8,128)(2,1)} %tokens_ref.5, bf16[2048,512]{1,0:T(8,128)(2,1)} %grad_ref.3, bf16[512,2304]{1,0:T(8,128)(2,1)} %bitcast.55, bf16[512,2304]{1,0:T(8,128)(2,1)} %bitcast.56, ...), custom_call_target="tpu_custom_call" | custom-call | flops 2147483648 | bytes 14680064 | tf_op jit(solution)/shard_map/mix/pallas_call | solution.py:534
  98.8 16.8 %all-to-all-done.w_ref = bf16[8,1024,256]{2,1,0:T(8,128)(2,1)} async-done(((bf16[8,1024,256]{2,1,0:T(8,128)(2,1)}), bf16[8,1024,256]{2,1,0:T(8,128)(2,1)}, u32[]{:S(2)}, u32[]{:S(2)}) %all-to-all-start) | async-done | bytes 4194336 | tf_op jit(solution)/shard_map/all_to_all | solution.py:810
  115.6 3.8 %all-to-all-start.1 = ((bf16[32,24,1024]{2,1,0:T(8,128)(2,1)}), bf16[32,24,1024]{2,1,0:T(8,128)(2,1)S(1)}, u32[]{:S(2)}, u32[]{:S(2)}) async-start(bf16[32,24,1024]{2,1,0:T(8,128)(2,1)} %bitcast.64), calls=%async_computation.1 | async-start | bytes 3145728 | tf_op jit(solution)/shard_map/all_to_all | solution.py:835
  119.5 0.0 copy-start.3
  119.5 38.6 %all-to-all-done.1 = bf16[32,24,1024]{2,1,0:T(8,128)(2,1)S(1)} async-done(((bf16[32,24,1024]{2,1,0:T(8,128)(2,1)}), bf16[32,24,1024]{2,1,0:T(8,128)(2,1)S(1)}, u32[]{:S(2)}, u32[]{:S(2)}) %all-to-all-start.1) | async-done | bytes 1572896 | tf_op jit(solution)/shard_map/all_to_all | solution.py:835
  158.1 11.2 %expert_rows.1 = bf16[768,1024]{1,0:T(8,128)(2,1)} custom-call(bf16[768,1024]{1,0:T(8,128)(2,1)S(1)} %bitcast.51, bf16[8,1024,256]{2,1,0:T(8,128)(2,1)} %all-to-all-done.w_ref, f32[8,256]{1,0:T(8,128)S(1)} %maximum_convert_fusion.bias_ref), custom_call_target="tpu_custom_call" | custom-call | flops 6442450944 | bytes 8388608 | tf_op jit(solution)/shard_map/expert_rows/pallas_call | solution.py:402
  169.2 0.0 copy-done.3
  169.2 0.0 copy-done.1
  169.3 3.4 %all-to-all-start.2 = ((bf16[32,24,1024]{2,1,0:T(8,128)(2,1)}), bf16[32,24,1024]{2,1,0:T(8,128)(2,1)}, u32[]{:S(2)}, u32[]{:S(2)}) async-start(bf16[32,24,1024]{2,1,0:T(8,128)(2,1)} %bitcast.22), calls=%async_computation.2 | async-start | bytes 3145728 | tf_op jit(solution)/shard_map/all_to_all | solution.py:835
  172.7 0.8 reshape_reshape.12.slots_ref
  173.5 0.7 reshape.74
  174.2 13.9 %expert_grads.1 = (bf16[8,1024,256]{2,1,0:T(8,128)(2,1)}, bf16[8,16,128]{2,1,0:T(8,128)(2,1)}) custom-call(bf16[768,1024]{1,0:T(8,128)(2,1)} %bitcast.52, bf16[8,1024,256]{2,1,0:T(8,128)(2,1)} %all-to-all-done.w_ref, f32[8,256]{1,0:T(8,128)} %copy-done.3), custom_call_target="tpu_custom_call" | custom-call | flops 6442450944 | bytes 14680064 | tf_op jit(solution)/shard_map/expert_grads/pallas_call | solution.py:453
  188.1 23.4 %all-to-all-done.2 = bf16[32,24,1024]{2,1,0:T(8,128)(2,1)} async-done(((bf16[32,24,1024]{2,1,0:T(8,128)(2,1)}), bf16[32,24,1024]{2,1,0:T(8,128)(2,1)}, u32[]{:S(2)}, u32[]{:S(2)}) %all-to-all-start.2) | async-done | bytes 1572896 | tf_op jit(solution)/shard_map/all_to_all | solution.py:835
  211.5 4.6 %all-to-all-start.3 = ((bf16[8,1024,256]{2,1,0:T(8,128)(2,1)}), bf16[8,1024,256]{2,1,0:T(8,128)(2,1)}, u32[]{:S(2)}, u32[]{:S(2)}) async-start(bf16[8,1024,256]{2,1,0:T(8,128)(2,1)} %get-tuple-element.74), calls=%async_computation.3 | async-start | bytes 8388608 | tf_op jit(solution)/shard_map/all_to_all | solution.py:810
  216.1 17.4 %combine.1 = (bf16[2048,512]{1,0:T(8,128)(2,1)}, f32[2048,512]{1,0:T(8,128)}, bf16[512,2048]{1,0:T(8,128)(2,1)}, f32[512,640]{1,0:T(8,128)}) custom-call(f32[2048,512]{1,0:T(8,128)} %get-tuple-element.53.residual_ref, bf16[2048,512]{1,0:T(8,128)(2,1)} %grad_ref.3, f32[2048,128]{1,0:T(8,128)} %get-tuple-element.54.probs_ref, ...), custom_call_target="tpu_custom_call" | custom-call | flops 3221225472 | bytes 25165824 | tf_op jit(solution)/shard_map/combine/pallas_call | solution.py:613
  233.5 0.0 copy-start.4
  233.5 0.0 copy-start.5
  233.5 47.5 %attention_backward.1.grad_ref.grads_ref = bf16[3,2048,512]{2,1,0:T(8,128)(2,1)} custom-call(bf16[2048,1536]{1,0:T(8,128)(2,1)} %get-tuple-element.51.q_ref.k_ref.v_ref, bf16[2048,1536]{1,0:T(8,128)(2,1)} %get-tuple-element.51.q_ref.k_ref.v_ref, bf16[512,2048]{1,0:T(8,128)(2,1)} %get-tuple-element.64.qt_ref, bf16[512,2048]{1,0:T(8,128)(2,1)} %get-tuple-element.65.kt_ref, ...), custom_call_target="tpu_custom_call" | custom-call | flops 49999998976 | bytes 16777216 | tf_op jit(solution)/shard_map/attention_backward/pallas_call | solution.py:181
  281.0 0.0 copy-done.4
  281.1 0.0 copy-done.5
  281.1 2.8 copy-done
  283.8 4.6 %weight_grads.1 = (bf16[2,128,2176]{2,1,0:T(8,128)(2,1)S(1)}, f32[2,128,2176]{2,1,0:T(8,128)S(1)}) custom-call(s32[1]{0:T(128)} %bitcast.24.core_ref, bf16[512,2048]{1,0:T(8,128)(2,1)S(1)} %copy-done.5, bf16[3,2048,512]{2,1,0:T(8,128)(2,1)S(1)} %copy-done, f32[512,640]{1,0:T(8,128)S(1)} %copy-done.4), custom_call_target="tpu_custom_call" | custom-call | flops 3221225472 | bytes 12582912 | tf_op jit(solution)/shard_map/weight_grads/pallas_call | solution.py:663
  288.4 0.1 collective-permute-start.6
  288.5 2.9 collective-permute-done.6
  291.4 1.1 fusion
  292.5 0.6 collective-permute-start.7
  293.1 11.7 %input_grads.1 = bf16[2048,512]{1,0:T(8,128)(2,1)} custom-call(bf16[3,2048,512]{2,1,0:T(8,128)(2,1)} %attention_backward.1.grad_ref.grads_ref, bf16[512,2304]{1,0:T(8,128)(2,1)} %bitcast.59, bf16[512,2304]{1,0:T(8,128)(2,1)} %bitcast.60, bf16[2048,512]{1,0:T(8,128)(2,1)} %tokens_ref.5, f32[2048,512]{1,0:T(8,128)} %get-tuple-element.73.residual_grad_ref), custom_call_target="tpu_custom_call" | custom-call | flops 3221225472 | bytes 18874368 | tf_op jit(solution)/shard_map/input_grads/pallas_call | solution.py:691
  304.8 2.5 collective-permute-done.7
  307.3 1.2 bitcast_add_fusion
  308.5 0.9 add_convert_fusion
  309.4 0.0 all-to-all-done.3.in_ref
  309.4 5.9 %all-to-all-start.4 = ((bf16[8,16,2176]{2,1,0:T(8,128)(2,1)}), bf16[8,16,2176]{2,1,0:T(8,128)(2,1)S(1)}, u32[]{:S(2)}, u32[]{:S(2)}) async-start(bf16[8,16,2176]{2,1,0:T(8,128)(2,1)} %add_convert_fusion), calls=%async_computation.4 | async-start | bytes 1114112 | tf_op jit(solution)/shard_map/all_to_all | solution.py:810
  315.2 7.2 %unpack_grads.1 = (f32[8,512,256]{2,1,0:T(8,128)}, f32[8,256,512]{2,1,0:T(8,128)}) custom-call(bf16[8,1024,256]{2,1,0:T(8,128)(2,1)} %all-to-all-done.3.in_ref), custom_call_target="tpu_custom_call" | custom-call | flops 1000000 | bytes 12582912 | tf_op jit(solution)/shard_map/unpack_grads/pallas_call | solution.py:326
  322.5 7.6 %all-to-all-done.4.pieces_ref = bf16[8,16,2176]{2,1,0:T(8,128)(2,1)S(1)} async-done(((bf16[8,16,2176]{2,1,0:T(8,128)(2,1)}), bf16[8,16,2176]{2,1,0:T(8,128)(2,1)S(1)}, u32[]{:S(2)}, u32[]{:S(2)}) %all-to-all-start.4) | async-done | bytes 557088 | tf_op jit(solution)/shard_map/all_to_all | solution.py:810
  330.1 0.8 finish.1
  (21 shorter events, 0.3 us)
Async XLA Ops:
  2.2 5.5 %collective-permute-start = (bf16[16,2304]{1,0:T(8,128)(2,1)}, bf16[16,2304]{1,0:T(8,128)(2,1)S(1)}, u32[]{:S(2)}, u32[]{:S(2)}) collective-permute-start(bf16[16,2304]{1,0:T(8,128)(2,1)} %pack_small.1.own_ref), channel_id=1, source_target_pairs={{0,1},{1,0},{2,3},{3,2},{4,5},{5,4},{6,7},{7,6},{8,9},{9,8},{10,11... | collective-permute-start | bytes 221192 | tf_op jit(solution)/shard_map/ppermute | solution.py:754
  7.7 16.6 %collective-permute-start.1 = (bf16[32,2304]{1,0:T(8,128)(2,1)S(1)}, bf16[32,2304]{1,0:T(8,128)(2,1)S(1)}, u32[]{:S(2)}, u32[]{:S(2)}) collective-permute-start(bf16[32,2304]{1,0:T(8,128)(2,1)S(1)} %bitcast.65), channel_id=1, source_target_pairs={{0,2},{1,3},{2,0},{3,1},{4,6},{5,7},{6,4},{7,5},{8,10},{9,11},{10,... | collective-permute-start | bytes 442376 | tf_op jit(solution)/shard_map/ppermute | solution.py:754
  9.9 14.5 %collective-permute-start.2 = (bf16[32,2304]{1,0:T(8,128)(2,1)S(1)}, bf16[32,2304]{1,0:T(8,128)(2,1)S(1)}, u32[]{:S(2)}, u32[]{:S(2)}) collective-permute-start(bf16[32,2304]{1,0:T(8,128)(2,1)S(1)} %bitcast.66), channel_id=1, source_target_pairs={{0,4},{1,5},{2,6},{3,7},{4,0},{5,1},{6,2},{7,3},{8,12},{9,13},{10,... | collective-permute-start | bytes 442376 | tf_op jit(solution)/shard_map/ppermute | solution.py:754
  12.5 11.9 %collective-permute-start.3 = (bf16[32,2304]{1,0:T(8,128)(2,1)S(1)}, bf16[32,2304]{1,0:T(8,128)(2,1)S(1)}, u32[]{:S(2)}, u32[]{:S(2)}) collective-permute-start(bf16[32,2304]{1,0:T(8,128)(2,1)S(1)} %bitcast.67), channel_id=1, source_target_pairs={{0,6},{1,7},{2,4},{3,5},{4,2},{5,3},{6,0},{7,1},{8,14},{9,15},{10,... | collective-permute-start | bytes 442376 | tf_op jit(solution)/shard_map/ppermute | solution.py:754
  18.2 97.3 %all-to-all-start = ((bf16[8,1024,256]{2,1,0:T(8,128)(2,1)}), bf16[8,1024,256]{2,1,0:T(8,128)(2,1)}, u32[]{:S(2)}, u32[]{:S(2)}) async-start(bf16[8,1024,256]{2,1,0:T(8,128)(2,1)} %pack_weights.1), calls=%async_computation | async-start | bytes 8388608 | tf_op jit(solution)/shard_map/all_to_all | solution.py:810
  24.4 12.9 %collective-permute-start.4 = (bf16[128,2304]{1,0:T(8,128)(2,1)S(1)}, bf16[128,2304]{1,0:T(8,128)(2,1)S(1)}, u32[]{:S(2)}, u32[]{:S(2)}) collective-permute-start(bf16[128,2304]{1,0:T(8,128)(2,1)S(1)} %bitcast.62), channel_id=1, source_target_pairs={{0,16},{8,24},{16,0},{24,8},{1,17},{9,25},{17,1},{25,9},{2,18},{10... | collective-permute-start | bytes 1769480 | tf_op jit(solution)/shard_map/ppermute | solution.py:754
  37.4 1.1 copy-start.6
  38.5 3.1 collective-permute-start.5
  115.6 42.5 %all-to-all-start.1 = ((bf16[32,24,1024]{2,1,0:T(8,128)(2,1)}), bf16[32,24,1024]{2,1,0:T(8,128)(2,1)S(1)}, u32[]{:S(2)}, u32[]{:S(2)}) async-start(bf16[32,24,1024]{2,1,0:T(8,128)(2,1)} %bitcast.64), calls=%async_computation.1 | async-start | bytes 3145728 | tf_op jit(solution)/shard_map/all_to_all | solution.py:835
  119.5 49.8 %copy-start.3 = (f32[8,256]{1,0:T(8,128)}, f32[8,256]{1,0:T(8,128)S(1)}, u32[]{:S(2)}) copy-start(f32[8,256]{1,0:T(8,128)S(1)} %maximum_convert_fusion.bias_ref) | copy-start | bytes 24580
  158.1 11.2 %copy-start.1 = (bf16[32,24,1024]{2,1,0:T(8,128)(2,1)}, bf16[32,24,1024]{2,1,0:T(8,128)(2,1)S(1)}, u32[]{:S(2)}) copy-start(bf16[32,24,1024]{2,1,0:T(8,128)(2,1)S(1)} %all-to-all-done.1) | copy-start | bytes 4718596
  169.3 42.3 %all-to-all-start.2 = ((bf16[32,24,1024]{2,1,0:T(8,128)(2,1)}), bf16[32,24,1024]{2,1,0:T(8,128)(2,1)}, u32[]{:S(2)}, u32[]{:S(2)}) async-start(bf16[32,24,1024]{2,1,0:T(8,128)(2,1)} %bitcast.22), calls=%async_computation.2 | async-start | bytes 3145728 | tf_op jit(solution)/shard_map/all_to_all | solution.py:835
  211.5 97.8 %all-to-all-start.3 = ((bf16[8,1024,256]{2,1,0:T(8,128)(2,1)}), bf16[8,1024,256]{2,1,0:T(8,128)(2,1)}, u32[]{:S(2)}, u32[]{:S(2)}) async-start(bf16[8,1024,256]{2,1,0:T(8,128)(2,1)} %get-tuple-element.74), calls=%async_computation.3 | async-start | bytes 8388608 | tf_op jit(solution)/shard_map/all_to_all | solution.py:810
  233.5 47.6 %copy-start.4 = (f32[512,640]{1,0:T(8,128)S(1)}, f32[512,640]{1,0:T(8,128)}, u32[]{:S(2)}) copy-start(f32[512,640]{1,0:T(8,128)} %get-tuple-element.69.sums_ref) | copy-start | bytes 3932164
  233.5 47.5 %copy-start.5 = (bf16[512,2048]{1,0:T(8,128)(2,1)S(1)}, bf16[512,2048]{1,0:T(8,128)(2,1)}, u32[]{:S(2)}) copy-start(bf16[512,2048]{1,0:T(8,128)(2,1)} %get-tuple-element.63.normed_t_ref) | copy-start | bytes 6291460
  281.1 2.8 copy-start
  288.4 3.0 collective-permute-start.6
  292.5 14.7 %collective-permute-start.7 = (bf16[128,2176]{1,0:T(8,128)(2,1)S(1)}, bf16[128,2176]{1,0:T(8,128)(2,1)S(1)}, u32[]{:S(2)}, u32[]{:S(2)}) collective-permute-start(bf16[128,2176]{1,0:T(8,128)(2,1)S(1)} %fusion), channel_id=1, source_target_pairs={{0,16},{8,24},{16,0},{24,8},{1,17},{9,25},{17,1},{25,9},{2,18},{10... | collective-permute-start | bytes 1671176 | tf_op jit(solution)/shard_map/ppermute | solution.py:754
  304.8 3.7 %copy-start.7 = (bf16[8,16,128]{2,1,0:T(8,128)(2,1)S(1)}, bf16[8,16,128]{2,1,0:T(8,128)(2,1)}, u32[]{:S(2)}) copy-start(bf16[8,16,128]{2,1,0:T(8,128)(2,1)} %get-tuple-element.72) | copy-start | bytes 98308
  309.4 20.7 %all-to-all-start.4 = ((bf16[8,16,2176]{2,1,0:T(8,128)(2,1)}), bf16[8,16,2176]{2,1,0:T(8,128)(2,1)S(1)}, u32[]{:S(2)}, u32[]{:S(2)}) async-start(bf16[8,16,2176]{2,1,0:T(8,128)(2,1)} %add_convert_fusion), calls=%async_computation.4 | async-start | bytes 1114112 | tf_op jit(solution)/shard_map/all_to_all | solution.py:810
  315.2 14.8 %copy-start.2 = (bf16[16,2304]{1,0:T(8,128)(2,1)S(1)}, bf16[16,2304]{1,0:T(8,128)(2,1)}, u32[]{:S(2)}) copy-start(bf16[16,2304]{1,0:T(8,128)(2,1)} %pack_small.1.own_ref) | copy-start | bytes 221188

commit v5 on v4

--- a/solution.py
+++ b/solution.py
@@ -202,7 +202,7 @@
 COMBINE = 512
 LANES = 128
 BIAS_LANE = 64
-SHARDS_A_STEP = 4
+SHARDS_A_STEP = 8
 GAIN_ONE = LANES - 2
 GAIN_TWO = LANES - 1
 

time: 332 us -> 332 us (level)
  no operation moved by 1% of the time
where the time goes in v5:
time: 332 us; the launch traced here: 331 us
  Pallas kernels  177 us (53%)
  waiting for transfers between devices  106 us (32%)
  starting transfers between devices  33.7 us (10%)
  local copies, waits for them, and re-layouts  6.9 us (2%)
  other arithmetic  6.3 us (2%)
    all_to_all x2, waiting for transfers between devices, exchange(): lax.all_to_all(rows, BOTH, split_axis=0, concat_axis=0, tiled=True, axis_...  62 us
    pallas_call x1, Pallas kernels, attention_backward(): pl.pallas_call(attention_backward_kernel, grid=(pairs,), in_specs=[pair_c...  47.5 us
    pallas_call x1, Pallas kernels, attention_forward(): pl.pallas_call(attention_forward_kernel, grid=(pairs,), in_specs=[pair_co...  31.9 us
    all_to_all x3, waiting for transfers between devices, along_shard(): lax.all_to_all(blocks, 'shard', split_axis=0, concat_axis=0, tiled=True)  24.3 us
    ppermute x8, waiting for transfers between devices, swap(): return lax.ppermute(block, axis, [(i, i ^ bits) for i in range(size)])  19.5 us
    pallas_call x1, Pallas kernels, combine(): call(combine_kernel, steps, [leading(COMBINE, D), leading(COMBINE, D), le...  17.4 us
    all_to_all x3, starting transfers between devices, along_shard(): lax.all_to_all(blocks, 'shard', split_axis=0, concat_axis=0, tiled=True)  16.5 us
    pallas_call x1, Pallas kernels, expert_grads(): call(expert_grad_kernel, shards, [fixed(count, 2 * D), leading(1, total,...  13.9 us
  transfers between devices with their start and end apart: 13, of which 9 were waited for; matrix products, arithmetic and copies ran while one was open for 3% of the time, Pallas kernels for 49%

profile of v5, /device:TPU:0, one launch (start us, length us, event | category | flops | bytes accessed | tf_op | source)
XLA Modules:
  0.0 330.6 jit_solution(4699900120465712657)
XLA Ops:
  0.6 1.6 pack_small.1.own_ref
  2.2 3.0 collective-permute-start
  5.2 0.9 bitcast_dynamic-update-slice_fusion.5
  6.1 1.6 collective-permute-done
  7.7 2.1 collective-permute-start.1
  9.9 2.6 collective-permute-start.2
  12.5 0.0 collective-permute-start.3
  12.5 5.7 %pack_weights.1 = bf16[8,1024,256]{2,1,0:T(8,128)(2,1)} custom-call(f32[8,512,256]{2,1,0:T(8,128)} %first_ref, f32[8,256,512]{2,1,0:T(8,128)} %second_ref), custom_call_target="tpu_custom_call" | custom-call | flops 1000000 | bytes 12582912 | tf_op jit(solution)/shard_map/pack_weights/pallas_call | solution.py:301
  18.2 6.1 %all-to-all-start = ((bf16[8,1024,256]{2,1,0:T(8,128)(2,1)}), bf16[8,1024,256]{2,1,0:T(8,128)(2,1)}, u32[]{:S(2)}, u32[]{:S(2)}) async-start(bf16[8,1024,256]{2,1,0:T(8,128)(2,1)} %pack_weights.1), calls=%async_computation | async-start | bytes 8388608 | tf_op jit(solution)/shard_map/all_to_all | solution.py:810
  24.3 0.0 collective-permute-done.1
  24.4 0.0 collective-permute-done.2
  24.4 0.0 collective-permute-done.3
  24.4 1.6 collective-permute-start.4
  26.0 11.3 %collective-permute-done.4 = bf16[128,2304]{1,0:T(8,128)(2,1)S(1)} collective-permute-done((bf16[128,2304]{1,0:T(8,128)(2,1)S(1)}, bf16[128,2304]{1,0:T(8,128)(2,1)S(1)}, u32[]{:S(2)}, u32[]{:S(2)}) %collective-permute-start.4) | collective-permute-done | bytes 589856 | tf_op jit(solution)/shard_map/ppermute | solution.py:754
  37.3 0.1 select_bitcast_fusion.3
  37.4 0.0 copy-start.6
  37.4 1.1 pad_maximum_fusion.1
  38.5 0.0 collective-permute-start.5
  38.6 0.0 copy-done.6
  38.6 0.1 copy.53
  38.7 0.2 fusion.1
  38.9 0.1 copy.54
  39.0 0.7 reshape_reshape.9.slots_ref
  39.7 0.7 reshape.73
  40.3 1.3 collective-permute-done.5
  41.6 0.2 select_bitcast_fusion.1
  41.8 1.6 pad_maximum_fusion
  43.4 10.0 %project.1 = (bf16[2048,1536]{1,0:T(8,128)(2,1)}, bf16[512,2048]{1,0:T(8,128)(2,1)}) custom-call(bf16[2048,512]{1,0:T(8,128)(2,1)} %tokens_ref.5, bf16[512,2304]{1,0:T(8,128)(2,1)} %bitcast.53, bf16[512,2304]{1,0:T(8,128)(2,1)} %bitcast.54), custom_call_target="tpu_custom_call" | custom-call | flops 3221225472 | bytes 12582912 | tf_op jit(solution)/shard_map/project/pallas_call | solution.py:479
  53.4 31.9 %attention_forward.1 = (bf16[2048,512]{1,0:T(8,128)(2,1)}, f32[4,2,2048]{2,1,0:T(2,128)}, bf16[512,2048]{1,0:T(8,128)(2,1)}, bf16[512,2048]{1,0:T(8,128)(2,1)}, bf16[512,2048]{1,0:T(8,128)(2,1)}) custom-call(bf16[2048,1536]{1,0:T(8,128)(2,1)} %get-tuple-element.51.q_ref.k_ref.v_ref, bf16[2048,1536]{1,0:T(8,128)(2,1)} %get-tuple-element.51.q_ref.k_ref.v_ref, ...), custom_call_target="tpu_custom_call" | custom-call | flops 10000000000 | bytes 8388608 | tf_op jit(solution)/shard_map/attention_forward/pallas_call | solution.py:159
  85.3 13.5 %mix.1 = (f32[2048,512]{1,0:T(8,128)}, f32[2048,128]{1,0:T(8,128)}, bf16[768,1024]{1,0:T(8,128)(2,1)}) custom-call(bf16[2048,512]{1,0:T(8,128)(2,1)} %get-tuple-element.52.attended_ref, bf16[2048,512]{1,0:T(8,128)(2,1)} %tokens_ref.5, bf16[2048,512]{1,0:T(8,128)(2,1)} %grad_ref.3, bf16[512,2304]{1,0:T(8,128)(2,1)} %bitcast.55, bf16[512,2304]{1,0:T(8,128)(2,1)} %bitcast.56, ...), custom_call_target="tpu_custom_call" | custom-call | flops 2147483648 | bytes 14680064 | tf_op jit(solution)/shard_map/mix/pallas_call | solution.py:534
  98.8 16.8 %all-to-all-done.w_ref = bf16[8,1024,256]{2,1,0:T(8,128)(2,1)} async-done(((bf16[8,1024,256]{2,1,0:T(8,128)(2,1)}), bf16[8,1024,256]{2,1,0:T(8,128)(2,1)}, u32[]{:S(2)}, u32[]{:S(2)}) %all-to-all-start) | async-done | bytes 4194336 | tf_op jit(solution)/shard_map/all_to_all | solution.py:810
  115.6 3.8 %all-to-all-start.1 = ((bf16[32,24,1024]{2,1,0:T(8,128)(2,1)}), bf16[32,24,1024]{2,1,0:T(8,128)(2,1)S(1)}, u32[]{:S(2)}, u32[]{:S(2)}) async-start(bf16[32,24,1024]{2,1,0:T(8,128)(2,1)} %bitcast.64), calls=%async_computation.1 | async-start | bytes 3145728 | tf_op jit(solution)/shard_map/all_to_all | solution.py:835
  119.5 0.0 copy-start.3
  119.5 38.6 %all-to-all-done.1 = bf16[32,24,1024]{2,1,0:T(8,128)(2,1)S(1)} async-done(((bf16[32,24,1024]{2,1,0:T(8,128)(2,1)}), bf16[32,24,1024]{2,1,0:T(8,128)(2,1)S(1)}, u32[]{:S(2)}, u32[]{:S(2)}) %all-to-all-start.1) | async-done | bytes 1572896 | tf_op jit(solution)/shard_map/all_to_all | solution.py:835
  158.1 10.9 %expert_rows.1 = bf16[768,1024]{1,0:T(8,128)(2,1)} custom-call(bf16[768,1024]{1,0:T(8,128)(2,1)S(1)} %bitcast.51, bf16[8,1024,256]{2,1,0:T(8,128)(2,1)} %all-to-all-done.w_ref, f32[8,256]{1,0:T(8,128)S(1)} %maximum_convert_fusion.bias_ref), custom_call_target="tpu_custom_call" | custom-call | flops 6442450944 | bytes 8388608 | tf_op jit(solution)/shard_map/expert_rows/pallas_call | solution.py:402
  169.0 0.0 copy-done.3
  169.0 0.0 copy-done.1
  169.0 3.4 %all-to-all-start.2 = ((bf16[32,24,1024]{2,1,0:T(8,128)(2,1)}), bf16[32,24,1024]{2,1,0:T(8,128)(2,1)}, u32[]{:S(2)}, u32[]{:S(2)}) async-start(bf16[32,24,1024]{2,1,0:T(8,128)(2,1)} %bitcast.22), calls=%async_computation.2 | async-start | bytes 3145728 | tf_op jit(solution)/shard_map/all_to_all | solution.py:835
  172.4 0.8 reshape_reshape.12.slots_ref
  173.2 0.7 reshape.74
  173.9 13.9 %expert_grads.1 = (bf16[8,1024,256]{2,1,0:T(8,128)(2,1)}, bf16[8,16,128]{2,1,0:T(8,128)(2,1)}) custom-call(bf16[768,1024]{1,0:T(8,128)(2,1)} %bitcast.52, bf16[8,1024,256]{2,1,0:T(8,128)(2,1)} %all-to-all-done.w_ref, f32[8,256]{1,0:T(8,128)} %copy-done.3), custom_call_target="tpu_custom_call" | custom-call | flops 6442450944 | bytes 14680064 | tf_op jit(solution)/shard_map/expert_grads/pallas_call | solution.py:453
  187.8 23.4 %all-to-all-done.2 = bf16[32,24,1024]{2,1,0:T(8,128)(2,1)} async-done(((bf16[32,24,1024]{2,1,0:T(8,128)(2,1)}), bf16[32,24,1024]{2,1,0:T(8,128)(2,1)}, u32[]{:S(2)}, u32[]{:S(2)}) %all-to-all-start.2) | async-done | bytes 1572896 | tf_op jit(solution)/shard_map/all_to_all | solution.py:835
  211.2 4.6 %all-to-all-start.3 = ((bf16[8,1024,256]{2,1,0:T(8,128)(2,1)}), bf16[8,1024,256]{2,1,0:T(8,128)(2,1)}, u32[]{:S(2)}, u32[]{:S(2)}) async-start(bf16[8,1024,256]{2,1,0:T(8,128)(2,1)} %get-tuple-element.74), calls=%async_computation.3 | async-start | bytes 8388608 | tf_op jit(solution)/shard_map/all_to_all | solution.py:810
  215.8 17.4 %combine.1 = (bf16[2048,512]{1,0:T(8,128)(2,1)}, f32[2048,512]{1,0:T(8,128)}, bf16[512,2048]{1,0:T(8,128)(2,1)}, f32[512,640]{1,0:T(8,128)}) custom-call(f32[2048,512]{1,0:T(8,128)} %get-tuple-element.53.residual_ref, bf16[2048,512]{1,0:T(8,128)(2,1)} %grad_ref.3, f32[2048,128]{1,0:T(8,128)} %get-tuple-element.54.probs_ref, ...), custom_call_target="tpu_custom_call" | custom-call | flops 3221225472 | bytes 25165824 | tf_op jit(solution)/shard_map/combine/pallas_call | solution.py:613
  233.2 0.0 copy-start.4
  233.2 0.0 copy-start.5
  233.2 47.5 %attention_backward.1.grad_ref.grads_ref = bf16[3,2048,512]{2,1,0:T(8,128)(2,1)} custom-call(bf16[2048,1536]{1,0:T(8,128)(2,1)} %get-tuple-element.51.q_ref.k_ref.v_ref, bf16[2048,1536]{1,0:T(8,128)(2,1)} %get-tuple-element.51.q_ref.k_ref.v_ref, bf16[512,2048]{1,0:T(8,128)(2,1)} %get-tuple-element.64.qt_ref, bf16[512,2048]{1,0:T(8,128)(2,1)} %get-tuple-element.65.kt_ref, ...), custom_call_target="tpu_custom_call" | custom-call | flops 49999998976 | bytes 16777216 | tf_op jit(solution)/shard_map/attention_backward/pallas_call | solution.py:181
  280.8 0.0 copy-done.4
  280.8 2.8 copy-done
  283.6 4.6 %weight_grads.1 = (bf16[2,128,2176]{2,1,0:T(8,128)(2,1)S(1)}, f32[2,128,2176]{2,1,0:T(8,128)S(1)}) custom-call(s32[1]{0:T(128)} %bitcast.24.core_ref, bf16[512,2048]{1,0:T(8,128)(2,1)S(1)} %copy-done.5, bf16[3,2048,512]{2,1,0:T(8,128)(2,1)S(1)} %copy-done, f32[512,640]{1,0:T(8,128)S(1)} %copy-done.4), custom_call_target="tpu_custom_call" | custom-call | flops 3221225472 | bytes 12582912 | tf_op jit(solution)/shard_map/weight_grads/pallas_call | solution.py:663
  288.2 0.1 collective-permute-start.6
  288.3 2.9 collective-permute-done.6
  291.1 1.1 fusion
  292.3 0.6 collective-permute-start.7
  292.9 11.7 %input_grads.1 = bf16[2048,512]{1,0:T(8,128)(2,1)} custom-call(bf16[3,2048,512]{2,1,0:T(8,128)(2,1)} %attention_backward.1.grad_ref.grads_ref, bf16[512,2304]{1,0:T(8,128)(2,1)} %bitcast.59, bf16[512,2304]{1,0:T(8,128)(2,1)} %bitcast.60, bf16[2048,512]{1,0:T(8,128)(2,1)} %tokens_ref.5, f32[2048,512]{1,0:T(8,128)} %get-tuple-element.73.residual_grad_ref), custom_call_target="tpu_custom_call" | custom-call | flops 3221225472 | bytes 18874368 | tf_op jit(solution)/shard_map/input_grads/pallas_call | solution.py:691
  304.5 2.5 collective-permute-done.7
  307.0 1.2 bitcast_add_fusion
  308.2 0.0 copy-done.7
  308.2 0.9 add_convert_fusion
  309.1 0.0 all-to-all-done.3.in_ref
  309.1 5.9 %all-to-all-start.4 = ((bf16[8,16,2176]{2,1,0:T(8,128)(2,1)}), bf16[8,16,2176]{2,1,0:T(8,128)(2,1)S(1)}, u32[]{:S(2)}, u32[]{:S(2)}) async-start(bf16[8,16,2176]{2,1,0:T(8,128)(2,1)} %add_convert_fusion), calls=%async_computation.4 | async-start | bytes 1114112 | tf_op jit(solution)/shard_map/all_to_all | solution.py:810
  315.0 7.2 %unpack_grads.1 = (f32[8,512,256]{2,1,0:T(8,128)}, f32[8,256,512]{2,1,0:T(8,128)}) custom-call(bf16[8,1024,256]{2,1,0:T(8,128)(2,1)} %all-to-all-done.3.in_ref), custom_call_target="tpu_custom_call" | custom-call | flops 1000000 | bytes 12582912 | tf_op jit(solution)/shard_map/unpack_grads/pallas_call | solution.py:326
  322.2 7.6 %all-to-all-done.4.pieces_ref = bf16[8,16,2176]{2,1,0:T(8,128)(2,1)S(1)} async-done(((bf16[8,16,2176]{2,1,0:T(8,128)(2,1)}), bf16[8,16,2176]{2,1,0:T(8,128)(2,1)S(1)}, u32[]{:S(2)}, u32[]{:S(2)}) %all-to-all-start.4) | async-done | bytes 557088 | tf_op jit(solution)/shard_map/all_to_all | solution.py:810
  329.8 0.8 finish.1
  (21 shorter events, 0.3 us)
Async XLA Ops:
  2.2 5.5 %collective-permute-start = (bf16[16,2304]{1,0:T(8,128)(2,1)}, bf16[16,2304]{1,0:T(8,128)(2,1)S(1)}, u32[]{:S(2)}, u32[]{:S(2)}) collective-permute-start(bf16[16,2304]{1,0:T(8,128)(2,1)} %pack_small.1.own_ref), channel_id=1, source_target_pairs={{0,1},{1,0},{2,3},{3,2},{4,5},{5,4},{6,7},{7,6},{8,9},{9,8},{10,11... | collective-permute-start | bytes 221192 | tf_op jit(solution)/shard_map/ppermute | solution.py:754
  7.7 16.6 %collective-permute-start.1 = (bf16[32,2304]{1,0:T(8,128)(2,1)S(1)}, bf16[32,2304]{1,0:T(8,128)(2,1)S(1)}, u32[]{:S(2)}, u32[]{:S(2)}) collective-permute-start(bf16[32,2304]{1,0:T(8,128)(2,1)S(1)} %bitcast.65), channel_id=1, source_target_pairs={{0,2},{1,3},{2,0},{3,1},{4,6},{5,7},{6,4},{7,5},{8,10},{9,11},{10,... | collective-permute-start | bytes 442376 | tf_op jit(solution)/shard_map/ppermute | solution.py:754
  9.9 14.5 %collective-permute-start.2 = (bf16[32,2304]{1,0:T(8,128)(2,1)S(1)}, bf16[32,2304]{1,0:T(8,128)(2,1)S(1)}, u32[]{:S(2)}, u32[]{:S(2)}) collective-permute-start(bf16[32,2304]{1,0:T(8,128)(2,1)S(1)} %bitcast.66), channel_id=1, source_target_pairs={{0,4},{1,5},{2,6},{3,7},{4,0},{5,1},{6,2},{7,3},{8,12},{9,13},{10,... | collective-permute-start | bytes 442376 | tf_op jit(solution)/shard_map/ppermute | solution.py:754
  12.5 11.9 %collective-permute-start.3 = (bf16[32,2304]{1,0:T(8,128)(2,1)S(1)}, bf16[32,2304]{1,0:T(8,128)(2,1)S(1)}, u32[]{:S(2)}, u32[]{:S(2)}) collective-permute-start(bf16[32,2304]{1,0:T(8,128)(2,1)S(1)} %bitcast.67), channel_id=1, source_target_pairs={{0,6},{1,7},{2,4},{3,5},{4,2},{5,3},{6,0},{7,1},{8,14},{9,15},{10,... | collective-permute-start | bytes 442376 | tf_op jit(solution)/shard_map/ppermute | solution.py:754
  18.2 97.3 %all-to-all-start = ((bf16[8,1024,256]{2,1,0:T(8,128)(2,1)}), bf16[8,1024,256]{2,1,0:T(8,128)(2,1)}, u32[]{:S(2)}, u32[]{:S(2)}) async-start(bf16[8,1024,256]{2,1,0:T(8,128)(2,1)} %pack_weights.1), calls=%async_computation | async-start | bytes 8388608 | tf_op jit(solution)/shard_map/all_to_all | solution.py:810
  24.4 12.9 %collective-permute-start.4 = (bf16[128,2304]{1,0:T(8,128)(2,1)S(1)}, bf16[128,2304]{1,0:T(8,128)(2,1)S(1)}, u32[]{:S(2)}, u32[]{:S(2)}) collective-permute-start(bf16[128,2304]{1,0:T(8,128)(2,1)S(1)} %bitcast.62), channel_id=1, source_target_pairs={{0,16},{8,24},{16,0},{24,8},{1,17},{9,25},{17,1},{25,9},{2,18},{10... | collective-permute-start | bytes 1769480 | tf_op jit(solution)/shard_map/ppermute | solution.py:754
  37.4 1.1 copy-start.6
  38.5 3.1 collective-permute-start.5
  115.6 42.5 %all-to-all-start.1 = ((bf16[32,24,1024]{2,1,0:T(8,128)(2,1)}), bf16[32,24,1024]{2,1,0:T(8,128)(2,1)S(1)}, u32[]{:S(2)}, u32[]{:S(2)}) async-start(bf16[32,24,1024]{2,1,0:T(8,128)(2,1)} %bitcast.64), calls=%async_computation.1 | async-start | bytes 3145728 | tf_op jit(solution)/shard_map/all_to_all | solution.py:835
  119.5 49.5 %copy-start.3 = (f32[8,256]{1,0:T(8,128)}, f32[8,256]{1,0:T(8,128)S(1)}, u32[]{:S(2)}) copy-start(f32[8,256]{1,0:T(8,128)S(1)} %maximum_convert_fusion.bias_ref) | copy-start | bytes 24580
  158.1 10.9 %copy-start.1 = (bf16[32,24,1024]{2,1,0:T(8,128)(2,1)}, bf16[32,24,1024]{2,1,0:T(8,128)(2,1)S(1)}, u32[]{:S(2)}) copy-start(bf16[32,24,1024]{2,1,0:T(8,128)(2,1)S(1)} %all-to-all-done.1) | copy-start | bytes 4718596
  169.0 42.3 %all-to-all-start.2 = ((bf16[32,24,1024]{2,1,0:T(8,128)(2,1)}), bf16[32,24,1024]{2,1,0:T(8,128)(2,1)}, u32[]{:S(2)}, u32[]{:S(2)}) async-start(bf16[32,24,1024]{2,1,0:T(8,128)(2,1)} %bitcast.22), calls=%async_computation.2 | async-start | bytes 3145728 | tf_op jit(solution)/shard_map/all_to_all | solution.py:835
  211.2 97.8 %all-to-all-start.3 = ((bf16[8,1024,256]{2,1,0:T(8,128)(2,1)}), bf16[8,1024,256]{2,1,0:T(8,128)(2,1)}, u32[]{:S(2)}, u32[]{:S(2)}) async-start(bf16[8,1024,256]{2,1,0:T(8,128)(2,1)} %get-tuple-element.74), calls=%async_computation.3 | async-start | bytes 8388608 | tf_op jit(solution)/shard_map/all_to_all | solution.py:810
  233.2 47.6 %copy-start.4 = (f32[512,640]{1,0:T(8,128)S(1)}, f32[512,640]{1,0:T(8,128)}, u32[]{:S(2)}) copy-start(f32[512,640]{1,0:T(8,128)} %get-tuple-element.69.sums_ref) | copy-start | bytes 3932164
  233.2 47.5 %copy-start.5 = (bf16[512,2048]{1,0:T(8,128)(2,1)S(1)}, bf16[512,2048]{1,0:T(8,128)(2,1)}, u32[]{:S(2)}) copy-start(bf16[512,2048]{1,0:T(8,128)(2,1)} %get-tuple-element.63.normed_t_ref) | copy-start | bytes 6291460
  280.8 2.8 copy-start
  288.2 3.0 collective-permute-start.6
  292.3 14.7 %collective-permute-start.7 = (bf16[128,2176]{1,0:T(8,128)(2,1)S(1)}, bf16[128,2176]{1,0:T(8,128)(2,1)S(1)}, u32[]{:S(2)}, u32[]{:S(2)}) collective-permute-start(bf16[128,2176]{1,0:T(8,128)(2,1)S(1)} %fusion), channel_id=1, source_target_pairs={{0,16},{8,24},{16,0},{24,8},{1,17},{9,25},{17,1},{25,9},{2,18},{10... | collective-permute-start | bytes 1671176 | tf_op jit(solution)/shard_map/ppermute | solution.py:754
  304.5 3.7 %copy-start.7 = (bf16[8,16,128]{2,1,0:T(8,128)(2,1)S(1)}, bf16[8,16,128]{2,1,0:T(8,128)(2,1)}, u32[]{:S(2)}) copy-start(bf16[8,16,128]{2,1,0:T(8,128)(2,1)} %get-tuple-element.72) | copy-start | bytes 98308
  309.1 20.7 %all-to-all-start.4 = ((bf16[8,16,2176]{2,1,0:T(8,128)(2,1)}), bf16[8,16,2176]{2,1,0:T(8,128)(2,1)S(1)}, u32[]{:S(2)}, u32[]{:S(2)}) async-start(bf16[8,16,2176]{2,1,0:T(8,128)(2,1)} %add_convert_fusion), calls=%async_computation.4 | async-start | bytes 1114112 | tf_op jit(solution)/shard_map/all_to_all | solution.py:810
  315.0 14.8 %copy-start.2 = (bf16[16,2304]{1,0:T(8,128)(2,1)S(1)}, bf16[16,2304]{1,0:T(8,128)(2,1)}, u32[]{:S(2)}) copy-start(bf16[16,2304]{1,0:T(8,128)(2,1)} %pack_small.1.own_ref) | copy-start | bytes 221188

commit v6 on v4

--- a/solution.py
+++ b/solution.py
@@ -671,7 +671,6 @@
         6 * length * D * D,
         12 * 2**20,
         "weight_grads",
-        24,
     )(core, normed_t, grads, sums)
 
 

time: 332 us -> 333 us (level)
  Pallas kernels: 177 us -> 181 us
    pallas_call x1, Pallas kernels: 4.59 us -> 8.97 us  [weight_grads(): call(weight_grad_kernel, 3, [pl.BlockSpec(memory_space=pltpu.SMEM), fixed...]
  transfers between devices with their start and end apart: 13 -> 13, of which waited for: 9 -> 9; matrix products, arithmetic and copies ran while one was open for 3% -> 3% of each run, Pallas kernels for 49% -> 51%
where the time goes in v6:
time: 333 us; the launch traced here: 331 us
  Pallas kernels  181 us (54%)
  waiting for transfers between devices  106 us (32%)
  starting transfers between devices  33.6 us (10%)
  other arithmetic  5.46 us (2%)
  local copies, waits for them, and re-layouts  4.11 us (1%)
    all_to_all x2, waiting for transfers between devices, exchange(): lax.all_to_all(rows, BOTH, split_axis=0, concat_axis=0, tiled=True, axis_...  62 us
    pallas_call x1, Pallas kernels, attention_backward(): pl.pallas_call(attention_backward_kernel, grid=(pairs,), in_specs=[pair_c...  47.4 us
    pallas_call x1, Pallas kernels, attention_forward(): pl.pallas_call(attention_forward_kernel, grid=(pairs,), in_specs=[pair_co...  31.9 us
    all_to_all x3, waiting for transfers between devices, along_shard(): lax.all_to_all(blocks, 'shard', split_axis=0, concat_axis=0, tiled=True)  24.2 us
    ppermute x8, waiting for transfers between devices, swap(): return lax.ppermute(block, axis, [(i, i ^ bits) for i in range(size)])  19.5 us
    pallas_call x1, Pallas kernels, combine(): call(combine_kernel, steps, [leading(COMBINE, D), leading(COMBINE, D), le...  17.4 us
    all_to_all x3, starting transfers between devices, along_shard(): lax.all_to_all(blocks, 'shard', split_axis=0, concat_axis=0, tiled=True)  16.5 us
    pallas_call x1, Pallas kernels, expert_grads(): call(expert_grad_kernel, shards, [fixed(count, 2 * D), leading(1, total,...  13.9 us
  transfers between devices with their start and end apart: 13, of which 9 were waited for; matrix products, arithmetic and copies ran while one was open for 3% of the time, Pallas kernels for 51%

profile of v6, /device:TPU:0, one launch (start us, length us, event | category | flops | bytes accessed | tf_op | source)
XLA Modules:
  0.0 331.3 jit_solution(5569220105038632970)
XLA Ops:
  0.6 1.5 pack_small.1.own_ref
  2.2 3.0 collective-permute-start
  5.2 0.9 bitcast_dynamic-update-slice_fusion.5
  6.1 1.6 collective-permute-done
  7.7 2.1 collective-permute-start.1
  9.9 2.6 collective-permute-start.2
  12.4 0.0 collective-permute-start.3
  12.4 5.7 %pack_weights.1 = bf16[8,1024,256]{2,1,0:T(8,128)(2,1)} custom-call(f32[8,512,256]{2,1,0:T(8,128)} %first_ref, f32[8,256,512]{2,1,0:T(8,128)} %second_ref), custom_call_target="tpu_custom_call" | custom-call | flops 1000000 | bytes 12582912 | tf_op jit(solution)/shard_map/pack_weights/pallas_call | solution.py:301
  18.2 6.1 %all-to-all-start = ((bf16[8,1024,256]{2,1,0:T(8,128)(2,1)}), bf16[8,1024,256]{2,1,0:T(8,128)(2,1)}, u32[]{:S(2)}, u32[]{:S(2)}) async-start(bf16[8,1024,256]{2,1,0:T(8,128)(2,1)} %pack_weights.1), calls=%async_computation | async-start | bytes 8388608 | tf_op jit(solution)/shard_map/all_to_all | solution.py:809
  24.3 0.0 collective-permute-done.1
  24.3 0.0 collective-permute-done.2
  24.4 0.0 collective-permute-done.3
  24.4 1.6 collective-permute-start.4
  26.0 11.3 %collective-permute-done.4 = bf16[128,2304]{1,0:T(8,128)(2,1)S(1)} collective-permute-done((bf16[128,2304]{1,0:T(8,128)(2,1)S(1)}, bf16[128,2304]{1,0:T(8,128)(2,1)S(1)}, u32[]{:S(2)}, u32[]{:S(2)}) %collective-permute-start.4) | collective-permute-done | bytes 589856 | tf_op jit(solution)/shard_map/ppermute | solution.py:753
  37.3 0.1 select_bitcast_fusion.3
  37.4 0.0 copy-start.4
  37.4 1.1 pad_maximum_fusion.1
  38.5 0.0 collective-permute-start.5
  38.5 0.0 copy-done.4
  38.5 0.1 copy.53
  38.7 0.2 fusion.1
  38.9 0.1 copy.54
  39.0 0.7 reshape_reshape.9.slots_ref
  39.7 0.7 reshape.73
  40.3 1.3 collective-permute-done.5
  41.6 0.2 select_bitcast_fusion.1
  41.8 1.6 pad_maximum_fusion
  43.4 10.0 %project.1 = (bf16[2048,1536]{1,0:T(8,128)(2,1)}, bf16[512,2048]{1,0:T(8,128)(2,1)}) custom-call(bf16[2048,512]{1,0:T(8,128)(2,1)} %tokens_ref.5, bf16[512,2304]{1,0:T(8,128)(2,1)} %bitcast.53, bf16[512,2304]{1,0:T(8,128)(2,1)} %bitcast.54), custom_call_target="tpu_custom_call" | custom-call | flops 3221225472 | bytes 12582912 | tf_op jit(solution)/shard_map/project/pallas_call | solution.py:479
  53.4 31.9 %attention_forward.1 = (bf16[2048,512]{1,0:T(8,128)(2,1)}, f32[4,2,2048]{2,1,0:T(2,128)}, bf16[512,2048]{1,0:T(8,128)(2,1)}, bf16[512,2048]{1,0:T(8,128)(2,1)}, bf16[512,2048]{1,0:T(8,128)(2,1)}) custom-call(bf16[2048,1536]{1,0:T(8,128)(2,1)} %get-tuple-element.51.q_ref.k_ref.v_ref, bf16[2048,1536]{1,0:T(8,128)(2,1)} %get-tuple-element.51.q_ref.k_ref.v_ref, ...), custom_call_target="tpu_custom_call" | custom-call | flops 10000000000 | bytes 8388608 | tf_op jit(solution)/shard_map/attention_forward/pallas_call | solution.py:159
  85.4 13.5 %mix.1 = (f32[2048,512]{1,0:T(8,128)}, f32[2048,128]{1,0:T(8,128)}, bf16[768,1024]{1,0:T(8,128)(2,1)}) custom-call(bf16[2048,512]{1,0:T(8,128)(2,1)} %get-tuple-element.52.attended_ref, bf16[2048,512]{1,0:T(8,128)(2,1)} %tokens_ref.5, bf16[2048,512]{1,0:T(8,128)(2,1)} %grad_ref.3, bf16[512,2304]{1,0:T(8,128)(2,1)} %bitcast.55, bf16[512,2304]{1,0:T(8,128)(2,1)} %bitcast.56, ...), custom_call_target="tpu_custom_call" | custom-call | flops 2147483648 | bytes 14680064 | tf_op jit(solution)/shard_map/mix/pallas_call | solution.py:534
  98.8 16.7 %all-to-all-done.w_ref = bf16[8,1024,256]{2,1,0:T(8,128)(2,1)} async-done(((bf16[8,1024,256]{2,1,0:T(8,128)(2,1)}), bf16[8,1024,256]{2,1,0:T(8,128)(2,1)}, u32[]{:S(2)}, u32[]{:S(2)}) %all-to-all-start) | async-done | bytes 4194336 | tf_op jit(solution)/shard_map/all_to_all | solution.py:809
  115.5 3.8 %all-to-all-start.1 = ((bf16[32,24,1024]{2,1,0:T(8,128)(2,1)}), bf16[32,24,1024]{2,1,0:T(8,128)(2,1)S(1)}, u32[]{:S(2)}, u32[]{:S(2)}) async-start(bf16[32,24,1024]{2,1,0:T(8,128)(2,1)} %bitcast.64), calls=%async_computation.1 | async-start | bytes 3145728 | tf_op jit(solution)/shard_map/all_to_all | solution.py:834
  119.5 0.0 copy-start.2
  119.5 38.6 %all-to-all-done.1 = bf16[32,24,1024]{2,1,0:T(8,128)(2,1)S(1)} async-done(((bf16[32,24,1024]{2,1,0:T(8,128)(2,1)}), bf16[32,24,1024]{2,1,0:T(8,128)(2,1)S(1)}, u32[]{:S(2)}, u32[]{:S(2)}) %all-to-all-start.1) | async-done | bytes 1572896 | tf_op jit(solution)/shard_map/all_to_all | solution.py:834
  158.0 0.0 copy-start
  158.0 11.2 %expert_rows.1 = bf16[768,1024]{1,0:T(8,128)(2,1)} custom-call(bf16[768,1024]{1,0:T(8,128)(2,1)S(1)} %bitcast.51, bf16[8,1024,256]{2,1,0:T(8,128)(2,1)} %all-to-all-done.w_ref, f32[8,256]{1,0:T(8,128)S(1)} %maximum_convert_fusion.bias_ref), custom_call_target="tpu_custom_call" | custom-call | flops 6442450944 | bytes 8388608 | tf_op jit(solution)/shard_map/expert_rows/pallas_call | solution.py:402
  169.2 0.0 copy-done.2
  169.2 0.0 copy-done
  169.2 3.4 %all-to-all-start.2 = ((bf16[32,24,1024]{2,1,0:T(8,128)(2,1)}), bf16[32,24,1024]{2,1,0:T(8,128)(2,1)}, u32[]{:S(2)}, u32[]{:S(2)}) async-start(bf16[32,24,1024]{2,1,0:T(8,128)(2,1)} %bitcast.22), calls=%async_computation.2 | async-start | bytes 3145728 | tf_op jit(solution)/shard_map/all_to_all | solution.py:834
  172.7 0.8 reshape_reshape.12.slots_ref
  173.5 0.7 reshape.74
  174.2 13.9 %expert_grads.1 = (bf16[8,1024,256]{2,1,0:T(8,128)(2,1)}, bf16[8,16,128]{2,1,0:T(8,128)(2,1)}) custom-call(bf16[768,1024]{1,0:T(8,128)(2,1)} %bitcast.52, bf16[8,1024,256]{2,1,0:T(8,128)(2,1)} %all-to-all-done.w_ref, f32[8,256]{1,0:T(8,128)} %copy-done.2), custom_call_target="tpu_custom_call" | custom-call | flops 6442450944 | bytes 14680064 | tf_op jit(solution)/shard_map/expert_grads/pallas_call | solution.py:453
  188.1 23.4 %all-to-all-done.2 = bf16[32,24,1024]{2,1,0:T(8,128)(2,1)} async-done(((bf16[32,24,1024]{2,1,0:T(8,128)(2,1)}), bf16[32,24,1024]{2,1,0:T(8,128)(2,1)}, u32[]{:S(2)}, u32[]{:S(2)}) %all-to-all-start.2) | async-done | bytes 1572896 | tf_op jit(solution)/shard_map/all_to_all | solution.py:834
  211.5 4.5 %all-to-all-start.3 = ((bf16[8,1024,256]{2,1,0:T(8,128)(2,1)}), bf16[8,1024,256]{2,1,0:T(8,128)(2,1)}, u32[]{:S(2)}, u32[]{:S(2)}) async-start(bf16[8,1024,256]{2,1,0:T(8,128)(2,1)} %get-tuple-element.74), calls=%async_computation.3 | async-start | bytes 8388608 | tf_op jit(solution)/shard_map/all_to_all | solution.py:809
  216.1 17.4 %combine.1 = (bf16[2048,512]{1,0:T(8,128)(2,1)}, f32[2048,512]{1,0:T(8,128)}, bf16[512,2048]{1,0:T(8,128)(2,1)}, f32[512,640]{1,0:T(8,128)}) custom-call(f32[2048,512]{1,0:T(8,128)} %get-tuple-element.53.residual_ref, bf16[2048,512]{1,0:T(8,128)(2,1)} %grad_ref.3, f32[2048,128]{1,0:T(8,128)} %get-tuple-element.54.probs_ref, ...), custom_call_target="tpu_custom_call" | custom-call | flops 3221225472 | bytes 25165824 | tf_op jit(solution)/shard_map/combine/pallas_call | solution.py:613
  233.4 47.4 %attention_backward.1.grad_ref.grads_ref = bf16[3,2048,512]{2,1,0:T(8,128)(2,1)} custom-call(bf16[2048,1536]{1,0:T(8,128)(2,1)} %get-tuple-element.51.q_ref.k_ref.v_ref, bf16[2048,1536]{1,0:T(8,128)(2,1)} %get-tuple-element.51.q_ref.k_ref.v_ref, bf16[512,2048]{1,0:T(8,128)(2,1)} %get-tuple-element.64.qt_ref, bf16[512,2048]{1,0:T(8,128)(2,1)} %get-tuple-element.65.kt_ref, ...), custom_call_target="tpu_custom_call" | custom-call | flops 49999998976 | bytes 16777216 | tf_op jit(solution)/shard_map/attention_backward/pallas_call | solution.py:181
  280.8 9.0 %weight_grads.1 = (bf16[2,128,2176]{2,1,0:T(8,128)(2,1)}, f32[2,128,2176]{2,1,0:T(8,128)}) custom-call(s32[1]{0:T(128)} %bitcast.24.core_ref, bf16[512,2048]{1,0:T(8,128)(2,1)} %get-tuple-element.63.normed_t_ref, bf16[3,2048,512]{2,1,0:T(8,128)(2,1)} %attention_backward.1.grad_ref.grads_ref, f32[512,640]{1,0:T(8,128)} %get-tuple-element.69.sums_ref), custom_call_target="tpu_custom_call" | custom-call | flops 3221225472 | bytes 12582912 | tf_op jit(solution)/shard_map/weight_grads/pallas_call | solution.py:663
  289.8 0.0 collective-permute-start.6
  289.8 3.0 collective-permute-done.6
  292.8 1.3 fusion
  294.1 0.6 collective-permute-start.7
  294.7 0.0 copy-start.3
  294.7 11.8 %input_grads.1 = bf16[2048,512]{1,0:T(8,128)(2,1)} custom-call(bf16[3,2048,512]{2,1,0:T(8,128)(2,1)} %attention_backward.1.grad_ref.grads_ref, bf16[512,2304]{1,0:T(8,128)(2,1)} %bitcast.59, bf16[512,2304]{1,0:T(8,128)(2,1)} %bitcast.60, bf16[2048,512]{1,0:T(8,128)(2,1)} %tokens_ref.5, f32[2048,512]{1,0:T(8,128)} %get-tuple-element.73.residual_grad_ref), custom_call_target="tpu_custom_call" | custom-call | flops 3221225472 | bytes 18874368 | tf_op jit(solution)/shard_map/input_grads/pallas_call | solution.py:690
  306.5 2.3 collective-permute-done.7
  308.8 0.0 copy-done.3
  308.8 0.2 bitcast_add_fusion
  309.0 0.0 copy-done.5
  309.0 0.9 add_convert_fusion
  309.9 0.0 all-to-all-done.3.in_ref
  309.9 5.9 %all-to-all-start.4 = ((bf16[8,16,2176]{2,1,0:T(8,128)(2,1)}), bf16[8,16,2176]{2,1,0:T(8,128)(2,1)S(1)}, u32[]{:S(2)}, u32[]{:S(2)}) async-start(bf16[8,16,2176]{2,1,0:T(8,128)(2,1)} %add_convert_fusion), calls=%async_computation.4 | async-start | bytes 1114112 | tf_op jit(solution)/shard_map/all_to_all | solution.py:809
  315.8 7.2 %unpack_grads.1 = (f32[8,512,256]{2,1,0:T(8,128)}, f32[8,256,512]{2,1,0:T(8,128)}) custom-call(bf16[8,1024,256]{2,1,0:T(8,128)(2,1)} %all-to-all-done.3.in_ref), custom_call_target="tpu_custom_call" | custom-call | flops 1000000 | bytes 12582912 | tf_op jit(solution)/shard_map/unpack_grads/pallas_call | solution.py:326
  323.0 7.5 %all-to-all-done.4.pieces_ref = bf16[8,16,2176]{2,1,0:T(8,128)(2,1)S(1)} async-done(((bf16[8,16,2176]{2,1,0:T(8,128)(2,1)}), bf16[8,16,2176]{2,1,0:T(8,128)(2,1)S(1)}, u32[]{:S(2)}, u32[]{:S(2)}) %all-to-all-start.4) | async-done | bytes 557088 | tf_op jit(solution)/shard_map/all_to_all | solution.py:809
  330.5 0.0 copy-done.1
  330.5 0.8 finish.1
  (17 shorter events, 0.3 us)
Async XLA Ops:
  2.2 5.5 %collective-permute-start = (bf16[16,2304]{1,0:T(8,128)(2,1)}, bf16[16,2304]{1,0:T(8,128)(2,1)S(1)}, u32[]{:S(2)}, u32[]{:S(2)}) collective-permute-start(bf16[16,2304]{1,0:T(8,128)(2,1)} %pack_small.1.own_ref), channel_id=1, source_target_pairs={{0,1},{1,0},{2,3},{3,2},{4,5},{5,4},{6,7},{7,6},{8,9},{9,8},{10,11... | collective-permute-start | bytes 221192 | tf_op jit(solution)/shard_map/ppermute | solution.py:753
  7.7 16.6 %collective-permute-start.1 = (bf16[32,2304]{1,0:T(8,128)(2,1)S(1)}, bf16[32,2304]{1,0:T(8,128)(2,1)S(1)}, u32[]{:S(2)}, u32[]{:S(2)}) collective-permute-start(bf16[32,2304]{1,0:T(8,128)(2,1)S(1)} %bitcast.65), channel_id=1, source_target_pairs={{0,2},{1,3},{2,0},{3,1},{4,6},{5,7},{6,4},{7,5},{8,10},{9,11},{10,... | collective-permute-start | bytes 442376 | tf_op jit(solution)/shard_map/ppermute | solution.py:753
  9.9 14.5 %collective-permute-start.2 = (bf16[32,2304]{1,0:T(8,128)(2,1)S(1)}, bf16[32,2304]{1,0:T(8,128)(2,1)S(1)}, u32[]{:S(2)}, u32[]{:S(2)}) collective-permute-start(bf16[32,2304]{1,0:T(8,128)(2,1)S(1)} %bitcast.66), channel_id=1, source_target_pairs={{0,4},{1,5},{2,6},{3,7},{4,0},{5,1},{6,2},{7,3},{8,12},{9,13},{10,... | collective-permute-start | bytes 442376 | tf_op jit(solution)/shard_map/ppermute | solution.py:753
  12.4 11.9 %collective-permute-start.3 = (bf16[32,2304]{1,0:T(8,128)(2,1)S(1)}, bf16[32,2304]{1,0:T(8,128)(2,1)S(1)}, u32[]{:S(2)}, u32[]{:S(2)}) collective-permute-start(bf16[32,2304]{1,0:T(8,128)(2,1)S(1)} %bitcast.67), channel_id=1, source_target_pairs={{0,6},{1,7},{2,4},{3,5},{4,2},{5,3},{6,0},{7,1},{8,14},{9,15},{10,... | collective-permute-start | bytes 442376 | tf_op jit(solution)/shard_map/ppermute | solution.py:753
  18.2 97.3 %all-to-all-start = ((bf16[8,1024,256]{2,1,0:T(8,128)(2,1)}), bf16[8,1024,256]{2,1,0:T(8,128)(2,1)}, u32[]{:S(2)}, u32[]{:S(2)}) async-start(bf16[8,1024,256]{2,1,0:T(8,128)(2,1)} %pack_weights.1), calls=%async_computation | async-start | bytes 8388608 | tf_op jit(solution)/shard_map/all_to_all | solution.py:809
  24.4 12.9 %collective-permute-start.4 = (bf16[128,2304]{1,0:T(8,128)(2,1)S(1)}, bf16[128,2304]{1,0:T(8,128)(2,1)S(1)}, u32[]{:S(2)}, u32[]{:S(2)}) collective-permute-start(bf16[128,2304]{1,0:T(8,128)(2,1)S(1)} %bitcast.62), channel_id=1, source_target_pairs={{0,16},{8,24},{16,0},{24,8},{1,17},{9,25},{17,1},{25,9},{2,18},{10... | collective-permute-start | bytes 1769480 | tf_op jit(solution)/shard_map/ppermute | solution.py:753
  37.4 1.1 copy-start.4
  38.5 3.1 collective-permute-start.5
  115.5 42.5 %all-to-all-start.1 = ((bf16[32,24,1024]{2,1,0:T(8,128)(2,1)}), bf16[32,24,1024]{2,1,0:T(8,128)(2,1)S(1)}, u32[]{:S(2)}, u32[]{:S(2)}) async-start(bf16[32,24,1024]{2,1,0:T(8,128)(2,1)} %bitcast.64), calls=%async_computation.1 | async-start | bytes 3145728 | tf_op jit(solution)/shard_map/all_to_all | solution.py:834
  119.5 49.8 %copy-start.2 = (f32[8,256]{1,0:T(8,128)}, f32[8,256]{1,0:T(8,128)S(1)}, u32[]{:S(2)}) copy-start(f32[8,256]{1,0:T(8,128)S(1)} %maximum_convert_fusion.bias_ref) | copy-start | bytes 24580
  158.0 11.2 %copy-start = (bf16[32,24,1024]{2,1,0:T(8,128)(2,1)}, bf16[32,24,1024]{2,1,0:T(8,128)(2,1)S(1)}, u32[]{:S(2)}) copy-start(bf16[32,24,1024]{2,1,0:T(8,128)(2,1)S(1)} %all-to-all-done.1) | copy-start | bytes 4718596
  169.2 42.3 %all-to-all-start.2 = ((bf16[32,24,1024]{2,1,0:T(8,128)(2,1)}), bf16[32,24,1024]{2,1,0:T(8,128)(2,1)}, u32[]{:S(2)}, u32[]{:S(2)}) async-start(bf16[32,24,1024]{2,1,0:T(8,128)(2,1)} %bitcast.22), calls=%async_computation.2 | async-start | bytes 3145728 | tf_op jit(solution)/shard_map/all_to_all | solution.py:834
  211.5 98.4 %all-to-all-start.3 = ((bf16[8,1024,256]{2,1,0:T(8,128)(2,1)}), bf16[8,1024,256]{2,1,0:T(8,128)(2,1)}, u32[]{:S(2)}, u32[]{:S(2)}) async-start(bf16[8,1024,256]{2,1,0:T(8,128)(2,1)} %get-tuple-element.74), calls=%async_computation.3 | async-start | bytes 8388608 | tf_op jit(solution)/shard_map/all_to_all | solution.py:809
  289.8 3.0 collective-permute-start.6
  294.1 14.7 %collective-permute-start.7 = (bf16[128,2176]{1,0:T(8,128)(2,1)S(1)}, bf16[128,2176]{1,0:T(8,128)(2,1)S(1)}, u32[]{:S(2)}, u32[]{:S(2)}) collective-permute-start(bf16[128,2176]{1,0:T(8,128)(2,1)S(1)} %fusion), channel_id=1, source_target_pairs={{0,16},{8,24},{16,0},{24,8},{1,17},{9,25},{17,1},{25,9},{2,18},{10... | collective-permute-start | bytes 1671176 | tf_op jit(solution)/shard_map/ppermute | solution.py:753
  294.7 14.1 %copy-start.3 = (f32[2,128,2176]{2,1,0:T(8,128)S(1)}, f32[2,128,2176]{2,1,0:T(8,128)}, u32[]{:S(2)}) copy-start(f32[2,128,2176]{2,1,0:T(8,128)} %get-tuple-element.70) | copy-start | bytes 6684676
  306.5 2.5 copy-start.5
  309.9 20.6 %all-to-all-start.4 = ((bf16[8,16,2176]{2,1,0:T(8,128)(2,1)}), bf16[8,16,2176]{2,1,0:T(8,128)(2,1)S(1)}, u32[]{:S(2)}, u32[]{:S(2)}) async-start(bf16[8,16,2176]{2,1,0:T(8,128)(2,1)} %add_convert_fusion), calls=%async_computation.4 | async-start | bytes 1114112 | tf_op jit(solution)/shard_map/all_to_all | solution.py:809
  315.8 14.7 %copy-start.1 = (bf16[16,2304]{1,0:T(8,128)(2,1)S(1)}, bf16[16,2304]{1,0:T(8,128)(2,1)}, u32[]{:S(2)}) copy-start(bf16[16,2304]{1,0:T(8,128)(2,1)} %pack_small.1.own_ref) | copy-start | bytes 221188
